TPU v7x, 256 devices: a whole 4x4x8 slice. The times are simulated.
256 devices in a mesh: section: 8 (over x, z_hi), ctx: 32 (over y, z_lo, core).
Axes of the slice: x: 4, y: 4, z: 8 (z_hi: 2, z_lo: 4; z = z_hi * 4 + z_lo), core: 2. Of those that a mesh axis runs over, the one named last changes fastest.
Arguments:
- hidden: bfloat16 [8, 8192, 4096], P('section', 'ctx'), may hold values from -6 to 6
- query: bfloat16 [8, 8192, 2048], P('section', 'ctx'), may hold values from -480 to 480
- keyv: bfloat16 [8, 8192, 2048], P('section', 'ctx'), may hold values from -6 to 6
- value: bfloat16 [8, 8192, 2048], P('section', 'ctx'), may hold values from -6 to 6
- segments: int32 [8, 8192], P('section', 'ctx'), may hold values from 0 to 15, as said below
- out_weight: bfloat16 [8, 2048, 4096], P('section', 'ctx'), may hold values from -0.125 to 0.125
Outputs:
- passed: bfloat16 [8, 8192, 4096], P('section', 'ctx')
Inputs may be any that keep to these rules, and one draw needn't show every extreme that they name: `segments`: within each micro-batch the numbers never fall along the tokens and each of 0 to 15 names one document of 256 to 768 tokens; in every micro-batch at least one document has exactly 768 tokens.
All inputs are finite; a program needn't handle non-finite values.
Results may differ from a plain program's by a relative error of at most 0.0085.
Values may be sent and summed in bfloat16 or wider, within the bound.
No kernel may reach another device: no remote copies, remote signals or barrier semaphores. Data moves between devices by JAX's collectives and lax.ppermute only.
A program may use at most 192 MiB of HBM per device.

v0:
```python
import jax
import jax.numpy as jnp
from jax import lax
from jax.sharding import PartitionSpec as P

DH = 128
SPAN = 3


def passed_along(value, axis, steps):
    count = lax.axis_size(axis)
    leading, last = (max(0, -steps), min(count, count - steps))
    return lax.ppermute(value, axis, [(source, source + steps) for source in range(leading, last)])


def shifted(array, axis, by):
    count = lax.axis_size(axis)
    return lax.ppermute(array, axis, [(i, (i + by) % count) for i in range(count)])


def on_device(hidden, query, keyv, value, segments, out_weight):
    resid = hidden[0].astype(jnp.float32)
    tokens_here, width = resid.shape
    columns = query.shape[2]
    heads = columns // DH
    depth = DH
    query_rows = query[0].reshape(tokens_here, heads, depth)
    key_rows = keyv[0]
    value_rows = value[0]
    labels = segments[0] + 1
    blocks = [(key_rows, value_rows, labels)]
    for offset in range(1, SPAN + 1):
        for sign in (1, -1):
            blocks.append(passed_along((key_rows, value_rows, labels), "ctx", sign * offset))
    count = len(blocks)
    key_stack = jnp.stack([entry[0] for entry in blocks]).reshape(count, tokens_here, heads, depth)
    value_stack = jnp.stack([entry[1] for entry in blocks]).reshape(
        count, tokens_here, heads, depth
    )
    matches = [labels[:, None] == entry[2][None, :] for entry in blocks]
    group = 8
    inv_scale = 1.0 / depth**0.5

    def head_group(first_head):
        query_part = lax.dynamic_slice_in_dim(query_rows, first_head, group, 1)
        key_part = lax.dynamic_slice_in_dim(key_stack, first_head, group, 2)
        value_part = lax.dynamic_slice_in_dim(value_stack, first_head, group, 2)
        score_list = []
        for index in range(count):

            def tile_scores(index=index):
                raw = jnp.einsum(
                    "qhd,khd->hqk", query_part, key_part[index], preferred_element_type=jnp.float32
                )
                return jnp.where(matches[index][None], raw * inv_scale, -1e30)

            score_list.append(tile_scores())
        scores = jnp.concatenate(score_list, axis=2)
        top = jnp.max(scores, axis=2, keepdims=True)
        expo = jnp.exp(scores - top)
        probs = (expo / jnp.sum(expo, axis=2, keepdims=True)).astype(jnp.bfloat16)
        summed = jnp.zeros((tokens_here, group, depth), jnp.float32)
        for index in range(count):
            piece = probs[:, :, index * tokens_here : (index + 1) * tokens_here]

            def tile_values(piece=piece, index=index):
                return jnp.einsum(
                    "hqk,khd->qhd", piece, value_part[index], preferred_element_type=jnp.float32
                )

            summed = summed + tile_values()
        return summed.astype(jnp.bfloat16)

    starts = jnp.arange(heads // group, dtype=jnp.int32) * group
    attended = lax.map(head_group, starts)
    attended = jnp.moveaxis(attended, 0, 1).reshape(tokens_here, columns)
    output = jnp.dot(
        attended,
        lax.all_gather(out_weight[0], "ctx", axis=0, tiled=True),
        preferred_element_type=jnp.float32,
    )
    result = (resid + output).astype(jnp.bfloat16)
    return shifted(result[None], "section", 1)


def solution(mesh):
    return jax.shard_map(
        on_device,
        mesh=mesh,
        in_specs=(
            P("section", "ctx", None),
            P("section", "ctx", None),
            P("section", "ctx", None),
            P("section", "ctx", None),
            P("section", "ctx"),
            P("section", "ctx", None),
        ),
        out_specs=P("section", "ctx", None),
        check_vma=False,
    )
```

profile of v0, /device:TPU:9, one launch (start us, length us, event | category | flops | bytes accessed | tf_op | source)
XLA Modules:
  0.0 617.6 jit_solution(15338361201466970750)
XLA Ops:
  8.7 4.1 collective-permute-start.6
  12.9 1.9 collective-permute-start
  14.8 2.4 collective-permute-start.1
  17.2 3.5 collective-permute-start.2
  20.8 4.4 collective-permute-start.3
  25.2 3.4 collective-permute-done.6
  28.6 22.5 %collective-permute-start.4 = (bf16[256,2048]{1,0:T(8,128)(2,1)}, bf16[256,2048]{1,0:T(8,128)(2,1)}, u32[]{:S(2)}, u32[]{:S(2)}) collective-permute-start(bf16[256,2048]{1,0:T(8,128)(2,1)} %bitcast.156), channel_id=1, source_target_pairs={{0,3},{1,4},{2,5},{3,6},{4,7},{5,8},{6,9},{7,10},{8,11},{9,12},{10... | collective-permute-start | bytes 3145736 | tf_op jit(solution)/shard_map/ppermute | solution.py:13
  51.2 33.6 %collective-permute-start.7 = (bf16[256,2048]{0,1:T(8,128)(2,1)S(1)}, bf16[256,2048]{0,1:T(8,128)(2,1)}, u32[]{:S(2)}, u32[]{:S(2)}) collective-permute-start(bf16[256,2048]{0,1:T(8,128)(2,1)S(1)} %bitcast.139), channel_id=1, source_target_pairs={{1,0},{2,1},{3,2},{4,3},{5,4},{6,5},{7,6},{8,7},{9,8},{10,9},{11,1... | collective-permute-start | bytes 3145736 | tf_op jit(solution)/shard_map/ppermute | solution.py:13
  84.8 40.4 %collective-permute-start.8 = (bf16[256,2048]{0,1:T(8,128)(2,1)S(1)}, bf16[256,2048]{0,1:T(8,128)(2,1)}, u32[]{:S(2)}, u32[]{:S(2)}) collective-permute-start(bf16[256,2048]{0,1:T(8,128)(2,1)S(1)} %bitcast.140), channel_id=1, source_target_pairs={{0,2},{1,3},{2,4},{3,5},{4,6},{5,7},{6,8},{7,9},{8,10},{9,11},{10,... | collective-permute-start | bytes 3145736 | tf_op jit(solution)/shard_map/ppermute | solution.py:13
  129.6 2.3 copy.35
  132.4 70.6 %collective-permute-start.10 = (bf16[256,2048]{0,1:T(8,128)(2,1)S(1)}, bf16[256,2048]{0,1:T(8,128)(2,1)}, u32[]{:S(2)}, u32[]{:S(2)}) collective-permute-start(bf16[256,2048]{0,1:T(8,128)(2,1)S(1)} %bitcast.142), channel_id=1, source_target_pairs={{0,3},{1,4},{2,5},{3,6},{4,7},{5,8},{6,9},{7,10},{8,11},{9,12},{10... | collective-permute-start | bytes 3145736 | tf_op jit(solution)/shard_map/ppermute | solution.py:13
  208.5 2.3 copy.30
  210.7 2.3 copy.31
  216.0 2.4 constant_dynamic-update-slice_fusion.12
  220.4 2.5 constant_dynamic-update-slice_fusion.11
  222.9 57.1 %collective-permute-start.12 = (s32[256]{0:T(256)S(1)}, s32[256]{0:T(256)S(1)}, u32[]{:S(2)}, u32[]{:S(2)}) collective-permute-start(s32[256]{0:T(256)S(1)} %bitcast.161), channel_id=1, source_target_pairs={{0,1},{1,2},{2,3},{3,4},{4,5},{5,6},{6,7},{7,8},{8,9},{9,10},{10,1... | collective-permute-start | bytes 3080 | tf_op jit(solution)/shard_map/ppermute | solution.py:13
  279.9 2.3 constant_dynamic-update-slice_fusion.10
  284.1 2.3 constant_dynamic-update-slice_fusion.9
  286.7 76.3 %collective-permute-start.14 = (s32[256]{0:T(256)S(1)}, s32[256]{0:T(256)S(1)}, u32[]{:S(2)}, u32[]{:S(2)}) collective-permute-start(s32[256]{0:T(256)S(1)} %bitcast.163), channel_id=1, source_target_pairs={{0,2},{1,3},{2,4},{3,5},{4,6},{5,7},{6,8},{7,9},{8,10},{9,11},{10,... | collective-permute-start | bytes 3080 | tf_op jit(solution)/shard_map/ppermute | solution.py:13
  363.1 2.3 constant_dynamic-update-slice_fusion.8
  367.3 2.3 constant_dynamic-update-slice_fusion.7
  375.9 5.7 collective-permute-start.16
  383.0 2.8 collective-permute-start.17
  386.9 1.9 collective-permute-done.17
  389.4 109.5 %while.12 = (s32[]{:T(128)}, bf16[2,256,8,128]{1,3,2,0:T(8,128)(2,1)}, s32[2]{0:T(128)}, bf16[7,256,16,128]{1,3,2,0:T(8,128)(2,1)}, bf16[256,16,128]{0,2,1:T(8,1...) while((s32[]{:T(128)}, ...), condition=%wide.region_9.10_spmd.clone.clone, body=%wide.region_0.9_spmd.clone.clone.sunk | while | flops 1910697984 | bytes 125905120 | solution.py:75
  393.5 3.1 fusion.104
  396.6 3.1 fusion.105
  399.7 3.0 fusion.106
  402.7 2.9 fusion.107
  405.6 3.0 fusion.108
  408.6 3.0 fusion.109
  411.6 3.0 fusion.110
  414.5 7.1 %fusion.111 = f32[8,256]{1,0:T(8,128)S(1)} fusion(f32[8,256,1792]{1,2,0:T(8,128)} %get-tuple-element.336, f32[8,256]{1,0:T(8,128)S(1)} %maximum_maximum_fusion.2), kind=kLoop, calls=%fused_computation.9.clone.1 | loop fusion | flops 7337984 | bytes 14696448 | tf_op jit(solution)/shard_map/while/body/eval_jaxpr/reduce_sum | solution.py:61
  421.6 10.2 %divide_convert_fusion.2 = bf16[8,256,1792]{1,2,0:T(8,128)(2,1)} fusion(f32[8,256,1792]{1,2,0:T(8,128)} %get-tuple-element.336, f32[8,256]{1,0:T(8,128)S(1)} %fusion.111, f32[8,256]{1,0:T(8,128)S(1)} %maximum_maximum_fusion.2), kind=kLoop, calls=%fused_computation.7.clone.1 | loop fusion | flops 11010048 | bytes 22036480 | tf_op jit(solution)/shard_map/while/body/eval_jaxpr/convert_element_type | solution.py:61
  433.7 2.1 convolution_add_fusion.11
  448.1 3.1 fusion.104
  451.2 3.1 fusion.105
  454.3 3.0 fusion.106
  457.3 2.9 fusion.107
  460.2 3.0 fusion.108
  463.2 3.0 fusion.109
  466.2 2.9 fusion.110
  469.2 7.1 %fusion.111 = f32[8,256]{1,0:T(8,128)S(1)} fusion(f32[8,256,1792]{1,2,0:T(8,128)} %get-tuple-element.336, f32[8,256]{1,0:T(8,128)S(1)} %maximum_maximum_fusion.2), kind=kLoop, calls=%fused_computation.9.clone.1 | loop fusion | flops 7337984 | bytes 14696448 | tf_op jit(solution)/shard_map/while/body/eval_jaxpr/reduce_sum | solution.py:61
  476.2 10.2 %divide_convert_fusion.2 = bf16[8,256,1792]{1,2,0:T(8,128)(2,1)} fusion(f32[8,256,1792]{1,2,0:T(8,128)} %get-tuple-element.336, f32[8,256]{1,0:T(8,128)S(1)} %fusion.111, f32[8,256]{1,0:T(8,128)S(1)} %maximum_maximum_fusion.2), kind=kLoop, calls=%fused_computation.7.clone.1 | loop fusion | flops 11010048 | bytes 22036480 | tf_op jit(solution)/shard_map/while/body/eval_jaxpr/convert_element_type | solution.py:61
  488.3 2.1 convolution_add_fusion.11
  498.9 10.7 %fusion.76 = bf16[1,256,4096]{2,1,0:T(8,128)(2,1)S(1)} fusion(bf16[256,2048]{0,1:T(8,128)(2,1)} %bitcast.160, bf16[1,2048,4096]{2,1,0:T(8,128)(2,1)} %all-gather.3.cloned.1.call-done, bf16[1,256,4096]{2,1,0:T(8,128)(2,1)S(1)} %copy-done.4), kind=kOutput, calls=%fused_computation.102 | convolution fusion | flops 4298113024 | bytes 22020096 | tf_op jit(solution)/shard_map/dot_general | solution.py:77
  509.7 4.5 collective-permute-start.18
  514.2 95.2 %collective-permute-done.18 = bf16[1,256,4096]{2,1,0:T(8,128)(2,1)S(1)} collective-permute-done((bf16[1,256,4096]{2,1,0:T(8,128)(2,1)S(1)}, bf16[1,256,4096]{2,1,0:T(8,128)(2,1)S(1)}, u32[]{:S(2)}, u32[]{:S(2)}) %collective-permute-start.18) | collective-permute-done | bytes 2097184 | tf_op jit(solution)/shard_map/ppermute | solution.py:18
  (130 shorter events, 57.1 us)
Async XLA Ops:
  6.5 200.6 %copy-start.22 = (s32[1,256]{1,0:T(1,128)S(1)}, s32[1,256]{1,0:T(1,128)}, u32[]{:S(2)}) copy-start(s32[1,256]{1,0:T(1,128)} %param.12) | copy-start | bytes 3076
  6.5 492.4 %all-gather.3.cloned.1.call-start = ((), (), s32[]{:S(2)}) async-start(), calls=%async_computation | async-start | bytes 17301504 | tf_op jit(solution)/shard_map/all_gather | solution.py:79
  8.7 19.8 %collective-permute-start.6 = (bf16[256,2048]{0,1:T(8,128)(2,1)S(1)}, bf16[256,2048]{0,1:T(8,128)(2,1)S(1)}, u32[]{:S(2)}, u32[]{:S(2)}) collective-permute-start(bf16[256,2048]{0,1:T(8,128)(2,1)S(1)} %bitcast.138), channel_id=1, source_target_pairs={{0,1},{1,2},{2,3},{3,4},{4,5},{5,6},{6,7},{7,8},{8,9},{9,10},{10,1... | collective-permute-start | bytes 3145736 | tf_op jit(solution)/shard_map/ppermute | solution.py:13
  12.9 38.3 %collective-permute-start = (bf16[256,2048]{1,0:T(8,128)(2,1)}, bf16[256,2048]{1,0:T(8,128)(2,1)S(1)}, u32[]{:S(2)}, u32[]{:S(2)}) collective-permute-start(bf16[256,2048]{1,0:T(8,128)(2,1)} %bitcast.152), channel_id=1, source_target_pairs={{0,1},{1,2},{2,3},{3,4},{4,5},{5,6},{6,7},{7,8},{8,9},{9,10},{10,1... | collective-permute-start | bytes 3145736 | tf_op jit(solution)/shard_map/ppermute | solution.py:13
  14.8 69.9 %collective-permute-start.1 = (bf16[256,2048]{1,0:T(8,128)(2,1)}, bf16[256,2048]{1,0:T(8,128)(2,1)S(1)}, u32[]{:S(2)}, u32[]{:S(2)}) collective-permute-start(bf16[256,2048]{1,0:T(8,128)(2,1)} %bitcast.153), channel_id=1, source_target_pairs={{1,0},{2,1},{3,2},{4,3},{5,4},{6,5},{7,6},{8,7},{9,8},{10,9},{11,1... | collective-permute-start | bytes 3145736 | tf_op jit(solution)/shard_map/ppermute | solution.py:13
  17.2 108.0 %collective-permute-start.2 = (bf16[256,2048]{1,0:T(8,128)(2,1)}, bf16[256,2048]{1,0:T(8,128)(2,1)S(1)}, u32[]{:S(2)}, u32[]{:S(2)}) collective-permute-start(bf16[256,2048]{1,0:T(8,128)(2,1)} %bitcast.154), channel_id=1, source_target_pairs={{0,2},{1,3},{2,4},{3,5},{4,6},{5,7},{6,8},{7,9},{8,10},{9,11},{10,... | collective-permute-start | bytes 3145736 | tf_op jit(solution)/shard_map/ppermute | solution.py:13
  20.8 111.7 %collective-permute-start.3 = (bf16[256,2048]{1,0:T(8,128)(2,1)}, bf16[256,2048]{1,0:T(8,128)(2,1)}, u32[]{:S(2)}, u32[]{:S(2)}) collective-permute-start(bf16[256,2048]{1,0:T(8,128)(2,1)} %bitcast.155), channel_id=1, source_target_pairs={{2,0},{3,1},{4,2},{5,3},{6,4},{7,5},{8,6},{9,7},{10,8},{11,9},{12,... | collective-permute-start | bytes 3145736 | tf_op jit(solution)/shard_map/ppermute | solution.py:13
  28.6 96.6 %copy-start.6 = (bf16[256,2048]{0,1:T(8,128)(2,1)}, bf16[256,2048]{0,1:T(8,128)(2,1)S(1)}, u32[]{:S(2)}) copy-start(bf16[256,2048]{0,1:T(8,128)(2,1)S(1)} %collective-permute-done.6) | copy-start | bytes 3145732
  28.6 175.6 %collective-permute-start.4 = (bf16[256,2048]{1,0:T(8,128)(2,1)}, bf16[256,2048]{1,0:T(8,128)(2,1)}, u32[]{:S(2)}, u32[]{:S(2)}) collective-permute-start(bf16[256,2048]{1,0:T(8,128)(2,1)} %bitcast.156), channel_id=1, source_target_pairs={{0,3},{1,4},{2,5},{3,6},{4,7},{5,8},{6,9},{7,10},{8,11},{9,12},{10... | collective-permute-start | bytes 3145736 | tf_op jit(solution)/shard_map/ppermute | solution.py:13
  51.2 167.3 %collective-permute-start.7 = (bf16[256,2048]{0,1:T(8,128)(2,1)S(1)}, bf16[256,2048]{0,1:T(8,128)(2,1)}, u32[]{:S(2)}, u32[]{:S(2)}) collective-permute-start(bf16[256,2048]{0,1:T(8,128)(2,1)S(1)} %bitcast.139), channel_id=1, source_target_pairs={{1,0},{2,1},{3,2},{4,3},{5,4},{6,5},{7,6},{8,7},{9,8},{10,9},{11,1... | collective-permute-start | bytes 3145736 | tf_op jit(solution)/shard_map/ppermute | solution.py:13
  84.7 40.4 %copy-start.8 = (bf16[256,2048]{1,0:T(8,128)(2,1)}, bf16[256,2048]{1,0:T(8,128)(2,1)S(1)}, u32[]{:S(2)}) copy-start(bf16[256,2048]{1,0:T(8,128)(2,1)S(1)} %collective-permute-done.1) | copy-start | bytes 3145732
  84.8 138.1 %collective-permute-start.8 = (bf16[256,2048]{0,1:T(8,128)(2,1)S(1)}, bf16[256,2048]{0,1:T(8,128)(2,1)}, u32[]{:S(2)}, u32[]{:S(2)}) collective-permute-start(bf16[256,2048]{0,1:T(8,128)(2,1)S(1)} %bitcast.140), channel_id=1, source_target_pairs={{0,2},{1,3},{2,4},{3,5},{4,6},{5,7},{6,8},{7,9},{8,10},{9,11},{10,... | collective-permute-start | bytes 3145736 | tf_op jit(solution)/shard_map/ppermute | solution.py:13
  126.2 156.0 %collective-permute-start.9 = (bf16[256,2048]{0,1:T(8,128)(2,1)S(1)}, bf16[256,2048]{0,1:T(8,128)(2,1)}, u32[]{:S(2)}, u32[]{:S(2)}) collective-permute-start(bf16[256,2048]{0,1:T(8,128)(2,1)S(1)} %bitcast.141), channel_id=1, source_target_pairs={{2,0},{3,1},{4,2},{5,3},{6,4},{7,5},{8,6},{9,7},{10,8},{11,9},{12,... | collective-permute-start | bytes 3145736 | tf_op jit(solution)/shard_map/ppermute | solution.py:13
  132.4 154.3 %collective-permute-start.10 = (bf16[256,2048]{0,1:T(8,128)(2,1)S(1)}, bf16[256,2048]{0,1:T(8,128)(2,1)}, u32[]{:S(2)}, u32[]{:S(2)}) collective-permute-start(bf16[256,2048]{0,1:T(8,128)(2,1)S(1)} %bitcast.142), channel_id=1, source_target_pairs={{0,3},{1,4},{2,5},{3,6},{4,7},{5,8},{6,9},{7,10},{8,11},{9,12},{10... | collective-permute-start | bytes 3145736 | tf_op jit(solution)/shard_map/ppermute | solution.py:13
  204.1 161.2 %collective-permute-start.11 = (bf16[256,2048]{0,1:T(8,128)(2,1)S(1)}, bf16[256,2048]{0,1:T(8,128)(2,1)}, u32[]{:S(2)}, u32[]{:S(2)}) collective-permute-start(bf16[256,2048]{0,1:T(8,128)(2,1)S(1)} %bitcast.144), channel_id=1, source_target_pairs={{3,0},{4,1},{5,2},{6,3},{7,4},{8,5},{9,6},{10,7},{11,8},{12,9},{13... | collective-permute-start | bytes 3145736 | tf_op jit(solution)/shard_map/ppermute | solution.py:13
  216.0 153.6 %copy-start.2 = (bf16[256,2048]{0,1:T(8,128)(2,1)S(1)}, bf16[256,2048]{0,1:T(8,128)(2,1)}, u32[]{:S(2)}) copy-start(bf16[256,2048]{0,1:T(8,128)(2,1)} %copy.29) | copy-start | bytes 3145732
  216.0 154.7 %copy-start.3 = (bf16[256,2048]{0,1:T(8,128)(2,1)S(1)}, bf16[256,2048]{0,1:T(8,128)(2,1)}, u32[]{:S(2)}) copy-start(bf16[256,2048]{0,1:T(8,128)(2,1)} %copy.30) | copy-start | bytes 3145732
  218.4 156.4 %collective-permute-start.5 = (bf16[256,2048]{1,0:T(8,128)(2,1)}, bf16[256,2048]{1,0:T(8,128)(2,1)S(1)}, u32[]{:S(2)}, u32[]{:S(2)}) collective-permute-start(bf16[256,2048]{1,0:T(8,128)(2,1)} %bitcast.157), channel_id=1, source_target_pairs={{3,0},{4,1},{5,2},{6,3},{7,4},{8,5},{9,6},{10,7},{11,8},{12,9},{13... | collective-permute-start | bytes 3145736 | tf_op jit(solution)/shard_map/ppermute | solution.py:13
  220.4 151.3 %copy-start.1 = (bf16[256,2048]{0,1:T(8,128)(2,1)S(1)}, bf16[256,2048]{0,1:T(8,128)(2,1)}, u32[]{:S(2)}) copy-start(bf16[256,2048]{0,1:T(8,128)(2,1)} %copy.31) | copy-start | bytes 3145732
  222.9 160.2 %collective-permute-start.12 = (s32[256]{0:T(256)S(1)}, s32[256]{0:T(256)S(1)}, u32[]{:S(2)}, u32[]{:S(2)}) collective-permute-start(s32[256]{0:T(256)S(1)} %bitcast.161), channel_id=1, source_target_pairs={{0,1},{1,2},{2,3},{3,4},{4,5},{5,6},{6,7},{7,8},{8,9},{9,10},{10,1... | collective-permute-start | bytes 3080 | tf_op jit(solution)/shard_map/ppermute | solution.py:13
  282.2 104.7 %collective-permute-start.13 = (s32[256]{0:T(256)S(1)}, s32[256]{0:T(256)S(1)}, u32[]{:S(2)}, u32[]{:S(2)}) collective-permute-start(s32[256]{0:T(256)S(1)} %bitcast.162), channel_id=1, source_target_pairs={{1,0},{2,1},{3,2},{4,3},{5,4},{6,5},{7,6},{8,7},{9,8},{10,9},{11,1... | collective-permute-start | bytes 3080 | tf_op jit(solution)/shard_map/ppermute | solution.py:13
  286.7 100.2 %collective-permute-start.14 = (s32[256]{0:T(256)S(1)}, s32[256]{0:T(256)S(1)}, u32[]{:S(2)}, u32[]{:S(2)}) collective-permute-start(s32[256]{0:T(256)S(1)} %bitcast.163), channel_id=1, source_target_pairs={{0,2},{1,3},{2,4},{3,5},{4,6},{5,7},{6,8},{7,9},{8,10},{9,11},{10,... | collective-permute-start | bytes 3080 | tf_op jit(solution)/shard_map/ppermute | solution.py:13
  365.4 21.5 %collective-permute-start.15 = (s32[256]{0:T(256)S(1)}, s32[256]{0:T(256)}, u32[]{:S(2)}, u32[]{:S(2)}) collective-permute-start(s32[256]{0:T(256)S(1)} %bitcast.164), channel_id=1, source_target_pairs={{2,0},{3,1},{4,2},{5,3},{6,4},{7,5},{8,6},{9,7},{10,8},{11,9},{12,... | collective-permute-start | bytes 3080 | tf_op jit(solution)/shard_map/ppermute | solution.py:13
  375.9 11.0 %collective-permute-start.16 = (s32[256]{0:T(256)S(1)}, s32[256]{0:T(256)S(1)}, u32[]{:S(2)}, u32[]{:S(2)}) collective-permute-start(s32[256]{0:T(256)S(1)} %bitcast.165), channel_id=1, source_target_pairs={{0,3},{1,4},{2,5},{3,6},{4,7},{5,8},{6,9},{7,10},{8,11},{9,12},{10... | collective-permute-start | bytes 3080 | tf_op jit(solution)/shard_map/ppermute | solution.py:13
  383.0 5.8 collective-permute-start.17
  389.4 109.5 %copy-start.4 = (bf16[1,256,4096]{2,1,0:T(8,128)(2,1)S(1)}, bf16[1,256,4096]{2,1,0:T(8,128)(2,1)}, u32[]{:S(2)}) copy-start(bf16[1,256,4096]{2,1,0:T(8,128)(2,1)} %param.8) | copy-start | bytes 6291460
  389.4 4.0 copy-start.12
  389.4 4.1 copy-start.14
  389.4 7.1 %copy-start.16 = (s32[256]{0:T(256)}, s32[256]{0:T(256)S(1)}, u32[]{:S(2)}) copy-start(s32[256]{0:T(256)S(1)} %get-tuple-element.396) | copy-start | bytes 3076 | tf_op jit(solution)/shard_map/while
  389.4 7.1 %copy-start.18 = (s32[256]{0:T(256)}, s32[256]{0:T(256)S(1)}, u32[]{:S(2)}) copy-start(s32[256]{0:T(256)S(1)} %get-tuple-element.397) | copy-start | bytes 3076 | tf_op jit(solution)/shard_map/while
  389.4 10.3 %copy-start.5 = (bf16[256,16,128]{0,2,1:T(8,128)(2,1)S(1)}, bf16[256,16,128]{0,2,1:T(8,128)(2,1)}, u32[]{:S(2)}) copy-start(bf16[256,16,128]{0,2,1:T(8,128)(2,1)} %get-tuple-element.392) | copy-start | bytes 3145732 | tf_op jit(solution)/shard_map/while
  431.8 5.7 copy-start
  435.8 6.0 copy-start.10
  437.6 6.5 %copy-start.13 = (s32[256]{0:T(256)S(1)}, s32[256]{0:T(256)}, u32[]{:S(2)}) copy-start(s32[256]{0:T(256)} %copy-done.12) | copy-start | bytes 3076 | tf_op jit(solution)/shard_map/while
  437.6 6.5 %copy-start.15 = (s32[256]{0:T(256)S(1)}, s32[256]{0:T(256)}, u32[]{:S(2)}) copy-start(s32[256]{0:T(256)} %copy-done.14) | copy-start | bytes 3076 | tf_op jit(solution)/shard_map/while
  437.6 6.5 %copy-start.17 = (s32[256]{0:T(256)S(1)}, s32[256]{0:T(256)}, u32[]{:S(2)}) copy-start(s32[256]{0:T(256)} %copy-done.16) | copy-start | bytes 3076 | tf_op jit(solution)/shard_map/while
  437.6 6.5 %copy-start.19 = (s32[256]{0:T(256)S(1)}, s32[256]{0:T(256)}, u32[]{:S(2)}) copy-start(s32[256]{0:T(256)} %copy-done.18) | copy-start | bytes 3076 | tf_op jit(solution)/shard_map/while
  444.1 4.0 copy-start.12
  444.1 7.1 %copy-start.16 = (s32[256]{0:T(256)}, s32[256]{0:T(256)S(1)}, u32[]{:S(2)}) copy-start(s32[256]{0:T(256)S(1)} %get-tuple-element.396) | copy-start | bytes 3076 | tf_op jit(solution)/shard_map/while
  444.1 7.1 %copy-start.18 = (s32[256]{0:T(256)}, s32[256]{0:T(256)S(1)}, u32[]{:S(2)}) copy-start(s32[256]{0:T(256)S(1)} %get-tuple-element.397) | copy-start | bytes 3076 | tf_op jit(solution)/shard_map/while
  444.1 10.2 %copy-start.5 = (bf16[256,16,128]{0,2,1:T(8,128)(2,1)S(1)}, bf16[256,16,128]{0,2,1:T(8,128)(2,1)}, u32[]{:S(2)}) copy-start(bf16[256,16,128]{0,2,1:T(8,128)(2,1)} %get-tuple-element.392) | copy-start | bytes 3145732 | tf_op jit(solution)/shard_map/while
  486.5 5.7 copy-start
  490.4 5.9 copy-start.10
  492.2 6.5 %copy-start.13 = (s32[256]{0:T(256)S(1)}, s32[256]{0:T(256)}, u32[]{:S(2)}) copy-start(s32[256]{0:T(256)} %copy-done.12) | copy-start | bytes 3076 | tf_op jit(solution)/shard_map/while
  492.2 6.5 %copy-start.15 = (s32[256]{0:T(256)S(1)}, s32[256]{0:T(256)}, u32[]{:S(2)}) copy-start(s32[256]{0:T(256)} %copy-done.14) | copy-start | bytes 3076 | tf_op jit(solution)/shard_map/while
  492.2 6.5 %copy-start.17 = (s32[256]{0:T(256)S(1)}, s32[256]{0:T(256)}, u32[]{:S(2)}) copy-start(s32[256]{0:T(256)} %copy-done.16) | copy-start | bytes 3076 | tf_op jit(solution)/shard_map/while
  492.2 6.5 %copy-start.19 = (s32[256]{0:T(256)S(1)}, s32[256]{0:T(256)}, u32[]{:S(2)}) copy-start(s32[256]{0:T(256)} %copy-done.18) | copy-start | bytes 3076 | tf_op jit(solution)/shard_map/while
  509.7 99.8 %collective-permute-start.18 = (bf16[1,256,4096]{2,1,0:T(8,128)(2,1)S(1)}, bf16[1,256,4096]{2,1,0:T(8,128)(2,1)S(1)}, u32[]{:S(2)}, u32[]{:S(2)}) collective-permute-start(bf16[1,256,4096]{2,1,0:T(8,128)(2,1)S(1)} %fusion.76), channel_id=1, source_target_pairs={{0,32},{32,64},{64,96},{96,128},{128,160},{160,192},{192,224},{224... | collective-permute-start | bytes 6291464 | tf_op jit(solution)/shard_map/ppermute | solution.py:18
  (7 other events, 10.4 us)
Sparse Core Ops, SparseCore 0:
  9.2 290.8 all-gather.2
where the time goes:
time: 620 us; the launch traced here: 618 us
  starting transfers between devices  339 us (55%)
  waiting for transfers between devices  102 us (16%)
  matrix products  75.1 us (12%)
  local copies, waits for them, and re-layouts  46.7 us (8%)
  other arithmetic  37.1 us (6%)
  between operations  13.7 us (2%)
    ppermute x18, starting transfers between devices, passed_along(): lax.ppermute(value, axis, [(source, source + steps) for source in range(l...  335 us
    ppermute x1, waiting for transfers between devices, shifted(): lax.ppermute(array, axis, [(i, (i + by) % count) for i in range(count)])  95.2 us
    dot_general x14, matrix products, tile_scores(): jnp.einsum('qhd,khd->hqk', query_part, key_part[index], preferred_element...  42.1 us
    unnamed x38, local copies, waits for them, and re-layouts  28.4 us
    dot_general x14, matrix products, tile_values(): jnp.einsum('hqk,khd->qhd', piece, value_part[index], preferred_element_ty...  22.3 us
    convert_element_type x2, other arithmetic, head_group(): probs = (expo / jnp.sum(expo, axis=2, keepdims=True)).astype(jnp.bfloat16)  20.4 us
    reduce_sum x2, other arithmetic, head_group(): probs = (expo / jnp.sum(expo, axis=2, keepdims=True)).astype(jnp.bfloat16)  14.2 us
  transfers between devices with their start and end apart: 20, of which 5 were waited for; matrix products, arithmetic and copies ran while one was open for 23% of the time, Pallas kernels for 0%

commit v1 on v0

v1 whole, which is shorter than its diff:
```python
import functools

import jax
import jax.numpy as jnp
from jax import lax
from jax.experimental import pallas as pl
from jax.experimental.pallas import tpu as pltpu
from jax.sharding import Mesh, PartitionSpec as P

DH = 128
SPAN = 3
BLK = 256
LINE = 8
PAIR = 256
REACH = 2 * SPAN + 1
BLOCKS = LINE + 2 * SPAN
MARK = 16
LOG2E = 1.4426950408889634
WINDOWS = (2, 3, 4, 5, 7)
PARTS = 2
CHIPS = LINE // 2
MIB = 1024 * 1024


ANY = pl.BlockSpec(memory_space=pl.ANY)
WHOLE = pl.BlockSpec(memory_space=pltpu.VMEM)
SCALARS = pl.BlockSpec(memory_space=pltpu.SMEM)


def run_copies(pairs, sems):
    copies = [pltpu.make_async_copy(src, dst, sems.at[index]) for index, (src, dst) in enumerate(pairs)]
    for copy in copies:
        copy.start()
    for copy in copies:
        copy.wait()


def pack_body(here_ref, *refs):
    arrays, mine_ref, other_ref = refs[:-2], refs[-2], refs[-1]
    chip, core = here_ref[0], here_ref[1]
    for j in range(LINE):

        def store(out_ref, j=j):
            for index, ref in enumerate(arrays):
                if ref.shape[0] == BLK:
                    piece = ref[:, j * PAIR : (j + 1) * PAIR]
                    out_ref[(j // 2) ^ chip, index * BLK : (index + 1) * BLK] = piece
                else:
                    labels = (ref[...] + 1).astype(jnp.float32)
                    out_ref[(j // 2) ^ chip, index * BLK :] = jnp.broadcast_to(labels, (MARK, BLK)).astype(jnp.bfloat16)

        pl.when(core == j % 2)(functools.partial(store, mine_ref))
        pl.when(core != j % 2)(functools.partial(store, other_ref))


def pack(here, *arrays):
    height = sum(BLK if array.shape[0] == BLK else MARK for array in arrays)
    out = jax.ShapeDtypeStruct((CHIPS, height, PAIR), jnp.bfloat16)
    return pl.pallas_call(
        pack_body,
        in_specs=[SCALARS] + [WHOLE] * len(arrays),
        out_specs=[WHOLE, WHOLE],
        out_shape=[out, out],
        compiler_params=pltpu.CompilerParams(vmem_limit_bytes=16 * MIB),
        cost_estimate=pl.CostEstimate(flops=0, bytes_accessed=2 * MIB, transcendentals=0),
        name="pack",
    )(here, *arrays)


def combine_body(mine_ref, got_ref, *refs):
    outs, sems = refs[:-1], refs[-1]
    run_copies(
        [(ref.at[k + 1], out.at[s]) for k, out in enumerate(outs) for s, ref in enumerate((mine_ref, got_ref))], sems
    )


def combine(mine, got):
    out = jax.ShapeDtypeStruct((2, *mine.shape[1:]), jnp.bfloat16)
    return pl.pallas_call(
        combine_body,
        in_specs=[ANY] * 2,
        out_specs=[ANY] * (CHIPS - 1),
        out_shape=[out] * (CHIPS - 1),
        scratch_shapes=[pltpu.SemaphoreType.DMA((2 * (CHIPS - 1),))],
        compiler_params=pltpu.CompilerParams(vmem_limit_bytes=4 * MIB),
        cost_estimate=pl.CostEstimate(flops=0, bytes_accessed=2 * MIB, transcendentals=0),
        name="combine",
    )(mine, got)


def assemble_body(here_ref, mine_ref, got_ref, *refs):
    far, out_ref, sems = refs[:-2], refs[-2], refs[-1]
    chip, core = here_ref[0], here_ref[1]
    pairs = [(mine_ref.at[0], out_ref.at[2 * chip + core]), (got_ref.at[0], out_ref.at[2 * chip + 1 - core])]
    for k, ref in enumerate(far):
        place = 2 * (chip ^ (k + 1))
        pairs += [(ref.at[0], out_ref.at[place + core]), (ref.at[1], out_ref.at[place + 1 - core])]
    run_copies(pairs, sems)


def assemble(here, mine, got, far):
    return pl.pallas_call(
        assemble_body,
        in_specs=[SCALARS] + [ANY] * (1 + CHIPS),
        out_specs=ANY,
        out_shape=jax.ShapeDtypeStruct((LINE, *mine.shape[1:]), jnp.bfloat16),
        scratch_shapes=[pltpu.SemaphoreType.DMA((LINE,))],
        compiler_params=pltpu.CompilerParams(vmem_limit_bytes=4 * MIB),
        cost_estimate=pl.CostEstimate(flops=0, bytes_accessed=2 * MIB, transcendentals=0),
        name="assemble",
    )(here, mine, got, *far)


def divide_body(here_ref, near_ref, *refs):
    far, own_ref, send_ref, sems = refs[:-3], refs[-3], refs[-2], refs[-1]
    core = here_ref[1]
    pairs = []
    for k, ref in enumerate((near_ref.at[0], *far)):
        pairs += [(ref.at[core], own_ref.at[k]), (ref.at[1 - core], send_ref.at[k])]
    run_copies(pairs, sems)


def divide(here, near, far):
    out = jax.ShapeDtypeStruct((CHIPS, BLK, PAIR), jnp.bfloat16)
    return pl.pallas_call(
        divide_body,
        in_specs=[SCALARS] + [ANY] * CHIPS,
        out_specs=[ANY, ANY],
        out_shape=[out, out],
        scratch_shapes=[pltpu.SemaphoreType.DMA((LINE,))],
        compiler_params=pltpu.CompilerParams(vmem_limit_bytes=4 * MIB),
        cost_estimate=pl.CostEstimate(flops=0, bytes_accessed=2 * MIB, transcendentals=0),
        name="divide",
    )(here, near, *far)


def attention_body(here_ref, query_ref, left_ref, kv_ref, right_ref, out_ref, keys, values, labels, sems):
    step = pl.program_id(0)

    @pl.when(step == 0)
    def _():
        pairs = []
        for dst, first, rows in ((keys, 0, BLK), (values, BLK, BLK), (labels, 2 * BLK, MARK)):
            at = 0
            for src, count in ((left_ref, SPAN), (kv_ref, LINE), (right_ref, SPAN)):
                pairs.append((src.at[:, pl.ds(first, rows)], dst.at[pl.ds(at, count)]))
                at += count
        run_copies(pairs, sems)

    own = jnp.max(labels[step + SPAN].astype(jnp.float32), axis=0, keepdims=True)
    first, last = jnp.min(own), jnp.max(own)
    marks = jnp.max(labels[...].astype(jnp.float32), axis=1)
    top, low = jnp.max(marks, axis=1, keepdims=True), jnp.min(marks, axis=1, keepdims=True)
    place = lax.broadcasted_iota(jnp.int32, (BLOCKS, 1), 0)
    beyond = (place >= SPAN + LINE) & (top == 0.0)
    before = jnp.where((top < first) & ~beyond, 1.0, 0.0)
    until = jnp.where((low <= last) & ~beyond, 1.0, 0.0)
    start = jnp.maximum(jnp.sum(before).astype(jnp.int32), step)
    stop = jnp.minimum(jnp.sum(until).astype(jnp.int32), step + REACH)
    needed = stop - start
    own_column = jnp.broadcast_to(own, (BLK, BLK)).T[:, 0:1]
    scale = LOG2E / DH**0.5

    def window(size):
        begin = jnp.minimum(start, step + REACH - size)
        far = jnp.concatenate([labels[begin + t, 0:1, :] for t in range(size)], axis=1).astype(jnp.float32)
        match = own_column == far
        for head in range(PAIR // DH):
            lanes = slice(head * DH, (head + 1) * DH)
            query = query_ref[0, :, lanes]
            key = keys[pl.ds(begin, size), :, lanes].reshape(size * BLK, DH)
            value = values[pl.ds(begin, size), :, lanes].reshape(size * BLK, DH)
            scores = lax.dot_general(query, key, (((1,), (1,)), ((), ())), preferred_element_type=jnp.float32)
            scores = jnp.where(match, scores, -1e30)
            peak = jnp.max(scores, axis=1, keepdims=True)
            expo = jnp.exp2((scores - peak) * scale)
            total = jnp.sum(expo, axis=1, keepdims=True)
            summed = jnp.dot(expo.astype(jnp.bfloat16), value, preferred_element_type=jnp.float32)
            out_ref[0, 0, :, lanes] = (summed / total).astype(jnp.bfloat16)

    smaller = 0
    for size in WINDOWS:
        pl.when((needed > smaller) & (needed <= size))(functools.partial(window, size))
        smaller = size


def attention(here, query, kv):
    return pl.pallas_call(
        attention_body,
        grid_spec=pltpu.PrefetchScalarGridSpec(
            num_scalar_prefetch=1,
            grid=(LINE,),
            in_specs=[pl.BlockSpec((1, BLK, PAIR), lambda i, here: (i, 0, 0))] + [ANY] * 3,
            out_specs=pl.BlockSpec((1, 1, BLK, PAIR), lambda i, here: ((i // 2) ^ here[0], i % 2, 0, 0)),
            scratch_shapes=[
                pltpu.VMEM((BLOCKS, BLK, PAIR), jnp.bfloat16),
                pltpu.VMEM((BLOCKS, BLK, PAIR), jnp.bfloat16),
                pltpu.VMEM((BLOCKS, MARK, PAIR), jnp.bfloat16),
                pltpu.SemaphoreType.DMA((9,)),
            ],
        ),
        out_shape=jax.ShapeDtypeStruct((CHIPS, 2, BLK, PAIR), jnp.bfloat16),
        compiler_params=pltpu.CompilerParams(dimension_semantics=("arbitrary",), vmem_limit_bytes=24 * MIB),
        cost_estimate=pl.CostEstimate(flops=2400000000, bytes_accessed=9 * MIB, transcendentals=4700000),
        name="attention",
    )(here, query, *kv)


def project_body(place_ref, own_ref, got_ref, hidden_ref, matrix_ref, out_ref, rows_ref, total_ref, sems):
    copies = []
    for n in range(LINE):
        first = pl.multiple_of(place_ref[1 + n] * PAIR, PAIR)
        copies.append(pltpu.make_async_copy(matrix_ref.at[pl.ds(first, PAIR)], rows_ref.at[n], sems.at[n]))
    for copy in copies:
        copy.start()
    total_ref[...] = hidden_ref[...].astype(jnp.float32)
    columns = out_ref.shape[1]
    for first in range(0, LINE, 2):
        for n in (first, first + 1):
            copies[n].wait()
        rows = [own_ref[n] if n < CHIPS else got_ref[n - CHIPS] for n in (first, first + 1)]
        for at in range(0, columns, PAIR):
            lanes = slice(at, at + PAIR)
            product = jnp.dot(rows[0], rows_ref[first, :, lanes], preferred_element_type=jnp.float32)
            product += jnp.dot(rows[1], rows_ref[first + 1, :, lanes], preferred_element_type=jnp.float32)
            if first < LINE - 2:
                total_ref[:, lanes] += product
            else:
                out_ref[:, lanes] = (total_ref[:, lanes] + product).astype(jnp.bfloat16)


def project(place, attended, hidden, matrix):
    columns = matrix.shape[1]
    rows = pl.BlockSpec((CHIPS, BLK, PAIR), lambda i, place: (0, 0, 0))
    return pl.pallas_call(
        project_body,
        grid_spec=pltpu.PrefetchScalarGridSpec(
            num_scalar_prefetch=1,
            grid=(1,),
            in_specs=[rows, rows, pl.BlockSpec((BLK, columns), lambda i, place: (0, place[0])), ANY],
            out_specs=pl.BlockSpec((BLK, columns), lambda i, place: (0, 0)),
            scratch_shapes=[
                pltpu.VMEM((LINE, PAIR, columns), jnp.bfloat16),
                pltpu.VMEM((BLK, columns), jnp.float32),
                pltpu.SemaphoreType.DMA((LINE,)),
            ],
        ),
        out_shape=jax.ShapeDtypeStruct((BLK, columns), jnp.bfloat16),
        compiler_params=pltpu.CompilerParams(dimension_semantics=("arbitrary",), vmem_limit_bytes=60 * MIB),
        cost_estimate=pl.CostEstimate(flops=0, bytes_accessed=0, transcendentals=0),
        name="project",
    )(place, *attended, hidden, matrix)


def after(value, *others):
    return lax.optimization_barrier((value, *others))[0]


def to_next_section(value):
    return lax.ppermute(value, ("x", "zh"), [(s, (s + 1) % 8) for s in range(8)])


def to_other_core(value):
    return lax.ppermute(value, "c", [(0, 1), (1, 0)])


def across(pieces):
    return [lax.ppermute(piece, "zl", [(z, z ^ (k + 1)) for z in range(CHIPS)]) for k, piece in enumerate(pieces)]


def on_device(hidden, query, keyv, value, segments, out_weight):
    core, chip = lax.axis_index("c"), lax.axis_index("zl")
    here = jnp.stack([chip, core]).astype(jnp.int32)
    hidden, weight = hidden[0], out_weight[0]
    half = hidden.shape[1] // 2
    part = half // PARTS

    near = lax.all_gather(weight, ("zl", "c"), axis=0, tiled=True)

    kv, kv_other = pack(here, keyv[0], value[0], segments)
    kv_got = to_other_core(kv_other)
    heads, heads_other = pack(here, query[0])
    heads_got = to_other_core(heads_other)
    kv_far = across(combine(kv, kv_got))
    heads_out = combine(heads, heads_got)
    kv_far = [after(piece, *heads_out) for piece in kv_far]
    heads_far = across(heads_out)
    kv = assemble(here, kv, kv_got, kv_far)
    left = lax.ppermute(kv[LINE - SPAN :], "y", [(i, i + 1) for i in range(3)])
    right = lax.ppermute(kv[:SPAN], "y", [(i + 1, i) for i in range(3)])
    heads = assemble(here, heads, heads_got, heads_far)

    near = after(near, left, right, *heads_far)
    mine = []
    for p in range(PARTS):
        piece = lax.dynamic_slice_in_dim(near, core * half + p * part, part, 1)
        mine.append(lax.all_gather(piece, "y", axis=0, tiled=True))

    attended = attention(here, heads, (left, kv, right))
    far = across([attended[k] for k in range(1, CHIPS)])
    own, send = divide(here, attended, far)
    attended = [own, to_other_core(send)]

    out = jnp.zeros(hidden.shape, hidden.dtype)
    chips = chip ^ jnp.arange(CHIPS, dtype=jnp.int32)
    order = jnp.concatenate([2 * chips + core, 2 * chips + 1 - core])
    made, arrived = [], []
    for p in range(PARTS):
        matrix = after(mine[p], *attended, *made, *arrived)
        for which, matrix in ((core, matrix), (1 - core, to_other_core(matrix))):
            place = jnp.concatenate([(which * PARTS + p)[None], order]).astype(jnp.int32)
            ready = [after(rows, *made[-1:], *arrived[: 2 * p]) for rows in attended]
            made.append(project(place, ready, hidden, matrix))
            arrived.append(to_next_section(made[-1]))
            out = lax.dynamic_update_slice(out, arrived[-1], (0, which * half + p * part))
    return out[None]


def solution(mesh):
    wide = Mesh(mesh.devices.reshape(4, 2, 4, 4, 2), ("x", "zh", "y", "zl", "c"))
    section, ctx = ("x", "zh"), ("y", "zl", "c")
    return jax.shard_map(
        on_device,
        mesh=wide,
        in_specs=(
            P(section, ctx, None),
            P(section, ctx, None),
            P(section, ctx, None),
            P(section, ctx, None),
            P(section, ctx),
            P(section, ctx, None),
        ),
        out_specs=P(section, ctx, None),
        check_vma=False,
    )
```

time: 620 us -> 310 us (0.50)
  the two profiles are of different devices: /device:TPU:9 before, /device:TPU:32 now
where the time goes in v1:
time: 310 us; the launch traced here: 309 us
  waiting for transfers between devices  208 us (67%)
  Pallas kernels  44.6 us (14%)
  starting transfers between devices  31.9 us (10%)
  between operations  13.3 us (4%)
  local copies, waits for them, and re-layouts  9.51 us (3%)
    ppermute x9, waiting for transfers between devices, across(): lax.ppermute(piece, 'zl', [(z, z ^ k + 1) for z in range(CHIPS)])  113 us
    ppermute x4, waiting for transfers between devices, to_next_section(): lax.ppermute(value, ('x', 'zh'), [(s, (s + 1) % 8) for s in range(8)])  48.5 us
    all_gather x2, waiting for transfers between devices, on_device(): mine.append(lax.all_gather(piece, 'y', axis=0, tiled=True))  39 us
    pallas_call x4, Pallas kernels, project(): pl.pallas_call(project_body, grid_spec=pltpu.PrefetchScalarGridSpec(num_s...  22.5 us
    pallas_call x1, Pallas kernels, attention(): pl.pallas_call(attention_body, grid_spec=pltpu.PrefetchScalarGridSpec(num...  14.1 us
    ppermute x4, starting transfers between devices, to_next_section(): lax.ppermute(value, ('x', 'zh'), [(s, (s + 1) % 8) for s in range(8)])  12.5 us
    ppermute x9, starting transfers between devices, across(): lax.ppermute(piece, 'zl', [(z, z ^ k + 1) for z in range(CHIPS)])  12.4 us
    ppermute x5, waiting for transfers between devices, to_other_core(): return lax.ppermute(value, 'c', [(0, 1), (1, 0)])  6.5 us
  transfers between devices with their start and end apart: 23, of which 16 were waited for; matrix products, arithmetic and copies ran while one was open for 1% of the time, Pallas kernels for 14%

profile of v1, /device:TPU:32, one launch (start us, length us, event | category | flops | bytes accessed | tf_op | source)
XLA Modules:
  0.0 308.6 jit_solution(3527522169640805277)
XLA Ops:
  6.5 0.7 all-gather.9.cloned.1.call-update
  7.4 1.2 copy-done.1
  8.6 1.2 copy-done.2
  9.8 0.7 copy-done.4
  10.5 0.9 pack.3
  11.5 2.7 collective-permute-done.4.got_ref
  14.4 2.0 collective-permute-start.7
  16.4 2.3 collective-permute-start.6
  19.2 0.7 pack.2
  20.1 1.9 collective-permute-done.got_ref
  22.0 0.9 combine.2
  22.9 45.9 %collective-permute-done.7.refs_2_ = bf16[2,528,256]{2,1,0:T(8,128)(2,1)S(1)} collective-permute-done((bf16[2,528,256]{2,1,0:T(8,128)(2,1)S(1)}, bf16[2,528,256]{2,1,0:T(8,128)(2,1)S(1)}, u32[]{:S(2)}, u32[]{:S(2)}) %collective-permute-start.7) | collective-permute-done | bytes 540704 | tf_op jit(solution)/shard_map/ppermute | solution.py:268
  68.8 23.1 %collective-permute-done.6.refs_1_ = bf16[2,528,256]{2,1,0:T(8,128)(2,1)S(1)} collective-permute-done((bf16[2,528,256]{2,1,0:T(8,128)(2,1)S(1)}, bf16[2,528,256]{2,1,0:T(8,128)(2,1)S(1)}, u32[]{:S(2)}, u32[]{:S(2)}) %collective-permute-start.6) | collective-permute-done | bytes 540704 | tf_op jit(solution)/shard_map/ppermute | solution.py:268
  91.9 0.9 assemble.3.kv_ref
  92.8 1.3 fusion.1
  94.0 5.2 %collective-permute-start.8 = (bf16[3,528,256]{2,1,0:T(8,128)(2,1)}, bf16[3,528,256]{2,1,0:T(8,128)(2,1)}, u32[]{:S(2)}, u32[]{:S(2)}) collective-permute-start(bf16[3,528,256]{2,1,0:T(8,128)(2,1)} %get-tuple-element.56), channel_id=1, source_target_pairs={{0,8},{8,16},{16,24},{1,9},{9,17},{17,25},{2,10},{10,18},{18,26},{... | collective-permute-start | bytes 2433032 | tf_op jit(solution)/shard_map/ppermute | solution.py:289
  99.2 1.3 collective-permute-start.9
  100.5 1.9 collective-permute-start.1
  102.5 1.6 collective-permute-start.2
  104.6 6.9 %collective-permute-done.1.refs_0_ = bf16[2,256,256]{2,1,0:T(8,128)(2,1)S(1)} collective-permute-done((bf16[2,256,256]{2,1,0:T(8,128)(2,1)}, bf16[2,256,256]{2,1,0:T(8,128)(2,1)S(1)}, u32[]{:S(2)}, u32[]{:S(2)}) %collective-permute-start.1) | collective-permute-done | bytes 262176 | tf_op jit(solution)/shard_map/ppermute | solution.py:268
  111.5 10.5 %collective-permute-done.2.refs_1_ = bf16[2,256,256]{2,1,0:T(8,128)(2,1)} collective-permute-done((bf16[2,256,256]{2,1,0:T(8,128)(2,1)}, bf16[2,256,256]{2,1,0:T(8,128)(2,1)}, u32[]{:S(2)}, u32[]{:S(2)}) %collective-permute-start.2) | collective-permute-done | bytes 262176 | tf_op jit(solution)/shard_map/ppermute | solution.py:268
  121.9 5.2 %collective-permute-done.3.refs_2_ = bf16[2,256,256]{2,1,0:T(8,128)(2,1)} collective-permute-done((bf16[2,256,256]{2,1,0:T(8,128)(2,1)}, bf16[2,256,256]{2,1,0:T(8,128)(2,1)}, u32[]{:S(2)}, u32[]{:S(2)}) %collective-permute-start.3) | collective-permute-done | bytes 262176 | tf_op jit(solution)/shard_map/ppermute | solution.py:268
  127.1 3.0 constant_dynamic-slice_fusion
  130.9 2.4 assemble.2.query_ref
  133.3 14.1 %attention.1.near_ref = bf16[4,2,256,256]{3,2,1,0:T(8,128)(2,1)S(1)} custom-call(s32[2]{0:T(128)S(1)} %pad_add_fusion.here_ref, bf16[8,256,256]{2,1,0:T(8,128)(2,1)S(1)} %assemble.2.query_ref, bf16[3,528,256]{2,1,0:T(8,128)(2,1)} %collective-permute-done.8.left_ref, bf16[8,528,256]{2,1,0:T(8,128)(2,1)S(1)} %assemble.3.kv_ref, ...), custom_call_target="tpu_custom_call" | custom-call | flops 2400000000 | bytes 9437184 | tf_op jit(solution)/shard_map/attention/pallas_call | solution.py:188
  147.6 1.8 collective-permute-start.11
  149.4 1.7 collective-permute-start.12
  151.1 5.8 %collective-permute-done.10.refs_0_ = bf16[2,256,256]{2,1,0:T(8,128)(2,1)S(1)} collective-permute-done((bf16[2,256,256]{2,1,0:T(8,128)(2,1)S(1)}, bf16[2,256,256]{2,1,0:T(8,128)(2,1)S(1)}, u32[]{:S(2)}, u32[]{:S(2)}) %collective-permute-start.10) | collective-permute-done | bytes 262176 | tf_op jit(solution)/shard_map/ppermute | solution.py:268
  156.9 9.7 %collective-permute-done.11.refs_1_ = bf16[2,256,256]{2,1,0:T(8,128)(2,1)S(1)} collective-permute-done((bf16[2,256,256]{2,1,0:T(8,128)(2,1)S(1)}, bf16[2,256,256]{2,1,0:T(8,128)(2,1)S(1)}, u32[]{:S(2)}, u32[]{:S(2)}) %collective-permute-start.11) | collective-permute-done | bytes 262176 | tf_op jit(solution)/shard_map/ppermute | solution.py:268
  166.5 5.8 %collective-permute-done.12.refs_2_ = bf16[2,256,256]{2,1,0:T(8,128)(2,1)S(1)} collective-permute-done((bf16[2,256,256]{2,1,0:T(8,128)(2,1)S(1)}, bf16[2,256,256]{2,1,0:T(8,128)(2,1)S(1)}, u32[]{:S(2)}, u32[]{:S(2)}) %collective-permute-start.12) | collective-permute-done | bytes 262176 | tf_op jit(solution)/shard_map/ppermute | solution.py:268
  172.3 2.0 divide.1
  174.3 0.8 copy-done
  175.1 1.9 collective-permute-done.13.got_ref
  177.0 5.5 %all-gather.5.cloned.1.call-done.matrix_ref = bf16[2048,1024]{1,0:T(8,128)(2,1)} async-done(((bf16[512,1024]{1,0:T(8,128)(2,1)}), bf16[2048,1024]{1,0:T(8,128)(2,1)}) %all-gather.5.cloned.1.call-update) | async-done | bytes 4194320 | tf_op jit(solution)/shard_map/all_gather | solution.py:297
  183.1 0.7 add_add_fusion.3
  183.8 5.5 %project.4 = bf16[256,1024]{1,0:T(8,128)(2,1)} custom-call(s32[9]{0:T(128)} %add_add_fusion.place_ref, bf16[4,256,256]{2,1,0:T(8,128)(2,1)} %copy-done, bf16[4,256,256]{2,1,0:T(8,128)(2,1)} %copy-done.5, bf16[256,4096]{1,0:T(8,128)(2,1)} %bitcast.28, bf16[2048,1024]{1,0:T(8,128)(2,1)} %all-gather.5.cloned.1.call-done.matrix_ref), custom_call_target="tpu_custom_call" | custom-call | tf_op jit(solution)/shard_map/project/pallas_call | solution.py:235
  189.3 5.0 %collective-permute-start.14 = (bf16[256,1024]{1,0:T(8,128)(2,1)}, bf16[256,1024]{1,0:T(8,128)(2,1)S(1)}, u32[]{:S(2)}, u32[]{:S(2)}) collective-permute-start(bf16[256,1024]{1,0:T(8,128)(2,1)} %project.4), channel_id=1, source_target_pairs={{0,32},{32,64},{64,96},{96,128},{128,160},{160,192},{192,224},{224... | collective-permute-start | bytes 1572872 | tf_op jit(solution)/shard_map/ppermute | solution.py:260
  194.2 6.0 %project.5 = bf16[256,1024]{1,0:T(8,128)(2,1)} custom-call(s32[9]{0:T(128)} %get-tuple-element.61.place_ref, bf16[4,256,256]{2,1,0:T(8,128)(2,1)} %copy-done, bf16[4,256,256]{2,1,0:T(8,128)(2,1)} %copy-done.5, bf16[256,4096]{1,0:T(8,128)(2,1)} %bitcast.29, bf16[2048,1024]{1,0:T(8,128)(2,1)} %collective-permute-done.15.matrix_ref), custom_call_target="tpu_custom_call" | custom-call | tf_op jit(solution)/shard_map/project/pallas_call | solution.py:235
  200.2 1.8 collective-permute-start.16
  202.0 33.5 %all-gather.7.cloned.1.call-done.matrix_ref = bf16[2048,1024]{1,0:T(8,128)(2,1)} async-done(((bf16[512,1024]{1,0:T(8,128)(2,1)}), bf16[2048,1024]{1,0:T(8,128)(2,1)}) %all-gather.7.cloned.1.call-update) | async-done | bytes 4194320 | tf_op jit(solution)/shard_map/all_gather | solution.py:297
  235.5 8.1 %collective-permute-done.16 = bf16[256,1024]{1,0:T(8,128)(2,1)S(1)} collective-permute-done((bf16[256,1024]{1,0:T(8,128)(2,1)}, bf16[256,1024]{1,0:T(8,128)(2,1)S(1)}, u32[]{:S(2)}, u32[]{:S(2)}) %collective-permute-start.16) | collective-permute-done | bytes 524320 | tf_op jit(solution)/shard_map/ppermute | solution.py:260
  243.6 5.5 %project.6 = bf16[256,1024]{1,0:T(8,128)(2,1)} custom-call(s32[9]{0:T(128)} %get-tuple-element.62.place_ref, bf16[4,256,256]{2,1,0:T(8,128)(2,1)} %copy-done, bf16[4,256,256]{2,1,0:T(8,128)(2,1)} %copy-done.5, bf16[256,4096]{1,0:T(8,128)(2,1)} %bitcast.30, bf16[2048,1024]{1,0:T(8,128)(2,1)} %all-gather.7.cloned.1.call-done.matrix_ref), custom_call_target="tpu_custom_call" | custom-call | tf_op jit(solution)/shard_map/project/pallas_call | solution.py:235
  249.1 2.9 collective-permute-start.17
  252.0 5.5 %project.7 = bf16[256,1024]{1,0:T(8,128)(2,1)} custom-call(s32[9]{0:T(128)} %get-tuple-element.60.place_ref, bf16[4,256,256]{2,1,0:T(8,128)(2,1)} %copy-done, bf16[4,256,256]{2,1,0:T(8,128)(2,1)} %copy-done.5, bf16[256,4096]{1,0:T(8,128)(2,1)} %bitcast.31, bf16[2048,1024]{1,0:T(8,128)(2,1)} %collective-permute-done.18.matrix_ref), custom_call_target="tpu_custom_call" | custom-call | tf_op jit(solution)/shard_map/project/pallas_call | solution.py:235
  257.5 2.9 collective-permute-start.19
  260.7 29.3 %collective-permute-done.17 = bf16[256,1024]{1,0:T(8,128)(2,1)S(1)} collective-permute-done((bf16[256,1024]{1,0:T(8,128)(2,1)}, bf16[256,1024]{1,0:T(8,128)(2,1)S(1)}, u32[]{:S(2)}, u32[]{:S(2)}) %collective-permute-start.17) | collective-permute-done | bytes 524320 | tf_op jit(solution)/shard_map/ppermute | solution.py:260
  290.1 11.1 %collective-permute-done.19 = bf16[256,1024]{1,0:T(8,128)(2,1)S(1)} collective-permute-done((bf16[256,1024]{1,0:T(8,128)(2,1)}, bf16[256,1024]{1,0:T(8,128)(2,1)S(1)}, u32[]{:S(2)}, u32[]{:S(2)}) %collective-permute-start.19) | collective-permute-done | bytes 524320 | tf_op jit(solution)/shard_map/ppermute | solution.py:260
  301.2 0.8 bitcast_dynamic-update-slice_fusion
  (39 shorter events, 3.4 us)
Async XLA Ops:
  6.5 120.6 %all-gather.9.cloned.1.call-start = ((), (), s32[]{:S(2)}) async-start(), calls=%async_computation.2 | async-start | bytes 4718592 | tf_op jit(solution)/shard_map/all_gather | solution.py:278
  7.3 175.2 %all-gather.5.cloned.1.call-start = ((), (), s32[]{:S(2)}) async-start(), calls=%async_computation | async-start | bytes 5242880 | tf_op jit(solution)/shard_map/all_gather | solution.py:297
  7.4 1.2 copy-start.1
  8.6 1.2 copy-start.2
  9.8 0.7 copy-start.4
  10.5 8.7 %copy-start.3 = (bf16[1,256,2048]{2,1,0:T(8,128)(2,1)S(1)}, bf16[1,256,2048]{2,1,0:T(8,128)(2,1)}, u32[]{:S(2)}) copy-start(bf16[1,256,2048]{2,1,0:T(8,128)(2,1)} %param.7) | copy-start | bytes 3145732
  11.4 2.8 collective-permute-start.4
  14.4 54.3 %collective-permute-start.7 = (bf16[2,528,256]{2,1,0:T(8,128)(2,1)S(1)}, bf16[2,528,256]{2,1,0:T(8,128)(2,1)S(1)}, u32[]{:S(2)}, u32[]{:S(2)}) collective-permute-start(bf16[2,528,256]{2,1,0:T(8,128)(2,1)S(1)} %get-tuple-element.40), channel_id=1, source_target_pairs={{0,6},{2,4},{4,2},{6,0},{1,7},{3,5},{5,3},{7,1},{8,14},{10,12},{12... | collective-permute-start | bytes 1622024 | tf_op jit(solution)/shard_map/ppermute | solution.py:268
  16.4 75.5 %collective-permute-start.6 = (bf16[2,528,256]{2,1,0:T(8,128)(2,1)S(1)}, bf16[2,528,256]{2,1,0:T(8,128)(2,1)S(1)}, u32[]{:S(2)}, u32[]{:S(2)}) collective-permute-start(bf16[2,528,256]{2,1,0:T(8,128)(2,1)S(1)} %get-tuple-element.38), channel_id=1, source_target_pairs={{0,4},{2,6},{4,0},{6,2},{1,5},{3,7},{5,1},{7,3},{8,12},{10,14},{12... | collective-permute-start | bytes 1622024 | tf_op jit(solution)/shard_map/ppermute | solution.py:268
  18.7 73.2 %collective-permute-start.5 = (bf16[2,528,256]{2,1,0:T(8,128)(2,1)S(1)}, bf16[2,528,256]{2,1,0:T(8,128)(2,1)S(1)}, u32[]{:S(2)}, u32[]{:S(2)}) collective-permute-start(bf16[2,528,256]{2,1,0:T(8,128)(2,1)S(1)} %get-tuple-element.36), channel_id=1, source_target_pairs={{0,2},{2,0},{4,6},{6,4},{1,3},{3,1},{5,7},{7,5},{8,10},{10,8},{12,... | collective-permute-start | bytes 1622024 | tf_op jit(solution)/shard_map/ppermute | solution.py:268
  20.0 2.0 collective-permute-start
  94.0 33.1 %collective-permute-start.8 = (bf16[3,528,256]{2,1,0:T(8,128)(2,1)}, bf16[3,528,256]{2,1,0:T(8,128)(2,1)}, u32[]{:S(2)}, u32[]{:S(2)}) collective-permute-start(bf16[3,528,256]{2,1,0:T(8,128)(2,1)} %get-tuple-element.56), channel_id=1, source_target_pairs={{0,8},{8,16},{16,24},{1,9},{9,17},{17,25},{2,10},{10,18},{18,26},{... | collective-permute-start | bytes 2433032 | tf_op jit(solution)/shard_map/ppermute | solution.py:289
  99.2 27.9 %collective-permute-start.9 = (bf16[3,528,256]{2,1,0:T(8,128)(2,1)}, bf16[3,528,256]{2,1,0:T(8,128)(2,1)}, u32[]{:S(2)}, u32[]{:S(2)}) collective-permute-start(bf16[3,528,256]{2,1,0:T(8,128)(2,1)} %get-tuple-element.55), channel_id=1, source_target_pairs={{8,0},{16,8},{24,16},{9,1},{17,9},{25,17},{10,2},{18,10},{26,18},{... | collective-permute-start | bytes 2433032 | tf_op jit(solution)/shard_map/ppermute | solution.py:290
  100.5 11.0 %collective-permute-start.1 = (bf16[2,256,256]{2,1,0:T(8,128)(2,1)}, bf16[2,256,256]{2,1,0:T(8,128)(2,1)S(1)}, u32[]{:S(2)}, u32[]{:S(2)}) collective-permute-start(bf16[2,256,256]{2,1,0:T(8,128)(2,1)} %get-tuple-element.31), channel_id=1, source_target_pairs={{0,2},{2,0},{4,6},{6,4},{1,3},{3,1},{5,7},{7,5},{8,10},{10,8},{12,... | collective-permute-start | bytes 786440 | tf_op jit(solution)/shard_map/ppermute | solution.py:268
  102.5 19.5 %collective-permute-start.2 = (bf16[2,256,256]{2,1,0:T(8,128)(2,1)}, bf16[2,256,256]{2,1,0:T(8,128)(2,1)}, u32[]{:S(2)}, u32[]{:S(2)}) collective-permute-start(bf16[2,256,256]{2,1,0:T(8,128)(2,1)} %get-tuple-element.32), channel_id=1, source_target_pairs={{0,4},{2,6},{4,0},{6,2},{1,5},{3,7},{5,1},{7,3},{8,12},{10,14},{12... | collective-permute-start | bytes 786440 | tf_op jit(solution)/shard_map/ppermute | solution.py:268
  104.1 23.0 %collective-permute-start.3 = (bf16[2,256,256]{2,1,0:T(8,128)(2,1)}, bf16[2,256,256]{2,1,0:T(8,128)(2,1)}, u32[]{:S(2)}, u32[]{:S(2)}) collective-permute-start(bf16[2,256,256]{2,1,0:T(8,128)(2,1)} %get-tuple-element.33), channel_id=1, source_target_pairs={{0,6},{2,4},{4,2},{6,0},{1,7},{3,5},{5,3},{7,1},{8,14},{10,12},{12... | collective-permute-start | bytes 786440 | tf_op jit(solution)/shard_map/ppermute | solution.py:268
  130.2 105.3 %all-gather.7.cloned.1.call-start = ((), (), s32[]{:S(2)}) async-start(), calls=%async_computation.1 | async-start | bytes 5242880 | tf_op jit(solution)/shard_map/all_gather | solution.py:297
  147.5 9.3 %collective-permute-start.10 = (bf16[2,256,256]{2,1,0:T(8,128)(2,1)S(1)}, bf16[2,256,256]{2,1,0:T(8,128)(2,1)S(1)}, u32[]{:S(2)}, u32[]{:S(2)}) collective-permute-start(bf16[2,256,256]{2,1,0:T(8,128)(2,1)S(1)} %get-tuple-element.59), channel_id=1, source_target_pairs={{0,2},{2,0},{4,6},{6,4},{1,3},{3,1},{5,7},{7,5},{8,10},{10,8},{12,... | collective-permute-start | bytes 786440 | tf_op jit(solution)/shard_map/ppermute | solution.py:268
  147.6 18.9 %collective-permute-start.11 = (bf16[2,256,256]{2,1,0:T(8,128)(2,1)S(1)}, bf16[2,256,256]{2,1,0:T(8,128)(2,1)S(1)}, u32[]{:S(2)}, u32[]{:S(2)}) collective-permute-start(bf16[2,256,256]{2,1,0:T(8,128)(2,1)S(1)} %get-tuple-element.58), channel_id=1, source_target_pairs={{0,4},{2,6},{4,0},{6,2},{1,5},{3,7},{5,1},{7,3},{8,12},{10,14},{12... | collective-permute-start | bytes 786440 | tf_op jit(solution)/shard_map/ppermute | solution.py:268
  149.4 22.9 %collective-permute-start.12 = (bf16[2,256,256]{2,1,0:T(8,128)(2,1)S(1)}, bf16[2,256,256]{2,1,0:T(8,128)(2,1)S(1)}, u32[]{:S(2)}, u32[]{:S(2)}) collective-permute-start(bf16[2,256,256]{2,1,0:T(8,128)(2,1)S(1)} %get-tuple-element.57), channel_id=1, source_target_pairs={{0,6},{2,4},{4,2},{6,0},{1,7},{3,5},{5,3},{7,1},{8,14},{10,12},{12... | collective-permute-start | bytes 786440 | tf_op jit(solution)/shard_map/ppermute | solution.py:268
  174.3 0.8 copy-start
  175.1 1.9 collective-permute-start.13
  177.0 6.7 %copy-start.5 = (bf16[4,256,256]{2,1,0:T(8,128)(2,1)}, bf16[4,256,256]{2,1,0:T(8,128)(2,1)S(1)}, u32[]{:S(2)}) copy-start(bf16[4,256,256]{2,1,0:T(8,128)(2,1)S(1)} %collective-permute-done.13.got_ref) | copy-start | bytes 1572868
  182.5 11.7 %collective-permute-start.15 = (bf16[2048,1024]{1,0:T(8,128)(2,1)}, bf16[2048,1024]{1,0:T(8,128)(2,1)}, u32[]{:S(2)}, u32[]{:S(2)}) collective-permute-start(bf16[2048,1024]{1,0:T(8,128)(2,1)} %all-gather.5.cloned.1.call-done.matrix_ref), channel_id=1, source_target_pairs={{0,1},{1,0},{2,3},{3,2},{4,5},{5,4},{6,7},{7,6},{8,9},{9,8},{10,11... | collective-permute-start | bytes 12582920 | tf_op jit(solution)/shard_map/ppermute | solution.py:264
  189.3 46.3 %collective-permute-start.14 = (bf16[256,1024]{1,0:T(8,128)(2,1)}, bf16[256,1024]{1,0:T(8,128)(2,1)S(1)}, u32[]{:S(2)}, u32[]{:S(2)}) collective-permute-start(bf16[256,1024]{1,0:T(8,128)(2,1)} %project.4), channel_id=1, source_target_pairs={{0,32},{32,64},{64,96},{96,128},{128,160},{160,192},{192,224},{224... | collective-permute-start | bytes 1572872 | tf_op jit(solution)/shard_map/ppermute | solution.py:260
  200.2 43.4 %collective-permute-start.16 = (bf16[256,1024]{1,0:T(8,128)(2,1)}, bf16[256,1024]{1,0:T(8,128)(2,1)S(1)}, u32[]{:S(2)}, u32[]{:S(2)}) collective-permute-start(bf16[256,1024]{1,0:T(8,128)(2,1)} %project.5), channel_id=1, source_target_pairs={{0,32},{32,64},{64,96},{96,128},{128,160},{160,192},{192,224},{224... | collective-permute-start | bytes 1572872 | tf_op jit(solution)/shard_map/ppermute | solution.py:260
  243.6 8.4 %collective-permute-start.18 = (bf16[2048,1024]{1,0:T(8,128)(2,1)}, bf16[2048,1024]{1,0:T(8,128)(2,1)}, u32[]{:S(2)}, u32[]{:S(2)}) collective-permute-start(bf16[2048,1024]{1,0:T(8,128)(2,1)} %all-gather.7.cloned.1.call-done.matrix_ref), channel_id=1, source_target_pairs={{0,1},{1,0},{2,3},{3,2},{4,5},{5,4},{6,7},{7,6},{8,9},{9,8},{10,11... | collective-permute-start | bytes 12582920 | tf_op jit(solution)/shard_map/ppermute | solution.py:264
  249.1 40.9 %collective-permute-start.17 = (bf16[256,1024]{1,0:T(8,128)(2,1)}, bf16[256,1024]{1,0:T(8,128)(2,1)S(1)}, u32[]{:S(2)}, u32[]{:S(2)}) collective-permute-start(bf16[256,1024]{1,0:T(8,128)(2,1)} %project.6), channel_id=1, source_target_pairs={{0,32},{32,64},{64,96},{96,128},{128,160},{160,192},{192,224},{224... | collective-permute-start | bytes 1572872 | tf_op jit(solution)/shard_map/ppermute | solution.py:260
  257.5 43.7 %collective-permute-start.19 = (bf16[256,1024]{1,0:T(8,128)(2,1)}, bf16[256,1024]{1,0:T(8,128)(2,1)S(1)}, u32[]{:S(2)}, u32[]{:S(2)}) collective-permute-start(bf16[256,1024]{1,0:T(8,128)(2,1)} %project.7), channel_id=1, source_target_pairs={{0,32},{32,64},{64,96},{96,128},{128,160},{160,192},{192,224},{224... | collective-permute-start | bytes 1572872 | tf_op jit(solution)/shard_map/ppermute | solution.py:260
  290.1 11.2 %copy-start.6 = (bf16[1,256,4096]{2,1,0:T(8,128)(2,1)}, bf16[1,256,4096]{2,1,0:T(8,128)(2,1)S(1)}, u32[]{:S(2)}) copy-start(bf16[1,256,4096]{2,1,0:T(8,128)(2,1)S(1)} %bitcast_dynamic-update-slice_fusion.1) | copy-start | bytes 6291460
Sparse Core Ops, SparseCore 0:
  9.1 93.9 all-gather.8
  130.3 52.0 all-gather.4
  184.3 51.1 all-gather.6

commit v2 on v1

--- a/solution.py
+++ b/solution.py
@@ -69,9 +69,7 @@
 
 def combine_body(mine_ref, got_ref, *refs):
     outs, sems = refs[:-1], refs[-1]
-    run_copies(
-        [(ref.at[k + 1], out.at[s]) for k, out in enumerate(outs) for s, ref in enumerate((mine_ref, got_ref))], sems
-    )
+    run_copies([(ref.at[k], out.at[s]) for k, out in enumerate(outs) for s, ref in enumerate((mine_ref, got_ref))], sems)
 
 
 def combine(mine, got):
@@ -79,36 +77,36 @@
     return pl.pallas_call(
         combine_body,
         in_specs=[ANY] * 2,
-        out_specs=[ANY] * (CHIPS - 1),
-        out_shape=[out] * (CHIPS - 1),
-        scratch_shapes=[pltpu.SemaphoreType.DMA((2 * (CHIPS - 1),))],
+        out_specs=[pl.BlockSpec(memory_space=pltpu.HBM)] * CHIPS,
+        out_shape=[out] * CHIPS,
+        scratch_shapes=[pltpu.SemaphoreType.DMA((LINE,))],
         compiler_params=pltpu.CompilerParams(vmem_limit_bytes=4 * MIB),
         cost_estimate=pl.CostEstimate(flops=0, bytes_accessed=2 * MIB, transcendentals=0),
         name="combine",
     )(mine, got)
 
 
-def assemble_body(here_ref, mine_ref, got_ref, *refs):
+def assemble_body(here_ref, *refs):
     far, out_ref, sems = refs[:-2], refs[-2], refs[-1]
     chip, core = here_ref[0], here_ref[1]
-    pairs = [(mine_ref.at[0], out_ref.at[2 * chip + core]), (got_ref.at[0], out_ref.at[2 * chip + 1 - core])]
+    pairs = []
     for k, ref in enumerate(far):
-        place = 2 * (chip ^ (k + 1))
+        place = 2 * (chip ^ k)
         pairs += [(ref.at[0], out_ref.at[place + core]), (ref.at[1], out_ref.at[place + 1 - core])]
     run_copies(pairs, sems)
 
 
-def assemble(here, mine, got, far):
+def assemble(here, far):
     return pl.pallas_call(
         assemble_body,
-        in_specs=[SCALARS] + [ANY] * (1 + CHIPS),
+        in_specs=[SCALARS] + [ANY] * CHIPS,
         out_specs=ANY,
-        out_shape=jax.ShapeDtypeStruct((LINE, *mine.shape[1:]), jnp.bfloat16),
+        out_shape=jax.ShapeDtypeStruct((LINE, *far[0].shape[1:]), jnp.bfloat16),
         scratch_shapes=[pltpu.SemaphoreType.DMA((LINE,))],
         compiler_params=pltpu.CompilerParams(vmem_limit_bytes=4 * MIB),
         cost_estimate=pl.CostEstimate(flops=0, bytes_accessed=2 * MIB, transcendentals=0),
         name="assemble",
-    )(here, mine, got, *far)
+    )(here, *far)
 
 
 def divide_body(here_ref, near_ref, *refs):
@@ -206,48 +204,50 @@
     )(here, query, *kv)
 
 
-def project_body(place_ref, own_ref, got_ref, hidden_ref, matrix_ref, out_ref, rows_ref, total_ref, sems):
+def project_body(place_ref, own_ref, got_ref, hidden_ref, matrix_ref, out_ref, rows_ref, rest_ref, total_ref, sems):
+    columns = out_ref.shape[1]
     copies = []
     for n in range(LINE):
         first = pl.multiple_of(place_ref[1 + n] * PAIR, PAIR)
         copies.append(pltpu.make_async_copy(matrix_ref.at[pl.ds(first, PAIR)], rows_ref.at[n], sems.at[n]))
-    for copy in copies:
+    first = pl.multiple_of(place_ref[0] * columns, columns)
+    rest = pltpu.make_async_copy(hidden_ref.at[:, pl.ds(first, columns)], rest_ref, sems.at[LINE])
+    for copy in (*copies, rest):
         copy.start()
-    total_ref[...] = hidden_ref[...].astype(jnp.float32)
-    columns = out_ref.shape[1]
     for first in range(0, LINE, 2):
         for n in (first, first + 1):
             copies[n].wait()
+        if first == LINE - 2:
+            rest.wait()
         rows = [own_ref[n] if n < CHIPS else got_ref[n - CHIPS] for n in (first, first + 1)]
         for at in range(0, columns, PAIR):
             lanes = slice(at, at + PAIR)
             product = jnp.dot(rows[0], rows_ref[first, :, lanes], preferred_element_type=jnp.float32)
             product += jnp.dot(rows[1], rows_ref[first + 1, :, lanes], preferred_element_type=jnp.float32)
-            if first < LINE - 2:
+            if first == 0:
+                total_ref[:, lanes] = product
+            elif first < LINE - 2:
                 total_ref[:, lanes] += product
             else:
-                out_ref[:, lanes] = (total_ref[:, lanes] + product).astype(jnp.bfloat16)
+                total = rest_ref[:, lanes].astype(jnp.float32) + (total_ref[:, lanes] + product)
+                out_ref[:, lanes] = total.astype(jnp.bfloat16)
 
 
 def project(place, attended, hidden, matrix):
     columns = matrix.shape[1]
-    rows = pl.BlockSpec((CHIPS, BLK, PAIR), lambda i, place: (0, 0, 0))
     return pl.pallas_call(
         project_body,
-        grid_spec=pltpu.PrefetchScalarGridSpec(
-            num_scalar_prefetch=1,
-            grid=(1,),
-            in_specs=[rows, rows, pl.BlockSpec((BLK, columns), lambda i, place: (0, place[0])), ANY],
-            out_specs=pl.BlockSpec((BLK, columns), lambda i, place: (0, 0)),
-            scratch_shapes=[
-                pltpu.VMEM((LINE, PAIR, columns), jnp.bfloat16),
-                pltpu.VMEM((BLK, columns), jnp.float32),
-                pltpu.SemaphoreType.DMA((LINE,)),
-            ],
-        ),
+        in_specs=[SCALARS, WHOLE, WHOLE, ANY, ANY],
+        out_specs=WHOLE,
+        scratch_shapes=[
+            pltpu.VMEM((LINE, PAIR, columns), jnp.bfloat16),
+            pltpu.VMEM((BLK, columns), jnp.bfloat16),
+            pltpu.VMEM((BLK, columns), jnp.float32),
+            pltpu.SemaphoreType.DMA((LINE + 1,)),
+        ],
         out_shape=jax.ShapeDtypeStruct((BLK, columns), jnp.bfloat16),
-        compiler_params=pltpu.CompilerParams(dimension_semantics=("arbitrary",), vmem_limit_bytes=60 * MIB),
-        cost_estimate=pl.CostEstimate(flops=0, bytes_accessed=0, transcendentals=0),
+        compiler_params=pltpu.CompilerParams(vmem_limit_bytes=60 * MIB),
+        cost_estimate=pl.CostEstimate(flops=2, bytes_accessed=2, transcendentals=0),
         name="project",
     )(place, *attended, hidden, matrix)
 
@@ -265,7 +265,8 @@
 
 
 def across(pieces):
-    return [lax.ppermute(piece, "zl", [(z, z ^ (k + 1)) for z in range(CHIPS)]) for k, piece in enumerate(pieces)]
+    far = [lax.ppermute(piece, "zl", [(z, z ^ k) for z in range(CHIPS)]) for k, piece in enumerate(pieces) if k]
+    return [pieces[0], *far]
 
 
 def on_device(hidden, query, keyv, value, segments, out_weight):
@@ -275,38 +276,44 @@
     half = hidden.shape[1] // 2
     part = half // PARTS
 
-    near = lax.all_gather(weight, ("zl", "c"), axis=0, tiled=True)
-
     kv, kv_other = pack(here, keyv[0], value[0], segments)
-    kv_got = to_other_core(kv_other)
+    kv_out = combine(kv, to_other_core(kv_other))
     heads, heads_other = pack(here, query[0])
-    heads_got = to_other_core(heads_other)
-    kv_far = across(combine(kv, kv_got))
-    heads_out = combine(heads, heads_got)
-    kv_far = [after(piece, *heads_out) for piece in kv_far]
+    heads_out = combine(heads, to_other_core(heads_other))
+
+    rows = [lax.dynamic_slice_in_dim(weight, which * half, half, 1) for which in (core, 1 - core)]
+    rows[1] = to_other_core(rows[1])
+    rows = [jnp.where(core == place, *rows) for place in (0, 1)]
+    rows = [jnp.concatenate([row[:, p * part : (p + 1) * part] for row in rows], axis=0) for p in range(PARTS)]
+
+    def gather(piece, axis):
+        return lax.all_gather(piece, axis, axis=0, tiled=True)
+
+    first = gather(rows[0], "zl")
+    kv_far = across(kv_out)
+    first = after(first, kv_far[1], kv_far[3], *heads_out)
+    kv_far[2] = after(kv_far[2], first)
+    first = gather(first, "y")
     heads_far = across(heads_out)
-    kv = assemble(here, kv, kv_got, kv_far)
+    kv = assemble(here, kv_far)
     left = lax.ppermute(kv[LINE - SPAN :], "y", [(i, i + 1) for i in range(3)])
     right = lax.ppermute(kv[:SPAN], "y", [(i + 1, i) for i in range(3)])
-    heads = assemble(here, heads, heads_got, heads_far)
-
-    near = after(near, left, right, *heads_far)
-    mine = []
-    for p in range(PARTS):
-        piece = lax.dynamic_slice_in_dim(near, core * half + p * part, part, 1)
-        mine.append(lax.all_gather(piece, "y", axis=0, tiled=True))
+    heads = assemble(here, heads_far)
+    second = gather(after(rows[1], left, right, *heads_far, first), "zl")
 
     attended = attention(here, heads, (left, kv, right))
-    far = across([attended[k] for k in range(1, CHIPS)])
-    own, send = divide(here, attended, far)
+    far = across([attended[k] for k in range(CHIPS)])
+    first = after(first, *far)
+    own, send = divide(here, attended, far[1:])
     attended = [own, to_other_core(send)]
+    second = gather(after(second, *attended), "y")
 
     out = jnp.zeros(hidden.shape, hidden.dtype)
     chips = chip ^ jnp.arange(CHIPS, dtype=jnp.int32)
     order = jnp.concatenate([2 * chips + core, 2 * chips + 1 - core])
     made, arrived = [], []
-    for p in range(PARTS):
-        matrix = after(mine[p], *attended, *made, *arrived)
+    for p, matrix in enumerate((first, after(second, *attended))):
+        matrix = after(matrix, *made, *arrived)
         for which, matrix in ((core, matrix), (1 - core, to_other_core(matrix))):
             place = jnp.concatenate([(which * PARTS + p)[None], order]).astype(jnp.int32)
             ready = [after(rows, *made[-1:], *arrived[: 2 * p]) for rows in attended]

time: 310 us -> 316 us (1.019)
  local copies, waits for them, and re-layouts: 9.51 us -> 13.6 us
    ppermute x1, waiting for transfers between devices: 0.01 us -> 6.8 us  [on_device(): right = lax.ppermute(kv[:SPAN], 'y', [(i + 1, i) for i in range(3)])]
    ppermute x9, waiting for transfers between devices: 113 us -> 106 us  [across(): lax.ppermute(piece, 'zl', [(z, z ^ k) for z in range(CHIPS)])]
    all_gather x3 -> x4, waiting for transfers between devices: 39 us -> 44.7 us  [gather(): return lax.all_gather(piece, axis, axis=0, tiled=True)]
    unnamed x14 -> x36, local copies, waits for them, and re-layouts: 3.95 us -> 9.28 us
    ppermute x5 -> x6, waiting for transfers between devices: 6.5 us -> 4.68 us  [to_other_core(): return lax.ppermute(value, 'c', [(0, 1), (1, 0)])]
  transfers between devices with their start and end apart: 23 -> 25, of which waited for: 16 -> 19; matrix products, arithmetic and copies ran while one was open for 1% -> 2% of each run, Pallas kernels for 14% -> 13%
where the time goes in v2:
time: 316 us; the launch traced here: 315 us
  waiting for transfers between devices  208 us (66%)
  Pallas kernels  42.4 us (13%)
  starting transfers between devices  34.3 us (11%)
  local copies, waits for them, and re-layouts  13.6 us (4%)
  between operations  13.4 us (4%)
    ppermute x9, waiting for transfers between devices, across(): lax.ppermute(piece, 'zl', [(z, z ^ k) for z in range(CHIPS)])  106 us
    ppermute x4, waiting for transfers between devices, to_next_section(): lax.ppermute(value, ('x', 'zh'), [(s, (s + 1) % 8) for s in range(8)])  46.2 us
    all_gather x4, waiting for transfers between devices, gather(): return lax.all_gather(piece, axis, axis=0, tiled=True)  44.7 us
    pallas_call x4, Pallas kernels, project(): pl.pallas_call(project_body, in_specs=[SCALARS, WHOLE, WHOLE, ANY, ANY],...  19.8 us
    pallas_call x1, Pallas kernels, attention(): pl.pallas_call(attention_body, grid_spec=pltpu.PrefetchScalarGridSpec(num...  13.7 us
    ppermute x4, starting transfers between devices, to_next_section(): lax.ppermute(value, ('x', 'zh'), [(s, (s + 1) % 8) for s in range(8)])  13.3 us
    ppermute x9, starting transfers between devices, across(): lax.ppermute(piece, 'zl', [(z, z ^ k) for z in range(CHIPS)])  13.1 us
    unnamed x36, local copies, waits for them, and re-layouts  9.28 us
  transfers between devices with their start and end apart: 25, of which 19 were waited for; matrix products, arithmetic and copies ran while one was open for 2% of the time, Pallas kernels for 13%

profile of v2, /device:TPU:32, one launch (start us, length us, event | category | flops | bytes accessed | tf_op | source)
XLA Modules:
  0.0 315.3 jit_solution(13006956975866914651)
XLA Ops:
  6.5 1.0 dynamic-slice_bitcast_fusion
  7.8 1.2 copy-done.1
  9.0 1.2 copy-done.2
  10.9 1.8 pack.3
  14.9 0.9 collective-permute-done.4.got_ref
  17.7 1.9 collective-permute-start.5
  19.6 2.0 collective-permute-start.8
  22.4 1.9 collective-permute-done.got_ref
  24.3 1.2 combine.2
  25.5 8.7 %collective-permute-done.5.refs_1_ = bf16[2,528,256]{2,1,0:T(8,128)(2,1)S(1)} collective-permute-done((bf16[2,528,256]{2,1,0:T(8,128)(2,1)S(1)}, bf16[2,528,256]{2,1,0:T(8,128)(2,1)S(1)}, u32[]{:S(2)}, u32[]{:S(2)}) %collective-permute-start.5) | collective-permute-done | bytes 540704 | tf_op jit(solution)/shard_map/ppermute | solution.py:268
  34.3 0.8 copy-done.6
  35.1 15.6 %collective-permute-done.8.refs_3_ = bf16[2,528,256]{2,1,0:T(8,128)(2,1)S(1)} collective-permute-done((bf16[2,528,256]{2,1,0:T(8,128)(2,1)S(1)}, bf16[2,528,256]{2,1,0:T(8,128)(2,1)S(1)}, u32[]{:S(2)}, u32[]{:S(2)}) %collective-permute-start.8) | collective-permute-done | bytes 540704 | tf_op jit(solution)/shard_map/ppermute | solution.py:268
  51.5 11.4 %all-gather.5.cloned.1.call-done = bf16[512,1024]{1,0:T(8,128)(2,1)} async-done(((bf16[128,1024]{1,0:T(8,128)(2,1)}), bf16[512,1024]{1,0:T(8,128)(2,1)}) %all-gather.5.cloned.1.call-update) | async-done | bytes 1048592 | tf_op jit(solution)/shard_map/all_gather | solution.py:290
  63.0 1.6 collective-permute-start.6
  64.5 23.1 %collective-permute-done.6.refs_2_ = bf16[2,528,256]{2,1,0:T(8,128)(2,1)S(1)} collective-permute-done((bf16[2,528,256]{2,1,0:T(8,128)(2,1)S(1)}, bf16[2,528,256]{2,1,0:T(8,128)(2,1)S(1)}, u32[]{:S(2)}, u32[]{:S(2)}) %collective-permute-start.6) | collective-permute-done | bytes 540704 | tf_op jit(solution)/shard_map/ppermute | solution.py:268
  87.7 1.0 copy-done.7
  88.7 1.0 copy-done.9
  89.8 0.9 assemble.3.kv_ref
  90.7 1.3 fusion.1
  92.0 1.3 collective-permute-start.10
  93.3 5.5 %collective-permute-start.9 = (bf16[3,528,256]{2,1,0:T(8,128)(2,1)}, bf16[3,528,256]{2,1,0:T(8,128)(2,1)}, u32[]{:S(2)}, u32[]{:S(2)}) collective-permute-start(bf16[3,528,256]{2,1,0:T(8,128)(2,1)} %get-tuple-element.60), channel_id=1, source_target_pairs={{0,8},{8,16},{16,24},{1,9},{9,17},{17,25},{2,10},{10,18},{18,26},{... | collective-permute-start | bytes 2433032 | tf_op jit(solution)/shard_map/ppermute | solution.py:299
  98.7 2.7 collective-permute-start.1
  103.7 7.2 %collective-permute-done.1.refs_1_ = bf16[2,256,256]{2,1,0:T(8,128)(2,1)S(1)} collective-permute-done((bf16[2,256,256]{2,1,0:T(8,128)(2,1)}, bf16[2,256,256]{2,1,0:T(8,128)(2,1)S(1)}, u32[]{:S(2)}, u32[]{:S(2)}) %collective-permute-start.1) | collective-permute-done | bytes 262176 | tf_op jit(solution)/shard_map/ppermute | solution.py:268
  110.9 9.6 %collective-permute-done.2.refs_2_ = bf16[2,256,256]{2,1,0:T(8,128)(2,1)S(1)} collective-permute-done((bf16[2,256,256]{2,1,0:T(8,128)(2,1)}, bf16[2,256,256]{2,1,0:T(8,128)(2,1)S(1)}, u32[]{:S(2)}, u32[]{:S(2)}) %collective-permute-start.2) | collective-permute-done | bytes 262176 | tf_op jit(solution)/shard_map/ppermute | solution.py:268
  120.5 4.6 %collective-permute-done.3.refs_3_ = bf16[2,256,256]{2,1,0:T(8,128)(2,1)S(1)} collective-permute-done((bf16[2,256,256]{2,1,0:T(8,128)(2,1)S(1)}, bf16[2,256,256]{2,1,0:T(8,128)(2,1)S(1)}, u32[]{:S(2)}, u32[]{:S(2)}) %collective-permute-start.3) | collective-permute-done | bytes 262176 | tf_op jit(solution)/shard_map/ppermute | solution.py:268
  125.0 6.8 %collective-permute-done.10.right_ref = bf16[3,528,256]{2,1,0:T(8,128)(2,1)} collective-permute-done((bf16[3,528,256]{2,1,0:T(8,128)(2,1)}, bf16[3,528,256]{2,1,0:T(8,128)(2,1)}, u32[]{:S(2)}, u32[]{:S(2)}) %collective-permute-start.10) | collective-permute-done | bytes 811040 | tf_op jit(solution)/shard_map/ppermute | solution.py:300
  131.8 1.6 all-gather.7.cloned.1.call-done.matrix_ref
  133.6 2.0 assemble.2.query_ref
  135.6 13.7 %attention.1.near_ref = bf16[4,2,256,256]{3,2,1,0:T(8,128)(2,1)S(1)} custom-call(s32[2]{0:T(128)S(1)} %pad_add_fusion.here_ref, bf16[8,256,256]{2,1,0:T(8,128)(2,1)S(1)} %assemble.2.query_ref, bf16[3,528,256]{2,1,0:T(8,128)(2,1)} %collective-permute-done.9.left_ref, bf16[8,528,256]{2,1,0:T(8,128)(2,1)S(1)} %assemble.3.kv_ref, ...), custom_call_target="tpu_custom_call" | custom-call | flops 2400000000 | bytes 9437184 | tf_op jit(solution)/shard_map/attention/pallas_call | solution.py:186
  149.7 2.8 collective-permute-start.12
  153.0 19.6 %collective-permute-done.11.refs_0_ = bf16[2,256,256]{2,1,0:T(8,128)(2,1)S(1)} collective-permute-done((bf16[2,256,256]{2,1,0:T(8,128)(2,1)S(1)}, bf16[2,256,256]{2,1,0:T(8,128)(2,1)S(1)}, u32[]{:S(2)}, u32[]{:S(2)}) %collective-permute-start.11) | collective-permute-done | bytes 262176 | tf_op jit(solution)/shard_map/ppermute | solution.py:268
  172.6 5.8 %collective-permute-done.12.refs_1_ = bf16[2,256,256]{2,1,0:T(8,128)(2,1)S(1)} collective-permute-done((bf16[2,256,256]{2,1,0:T(8,128)(2,1)S(1)}, bf16[2,256,256]{2,1,0:T(8,128)(2,1)S(1)}, u32[]{:S(2)}, u32[]{:S(2)}) %collective-permute-start.12) | collective-permute-done | bytes 262176 | tf_op jit(solution)/shard_map/ppermute | solution.py:268
  178.4 11.8 %collective-permute-done.13.refs_2_ = bf16[2,256,256]{2,1,0:T(8,128)(2,1)S(1)} collective-permute-done((bf16[2,256,256]{2,1,0:T(8,128)(2,1)S(1)}, bf16[2,256,256]{2,1,0:T(8,128)(2,1)S(1)}, u32[]{:S(2)}, u32[]{:S(2)}) %collective-permute-start.13) | collective-permute-done | bytes 262176 | tf_op jit(solution)/shard_map/ppermute | solution.py:268
  190.2 2.0 divide.1
  193.0 1.9 collective-permute-done.14.got_ref
  196.5 4.8 %project.4 = bf16[256,1024]{1,0:T(8,128)(2,1)} custom-call(s32[9]{0:T(128)} %add_add_fusion.place_ref, bf16[4,256,256]{2,1,0:T(8,128)(2,1)} %copy-done, bf16[4,256,256]{2,1,0:T(8,128)(2,1)} %copy-done.13, bf16[256,4096]{1,0:T(8,128)(2,1)} %bitcast.32, bf16[2048,1024]{1,0:T(8,128)(2,1)} %all-gather.7.cloned.1.call-done.matrix_ref), custom_call_target="tpu_custom_call" | custom-call | flops 2 | bytes 2 | tf_op jit(solution)/shard_map/project/pallas_call | solution.py:238
  201.3 4.0 %collective-permute-start.15 = (bf16[256,1024]{1,0:T(8,128)(2,1)}, bf16[256,1024]{1,0:T(8,128)(2,1)S(1)}, u32[]{:S(2)}, u32[]{:S(2)}) collective-permute-start(bf16[256,1024]{1,0:T(8,128)(2,1)} %project.4), channel_id=1, source_target_pairs={{0,32},{32,64},{64,96},{96,128},{128,160},{160,192},{192,224},{224... | collective-permute-start | bytes 1572872 | tf_op jit(solution)/shard_map/ppermute | solution.py:260
  205.3 5.3 %project.5 = bf16[256,1024]{1,0:T(8,128)(2,1)} custom-call(s32[9]{0:T(128)} %get-tuple-element.71.place_ref, bf16[4,256,256]{2,1,0:T(8,128)(2,1)} %copy-done, bf16[4,256,256]{2,1,0:T(8,128)(2,1)} %copy-done.13, bf16[256,4096]{1,0:T(8,128)(2,1)} %bitcast.33, bf16[2048,1024]{1,0:T(8,128)(2,1)} %collective-permute-done.16.matrix_ref), custom_call_target="tpu_custom_call" | custom-call | flops 2 | bytes 2 | tf_op jit(solution)/shard_map/project/pallas_call | solution.py:238
  210.6 3.2 %collective-permute-start.17 = (bf16[256,1024]{1,0:T(8,128)(2,1)}, bf16[256,1024]{1,0:T(8,128)(2,1)S(1)}, u32[]{:S(2)}, u32[]{:S(2)}) collective-permute-start(bf16[256,1024]{1,0:T(8,128)(2,1)} %project.5), channel_id=1, source_target_pairs={{0,32},{32,64},{64,96},{96,128},{128,160},{160,192},{192,224},{224... | collective-permute-start | bytes 1572872 | tf_op jit(solution)/shard_map/ppermute | solution.py:260
  213.8 31.7 %all-gather.11.cloned.1.call-done.matrix_ref = bf16[2048,1024]{1,0:T(8,128)(2,1)} async-done(((bf16[512,1024]{1,0:T(8,128)(2,1)}), bf16[2048,1024]{1,0:T(8,128)(2,1)}) %all-gather.11.cloned.1.call-update) | async-done | bytes 4194320 | tf_op jit(solution)/shard_map/all_gather | solution.py:290
  245.5 5.3 %collective-permute-done.17 = bf16[256,1024]{1,0:T(8,128)(2,1)S(1)} collective-permute-done((bf16[256,1024]{1,0:T(8,128)(2,1)}, bf16[256,1024]{1,0:T(8,128)(2,1)S(1)}, u32[]{:S(2)}, u32[]{:S(2)}) %collective-permute-start.17) | collective-permute-done | bytes 524320 | tf_op jit(solution)/shard_map/ppermute | solution.py:260
  250.8 4.8 %project.6 = bf16[256,1024]{1,0:T(8,128)(2,1)} custom-call(s32[9]{0:T(128)} %get-tuple-element.72.place_ref, bf16[4,256,256]{2,1,0:T(8,128)(2,1)} %copy-done, bf16[4,256,256]{2,1,0:T(8,128)(2,1)} %copy-done.13, bf16[256,4096]{1,0:T(8,128)(2,1)} %bitcast.34, bf16[2048,1024]{1,0:T(8,128)(2,1)} %all-gather.11.cloned.1.call-done.matrix_ref), custom_call_target="tpu_custom_call" | custom-call | flops 2 | bytes 2 | tf_op jit(solution)/shard_map/project/pallas_call | solution.py:238
  255.6 3.5 %collective-permute-start.18 = (bf16[256,1024]{1,0:T(8,128)(2,1)}, bf16[256,1024]{1,0:T(8,128)(2,1)S(1)}, u32[]{:S(2)}, u32[]{:S(2)}) collective-permute-start(bf16[256,1024]{1,0:T(8,128)(2,1)} %project.6), channel_id=1, source_target_pairs={{0,32},{32,64},{64,96},{96,128},{128,160},{160,192},{192,224},{224... | collective-permute-start | bytes 1572872 | tf_op jit(solution)/shard_map/ppermute | solution.py:260
  259.2 4.8 %project.7 = bf16[256,1024]{1,0:T(8,128)(2,1)} custom-call(s32[9]{0:T(128)} %get-tuple-element.70.place_ref, bf16[4,256,256]{2,1,0:T(8,128)(2,1)} %copy-done, bf16[4,256,256]{2,1,0:T(8,128)(2,1)} %copy-done.13, bf16[256,4096]{1,0:T(8,128)(2,1)} %bitcast.35, bf16[2048,1024]{1,0:T(8,128)(2,1)} %collective-permute-done.19.matrix_ref), custom_call_target="tpu_custom_call" | custom-call | flops 2 | bytes 2 | tf_op jit(solution)/shard_map/project/pallas_call | solution.py:238
  264.0 2.6 collective-permute-start.20
  267.0 29.8 %collective-permute-done.18 = bf16[256,1024]{1,0:T(8,128)(2,1)S(1)} collective-permute-done((bf16[256,1024]{1,0:T(8,128)(2,1)}, bf16[256,1024]{1,0:T(8,128)(2,1)S(1)}, u32[]{:S(2)}, u32[]{:S(2)}) %collective-permute-start.18) | collective-permute-done | bytes 524320 | tf_op jit(solution)/shard_map/ppermute | solution.py:260
  296.8 11.1 %collective-permute-done.20 = bf16[256,1024]{1,0:T(8,128)(2,1)S(1)} collective-permute-done((bf16[256,1024]{1,0:T(8,128)(2,1)}, bf16[256,1024]{1,0:T(8,128)(2,1)S(1)}, u32[]{:S(2)}, u32[]{:S(2)}) %collective-permute-start.20) | collective-permute-done | bytes 524320 | tf_op jit(solution)/shard_map/ppermute | solution.py:260
  307.9 0.8 bitcast_dynamic-update-slice_fusion
  (70 shorter events, 12.6 us)
Async XLA Ops:
  6.5 6.7 %copy-start.15 = (bf16[1,64,4096]{2,1,0:T(8,128)(2,1)S(1)}, bf16[1,64,4096]{2,1,0:T(8,128)(2,1)}, u32[]{:S(2)}) copy-start(bf16[1,64,4096]{2,1,0:T(8,128)(2,1)} %param.11) | copy-start | bytes 1572868
  6.5 56.4 %all-gather.5.cloned.1.call-start = ((), (), s32[]{:S(2)}) async-start(), calls=%async_computation | async-start | bytes 1310720 | tf_op jit(solution)/shard_map/all_gather | solution.py:290
  7.6 5.6 %collective-permute-start.7 = (bf16[64,2048]{1,0:T(8,128)(2,1)S(1)}, bf16[64,2048]{1,0:T(8,128)(2,1)S(1)}, u32[]{:S(2)}, u32[]{:S(2)}) collective-permute-start(bf16[64,2048]{1,0:T(8,128)(2,1)S(1)} %dynamic-slice_bitcast_fusion), channel_id=1, source_target_pairs={{0,1},{1,0},{2,3},{3,2},{4,5},{5,4},{6,7},{7,6},{8,9},{9,8},{10,11... | collective-permute-start | bytes 786440 | tf_op jit(solution)/shard_map/ppermute | solution.py:264
  7.8 1.2 copy-start.1
  9.0 1.2 copy-start.2
  10.2 0.7 copy-start.10
  12.7 3.0 collective-permute-start.4
  13.3 8.2 %copy-start.3 = (bf16[1,256,2048]{2,1,0:T(8,128)(2,1)S(1)}, bf16[1,256,2048]{2,1,0:T(8,128)(2,1)}, u32[]{:S(2)}) copy-start(bf16[1,256,2048]{2,1,0:T(8,128)(2,1)} %param.7) | copy-start | bytes 3145732
  14.8 118.5 %all-gather.7.cloned.1.call-start = ((), (), s32[]{:S(2)}) async-start(), calls=%async_computation.1 | async-start | bytes 5242880 | tf_op jit(solution)/shard_map/all_gather | solution.py:290
  16.1 0.8 copy-start.4
  16.9 0.8 copy-start.11
  17.7 45.3 %copy-start.12 = (bf16[2,528,256]{2,1,0:T(8,128)(2,1)S(1)}, bf16[2,528,256]{2,1,0:T(8,128)(2,1)}, u32[]{:S(2)}) copy-start(bf16[2,528,256]{2,1,0:T(8,128)(2,1)} %copy-done.11) | copy-start | bytes 1622020
  17.7 16.5 %collective-permute-start.5 = (bf16[2,528,256]{2,1,0:T(8,128)(2,1)S(1)}, bf16[2,528,256]{2,1,0:T(8,128)(2,1)S(1)}, u32[]{:S(2)}, u32[]{:S(2)}) collective-permute-start(bf16[2,528,256]{2,1,0:T(8,128)(2,1)S(1)} %get-tuple-element.41), channel_id=1, source_target_pairs={{0,2},{2,0},{4,6},{6,4},{1,3},{3,1},{5,7},{7,5},{8,10},{10,8},{12,... | collective-permute-start | bytes 1622024 | tf_op jit(solution)/shard_map/ppermute | solution.py:268
  19.6 31.1 %collective-permute-start.8 = (bf16[2,528,256]{2,1,0:T(8,128)(2,1)S(1)}, bf16[2,528,256]{2,1,0:T(8,128)(2,1)S(1)}, u32[]{:S(2)}, u32[]{:S(2)}) collective-permute-start(bf16[2,528,256]{2,1,0:T(8,128)(2,1)S(1)} %get-tuple-element.43), channel_id=1, source_target_pairs={{0,6},{2,4},{4,2},{6,0},{1,7},{3,5},{5,3},{7,1},{8,14},{10,12},{12... | collective-permute-start | bytes 1622024 | tf_op jit(solution)/shard_map/ppermute | solution.py:268
  22.3 65.4 %copy-start.5 = (bf16[2,528,256]{2,1,0:T(8,128)(2,1)S(1)}, bf16[2,528,256]{2,1,0:T(8,128)(2,1)}, u32[]{:S(2)}) copy-start(bf16[2,528,256]{2,1,0:T(8,128)(2,1)} %copy-done.4) | copy-start | bytes 1622020
  22.3 2.0 collective-permute-start
  34.2 0.8 copy-start.6
  50.7 0.8 copy-start.8
  62.9 132.0 %all-gather.9.cloned.1.call-start = ((), (), s32[]{:S(2)}) async-start(), calls=%async_computation.2 | async-start | bytes 1310720 | tf_op jit(solution)/shard_map/all_gather | solution.py:290
  63.0 24.7 %collective-permute-start.6 = (bf16[2,528,256]{2,1,0:T(8,128)(2,1)S(1)}, bf16[2,528,256]{2,1,0:T(8,128)(2,1)S(1)}, u32[]{:S(2)}, u32[]{:S(2)}) collective-permute-start(bf16[2,528,256]{2,1,0:T(8,128)(2,1)S(1)} %copy-done.12), channel_id=1, source_target_pairs={{0,4},{2,6},{4,0},{6,2},{1,5},{3,7},{5,1},{7,3},{8,12},{10,14},{12... | collective-permute-start | bytes 1622024 | tf_op jit(solution)/shard_map/ppermute | solution.py:268
  87.7 1.0 copy-start.7
  88.7 1.0 copy-start.9
  90.7 12.3 %copy-start.16 = (bf16[64,1024]{1,0:T(8,128)(2,1)S(1)}, bf16[64,1024]{1,0:T(8,128)(2,1)}, u32[]{:S(2)}) copy-start(bf16[64,1024]{1,0:T(8,128)(2,1)} %get-tuple-element.66) | copy-start | bytes 393220
  90.7 12.2 %copy-start.17 = (bf16[64,1024]{1,0:T(8,128)(2,1)S(1)}, bf16[64,1024]{1,0:T(8,128)(2,1)}, u32[]{:S(2)}) copy-start(bf16[64,1024]{1,0:T(8,128)(2,1)} %get-tuple-element.76) | copy-start | bytes 393220
  92.0 39.8 %collective-permute-start.10 = (bf16[3,528,256]{2,1,0:T(8,128)(2,1)}, bf16[3,528,256]{2,1,0:T(8,128)(2,1)}, u32[]{:S(2)}, u32[]{:S(2)}) collective-permute-start(bf16[3,528,256]{2,1,0:T(8,128)(2,1)} %get-tuple-element.59), channel_id=1, source_target_pairs={{8,0},{16,8},{24,16},{9,1},{17,9},{25,17},{10,2},{18,10},{26,18},{... | collective-permute-start | bytes 2433032 | tf_op jit(solution)/shard_map/ppermute | solution.py:300
  93.3 38.5 %collective-permute-start.9 = (bf16[3,528,256]{2,1,0:T(8,128)(2,1)}, bf16[3,528,256]{2,1,0:T(8,128)(2,1)}, u32[]{:S(2)}, u32[]{:S(2)}) collective-permute-start(bf16[3,528,256]{2,1,0:T(8,128)(2,1)} %get-tuple-element.60), channel_id=1, source_target_pairs={{0,8},{8,16},{16,24},{1,9},{9,17},{17,25},{2,10},{10,18},{18,26},{... | collective-permute-start | bytes 2433032 | tf_op jit(solution)/shard_map/ppermute | solution.py:299
  98.7 12.1 %collective-permute-start.1 = (bf16[2,256,256]{2,1,0:T(8,128)(2,1)}, bf16[2,256,256]{2,1,0:T(8,128)(2,1)S(1)}, u32[]{:S(2)}, u32[]{:S(2)}) collective-permute-start(bf16[2,256,256]{2,1,0:T(8,128)(2,1)} %get-tuple-element.35), channel_id=1, source_target_pairs={{0,2},{2,0},{4,6},{6,4},{1,3},{3,1},{5,7},{7,5},{8,10},{10,8},{12,... | collective-permute-start | bytes 786440 | tf_op jit(solution)/shard_map/ppermute | solution.py:268
  101.4 19.0 %collective-permute-start.2 = (bf16[2,256,256]{2,1,0:T(8,128)(2,1)}, bf16[2,256,256]{2,1,0:T(8,128)(2,1)S(1)}, u32[]{:S(2)}, u32[]{:S(2)}) collective-permute-start(bf16[2,256,256]{2,1,0:T(8,128)(2,1)} %get-tuple-element.36), channel_id=1, source_target_pairs={{0,4},{2,6},{4,0},{6,2},{1,5},{3,7},{5,1},{7,3},{8,12},{10,14},{12... | collective-permute-start | bytes 786440 | tf_op jit(solution)/shard_map/ppermute | solution.py:268
  102.1 22.9 %collective-permute-start.3 = (bf16[2,256,256]{2,1,0:T(8,128)(2,1)S(1)}, bf16[2,256,256]{2,1,0:T(8,128)(2,1)S(1)}, u32[]{:S(2)}, u32[]{:S(2)}) collective-permute-start(bf16[2,256,256]{2,1,0:T(8,128)(2,1)S(1)} %get-tuple-element.37), channel_id=1, source_target_pairs={{0,6},{2,4},{4,2},{6,0},{1,7},{3,5},{5,3},{7,1},{8,14},{10,12},{12... | collective-permute-start | bytes 786440 | tf_op jit(solution)/shard_map/ppermute | solution.py:268
  133.4 112.0 %all-gather.11.cloned.1.call-start = ((), (), s32[]{:S(2)}) async-start(), calls=%async_computation.3 | async-start | bytes 5242880 | tf_op jit(solution)/shard_map/all_gather | solution.py:290
  149.4 23.2 %collective-permute-start.11 = (bf16[2,256,256]{2,1,0:T(8,128)(2,1)S(1)}, bf16[2,256,256]{2,1,0:T(8,128)(2,1)S(1)}, u32[]{:S(2)}, u32[]{:S(2)}) collective-permute-start(bf16[2,256,256]{2,1,0:T(8,128)(2,1)S(1)} %get-tuple-element.63), channel_id=1, source_target_pairs={{0,2},{2,0},{4,6},{6,4},{1,3},{3,1},{5,7},{7,5},{8,10},{10,8},{12,... | collective-permute-start | bytes 786440 | tf_op jit(solution)/shard_map/ppermute | solution.py:268
  149.7 28.6 %collective-permute-start.12 = (bf16[2,256,256]{2,1,0:T(8,128)(2,1)S(1)}, bf16[2,256,256]{2,1,0:T(8,128)(2,1)S(1)}, u32[]{:S(2)}, u32[]{:S(2)}) collective-permute-start(bf16[2,256,256]{2,1,0:T(8,128)(2,1)S(1)} %get-tuple-element.62), channel_id=1, source_target_pairs={{0,4},{2,6},{4,0},{6,2},{1,5},{3,7},{5,1},{7,3},{8,12},{10,14},{12... | collective-permute-start | bytes 786440 | tf_op jit(solution)/shard_map/ppermute | solution.py:268
  152.5 37.7 %collective-permute-start.13 = (bf16[2,256,256]{2,1,0:T(8,128)(2,1)S(1)}, bf16[2,256,256]{2,1,0:T(8,128)(2,1)S(1)}, u32[]{:S(2)}, u32[]{:S(2)}) collective-permute-start(bf16[2,256,256]{2,1,0:T(8,128)(2,1)S(1)} %get-tuple-element.61), channel_id=1, source_target_pairs={{0,6},{2,4},{4,2},{6,0},{1,7},{3,5},{5,3},{7,1},{8,14},{10,12},{12... | collective-permute-start | bytes 786440 | tf_op jit(solution)/shard_map/ppermute | solution.py:268
  192.2 0.8 copy-start
  193.0 1.9 collective-permute-start.14
  194.9 1.6 copy-start.13
  194.9 10.4 %collective-permute-start.16 = (bf16[2048,1024]{1,0:T(8,128)(2,1)}, bf16[2048,1024]{1,0:T(8,128)(2,1)}, u32[]{:S(2)}, u32[]{:S(2)}) collective-permute-start(bf16[2048,1024]{1,0:T(8,128)(2,1)} %all-gather.7.cloned.1.call-done.matrix_ref), channel_id=1, source_target_pairs={{0,1},{1,0},{2,3},{3,2},{4,5},{5,4},{6,7},{7,6},{8,9},{9,8},{10,11... | collective-permute-start | bytes 12582920 | tf_op jit(solution)/shard_map/ppermute | solution.py:264
  201.3 44.1 %collective-permute-start.15 = (bf16[256,1024]{1,0:T(8,128)(2,1)}, bf16[256,1024]{1,0:T(8,128)(2,1)S(1)}, u32[]{:S(2)}, u32[]{:S(2)}) collective-permute-start(bf16[256,1024]{1,0:T(8,128)(2,1)} %project.4), channel_id=1, source_target_pairs={{0,32},{32,64},{64,96},{96,128},{128,160},{160,192},{192,224},{224... | collective-permute-start | bytes 1572872 | tf_op jit(solution)/shard_map/ppermute | solution.py:260
  210.6 40.2 %collective-permute-start.17 = (bf16[256,1024]{1,0:T(8,128)(2,1)}, bf16[256,1024]{1,0:T(8,128)(2,1)S(1)}, u32[]{:S(2)}, u32[]{:S(2)}) collective-permute-start(bf16[256,1024]{1,0:T(8,128)(2,1)} %project.5), channel_id=1, source_target_pairs={{0,32},{32,64},{64,96},{96,128},{128,160},{160,192},{192,224},{224... | collective-permute-start | bytes 1572872 | tf_op jit(solution)/shard_map/ppermute | solution.py:260
  250.8 8.4 %collective-permute-start.19 = (bf16[2048,1024]{1,0:T(8,128)(2,1)}, bf16[2048,1024]{1,0:T(8,128)(2,1)}, u32[]{:S(2)}, u32[]{:S(2)}) collective-permute-start(bf16[2048,1024]{1,0:T(8,128)(2,1)} %all-gather.11.cloned.1.call-done.matrix_ref), channel_id=1, source_target_pairs={{0,1},{1,0},{2,3},{3,2},{4,5},{5,4},{6,7},{7,6},{8,9},{9,8},{10,11... | collective-permute-start | bytes 12582920 | tf_op jit(solution)/shard_map/ppermute | solution.py:264
  255.6 41.1 %collective-permute-start.18 = (bf16[256,1024]{1,0:T(8,128)(2,1)}, bf16[256,1024]{1,0:T(8,128)(2,1)S(1)}, u32[]{:S(2)}, u32[]{:S(2)}) collective-permute-start(bf16[256,1024]{1,0:T(8,128)(2,1)} %project.6), channel_id=1, source_target_pairs={{0,32},{32,64},{64,96},{96,128},{128,160},{160,192},{192,224},{224... | collective-permute-start | bytes 1572872 | tf_op jit(solution)/shard_map/ppermute | solution.py:260
  264.0 43.9 %collective-permute-start.20 = (bf16[256,1024]{1,0:T(8,128)(2,1)}, bf16[256,1024]{1,0:T(8,128)(2,1)S(1)}, u32[]{:S(2)}, u32[]{:S(2)}) collective-permute-start(bf16[256,1024]{1,0:T(8,128)(2,1)} %project.7), channel_id=1, source_target_pairs={{0,32},{32,64},{64,96},{96,128},{128,160},{160,192},{192,224},{224... | collective-permute-start | bytes 1572872 | tf_op jit(solution)/shard_map/ppermute | solution.py:260
  296.8 11.2 %copy-start.14 = (bf16[1,256,4096]{2,1,0:T(8,128)(2,1)}, bf16[1,256,4096]{2,1,0:T(8,128)(2,1)S(1)}, u32[]{:S(2)}) copy-start(bf16[1,256,4096]{2,1,0:T(8,128)(2,1)S(1)} %bitcast_dynamic-update-slice_fusion.1) | copy-start | bytes 6291460
Sparse Core Ops, SparseCore 0:
  15.0 47.8 all-gather.4
  64.7 68.6 all-gather.6
  135.2 51.9 all-gather.8
  195.1 50.3 all-gather.10

commit v3 on v2

--- a/solution.py
+++ b/solution.py
@@ -132,7 +132,7 @@
     )(here, near, *far)
 
 
-def attention_body(here_ref, query_ref, left_ref, kv_ref, right_ref, out_ref, keys, values, labels, sems):
+def attention_body(here_ref, query_ref, left_ref, kv_ref, right_ref, out_ref, keys, values, labels, bounds, sems):
     step = pl.program_id(0)
 
     @pl.when(step == 0)
@@ -145,16 +145,19 @@
                 at += count
         run_copies(pairs, sems)
 
+        marks = jnp.max(labels[...].astype(jnp.float32), axis=1)
+        top, low = jnp.max(marks, axis=1, keepdims=True), jnp.min(marks, axis=1, keepdims=True)
+        place = lax.broadcasted_iota(jnp.int32, (BLOCKS, 1), 0)
+        beyond = (place >= SPAN + LINE) & (top == 0.0)
+        for index, value in enumerate((top, low)):
+            bounds[index] = jnp.broadcast_to(jnp.where(beyond, 99.0, value), (BLOCKS, DH))
+
     own = jnp.max(labels[step + SPAN].astype(jnp.float32), axis=0, keepdims=True)
-    first, last = jnp.min(own), jnp.max(own)
-    marks = jnp.max(labels[...].astype(jnp.float32), axis=1)
-    top, low = jnp.max(marks, axis=1, keepdims=True), jnp.min(marks, axis=1, keepdims=True)
-    place = lax.broadcasted_iota(jnp.int32, (BLOCKS, 1), 0)
-    beyond = (place >= SPAN + LINE) & (top == 0.0)
-    before = jnp.where((top < first) & ~beyond, 1.0, 0.0)
-    until = jnp.where((low <= last) & ~beyond, 1.0, 0.0)
-    start = jnp.maximum(jnp.sum(before).astype(jnp.int32), step)
-    stop = jnp.minimum(jnp.sum(until).astype(jnp.int32), step + REACH)
+    before = bounds[0] < jnp.min(own, axis=1, keepdims=True)
+    until = bounds[1] <= jnp.max(own, axis=1, keepdims=True)
+    counts = jnp.sum(jnp.where(before, 16.0, 0.0) + jnp.where(until, 1.0, 0.0), axis=0, keepdims=True)
+    both = jnp.max(counts).astype(jnp.int32)
+    start, stop = jnp.maximum(both // 16, step), jnp.minimum(both % 16, step + REACH)
     needed = stop - start
     own_column = jnp.broadcast_to(own, (BLK, BLK)).T[:, 0:1]
     scale = LOG2E / DH**0.5
@@ -194,6 +197,7 @@
                 pltpu.VMEM((BLOCKS, BLK, PAIR), jnp.bfloat16),
                 pltpu.VMEM((BLOCKS, BLK, PAIR), jnp.bfloat16),
                 pltpu.VMEM((BLOCKS, MARK, PAIR), jnp.bfloat16),
+                pltpu.VMEM((2, BLOCKS, DH), jnp.float32),
                 pltpu.SemaphoreType.DMA((9,)),
             ],
         ),
@@ -289,34 +293,32 @@
     def gather(piece, axis):
         return lax.all_gather(piece, axis, axis=0, tiled=True)
 
-    first = gather(rows[0], "zl")
+    first, second = gather(rows[0], "zl"), gather(rows[1], "zl")
     kv_far = across(kv_out)
-    first = after(first, kv_far[1], kv_far[3], *heads_out)
-    kv_far[2] = after(kv_far[2], first)
-    first = gather(first, "y")
+    kv_far[2] = after(kv_far[2], *heads_out)
     heads_far = across(heads_out)
     kv = assemble(here, kv_far)
+    first = gather(after(first, kv), "y")
     left = lax.ppermute(kv[LINE - SPAN :], "y", [(i, i + 1) for i in range(3)])
     right = lax.ppermute(kv[:SPAN], "y", [(i + 1, i) for i in range(3)])
     heads = assemble(here, heads_far)
-    second = gather(after(rows[1], left, right, *heads_far, first), "zl")
+    second = gather(after(second, left, right, *heads_far), "y")
 
     attended = attention(here, heads, (left, kv, right))
     far = across([attended[k] for k in range(CHIPS)])
     first = after(first, *far)
     own, send = divide(here, attended, far[1:])
     attended = [own, to_other_core(send)]
-    second = gather(after(second, *attended), "y")
 
     out = jnp.zeros(hidden.shape, hidden.dtype)
     chips = chip ^ jnp.arange(CHIPS, dtype=jnp.int32)
     order = jnp.concatenate([2 * chips + core, 2 * chips + 1 - core])
     made, arrived = [], []
-    for p, matrix in enumerate((first, after(second, *attended))):
-        matrix = after(matrix, *made, *arrived)
+    for p, matrix in enumerate((first, second)):
+        matrix = after(matrix, *attended, *made[-1:], *arrived[-2:-1])
         for which, matrix in ((core, matrix), (1 - core, to_other_core(matrix))):
             place = jnp.concatenate([(which * PARTS + p)[None], order]).astype(jnp.int32)
-            ready = [after(rows, *made[-1:], *arrived[: 2 * p]) for rows in attended]
+            ready = [after(rows, *made[-1:], *arrived[-2:-1]) for rows in attended]
             made.append(project(place, ready, hidden, matrix))
             arrived.append(to_next_section(made[-1]))
             out = lax.dynamic_update_slice(out, arrived[-1], (0, which * half + p * part))

time: 316 us -> 300 us (0.949)
  local copies, waits for them, and re-layouts: 13.6 us -> 4.55 us
  starting transfers between devices: 34.3 us -> 27.4 us
    all_gather x4, waiting for transfers between devices: 44.7 us -> 0.03 us  [gather(): return lax.all_gather(piece, axis, axis=0, tiled=True)]
    ppermute x4, waiting for transfers between devices: 46.2 us -> 84.6 us  [to_next_section(): lax.ppermute(value, ('x', 'zh'), [(s, (s + 1) % 8) for s in range(8)])]
    unnamed x36 -> x14, local copies, waits for them, and re-layouts: 9.28 us -> 0.86 us
    ppermute x9, waiting for transfers between devices: 106 us -> 114 us  [across(): lax.ppermute(piece, 'zl', [(z, z ^ k) for z in range(CHIPS)])]
    ppermute x1, waiting for transfers between devices: 6.8 us -> 0.01 us  [on_device(): right = lax.ppermute(kv[:SPAN], 'y', [(i + 1, i) for i in range(3)])]
    ppermute x4, starting transfers between devices: 13.3 us -> 8.42 us  [to_next_section(): lax.ppermute(value, ('x', 'zh'), [(s, (s + 1) % 8) for s in range(8)])]
  transfers between devices with their start and end apart: 25 -> 25, of which waited for: 19 -> 17; matrix products, arithmetic and copies ran while one was open for 2% -> 1% of each run, Pallas kernels for 13% -> 15%
where the time goes in v3:
time: 300 us; the launch traced here: 299 us
  waiting for transfers between devices  206 us (69%)
  Pallas kernels  44.2 us (15%)
  starting transfers between devices  27.4 us (9%)
  between operations  13.4 us (4%)
  local copies, waits for them, and re-layouts  4.55 us (2%)
  other arithmetic  3.84 us (1%)
    ppermute x9, waiting for transfers between devices, across(): lax.ppermute(piece, 'zl', [(z, z ^ k) for z in range(CHIPS)])  114 us
    ppermute x4, waiting for transfers between devices, to_next_section(): lax.ppermute(value, ('x', 'zh'), [(s, (s + 1) % 8) for s in range(8)])  84.6 us
    pallas_call x4, Pallas kernels, project(): pl.pallas_call(project_body, in_specs=[SCALARS, WHOLE, WHOLE, ANY, ANY],...  19.4 us
    pallas_call x1, Pallas kernels, attention(): pl.pallas_call(attention_body, grid_spec=pltpu.PrefetchScalarGridSpec(num...  15.8 us
    ppermute x9, starting transfers between devices, across(): lax.ppermute(piece, 'zl', [(z, z ^ k) for z in range(CHIPS)])  12.4 us
    ppermute x4, starting transfers between devices, to_next_section(): lax.ppermute(value, ('x', 'zh'), [(s, (s + 1) % 8) for s in range(8)])  8.42 us
    ppermute x6, waiting for transfers between devices, to_other_core(): return lax.ppermute(value, 'c', [(0, 1), (1, 0)])  7.3 us
  transfers between devices with their start and end apart: 25, of which 17 were waited for; matrix products, arithmetic and copies ran while one was open for 1% of the time, Pallas kernels for 15%

profile of v3, /device:TPU:32, one launch (start us, length us, event | category | flops | bytes accessed | tf_op | source)
XLA Modules:
  0.0 298.9 jit_solution(17404321829054211472)
XLA Ops:
  6.5 1.1 dynamic-slice_bitcast_fusion
  7.8 1.5 collective-permute-done.14
  9.3 1.0 bitcast_select_fusion.1
  10.4 0.7 pad_maximum_fusion
  11.3 1.8 pack.3
  13.2 0.7 pad_maximum_fusion.1
  14.0 2.0 collective-permute-done.4.got_ref
  16.0 0.3 combine.3
  16.3 3.4 %collective-permute-start.6 = (bf16[2,528,256]{2,1,0:T(8,128)(2,1)S(1)}, bf16[2,528,256]{2,1,0:T(8,128)(2,1)S(1)}, u32[]{:S(2)}, u32[]{:S(2)}) collective-permute-start(bf16[2,528,256]{2,1,0:T(8,128)(2,1)S(1)} %get-tuple-element.41), channel_id=1, source_target_pairs={{0,4},{2,6},{4,0},{6,2},{1,5},{3,7},{5,1},{7,3},{8,12},{10,14},{12... | collective-permute-start | bytes 1622024 | tf_op jit(solution)/shard_map/ppermute | solution.py:272
  19.8 0.6 collective-permute-start.7
  20.4 0.7 pack.2
  21.2 1.9 collective-permute-done.got_ref
  23.1 1.2 combine.2
  24.3 35.5 %collective-permute-done.6.refs_2_ = bf16[2,528,256]{2,1,0:T(8,128)(2,1)S(1)} collective-permute-done((bf16[2,528,256]{2,1,0:T(8,128)(2,1)S(1)}, bf16[2,528,256]{2,1,0:T(8,128)(2,1)S(1)}, u32[]{:S(2)}, u32[]{:S(2)}) %collective-permute-start.6) | collective-permute-done | bytes 540704 | tf_op jit(solution)/shard_map/ppermute | solution.py:272
  59.7 1.6 collective-permute-done.5.refs_1_
  61.3 33.8 %collective-permute-done.7.refs_3_ = bf16[2,528,256]{2,1,0:T(8,128)(2,1)S(1)} collective-permute-done((bf16[2,528,256]{2,1,0:T(8,128)(2,1)S(1)}, bf16[2,528,256]{2,1,0:T(8,128)(2,1)S(1)}, u32[]{:S(2)}, u32[]{:S(2)}) %collective-permute-start.7) | collective-permute-done | bytes 540704 | tf_op jit(solution)/shard_map/ppermute | solution.py:272
  95.1 0.9 assemble.3.kv_ref
  96.1 1.3 fusion.1
  97.4 4.6 %collective-permute-start.8 = (bf16[3,528,256]{2,1,0:T(8,128)(2,1)}, bf16[3,528,256]{2,1,0:T(8,128)(2,1)}, u32[]{:S(2)}, u32[]{:S(2)}) collective-permute-start(bf16[3,528,256]{2,1,0:T(8,128)(2,1)} %get-tuple-element.58), channel_id=1, source_target_pairs={{0,8},{8,16},{16,24},{1,9},{9,17},{17,25},{2,10},{10,18},{18,26},{... | collective-permute-start | bytes 2433032 | tf_op jit(solution)/shard_map/ppermute | solution.py:302
  102.0 1.3 collective-permute-start.9
  103.4 4.3 %collective-permute-start.2 = (bf16[2,256,256]{2,1,0:T(8,128)(2,1)}, bf16[2,256,256]{2,1,0:T(8,128)(2,1)S(1)}, u32[]{:S(2)}, u32[]{:S(2)}) collective-permute-start(bf16[2,256,256]{2,1,0:T(8,128)(2,1)} %get-tuple-element.35), channel_id=1, source_target_pairs={{0,4},{2,6},{4,0},{6,2},{1,5},{3,7},{5,1},{7,3},{8,12},{10,14},{12... | collective-permute-start | bytes 786440 | tf_op jit(solution)/shard_map/ppermute | solution.py:272
  107.7 6.9 %collective-permute-done.1.refs_1_ = bf16[2,256,256]{2,1,0:T(8,128)(2,1)S(1)} collective-permute-done((bf16[2,256,256]{2,1,0:T(8,128)(2,1)}, bf16[2,256,256]{2,1,0:T(8,128)(2,1)S(1)}, u32[]{:S(2)}, u32[]{:S(2)}) %collective-permute-start.1) | collective-permute-done | bytes 262176 | tf_op jit(solution)/shard_map/ppermute | solution.py:272
  114.6 11.4 %collective-permute-done.2.refs_2_ = bf16[2,256,256]{2,1,0:T(8,128)(2,1)S(1)} collective-permute-done((bf16[2,256,256]{2,1,0:T(8,128)(2,1)}, bf16[2,256,256]{2,1,0:T(8,128)(2,1)S(1)}, u32[]{:S(2)}, u32[]{:S(2)}) %collective-permute-start.2) | collective-permute-done | bytes 262176 | tf_op jit(solution)/shard_map/ppermute | solution.py:272
  126.0 3.6 %collective-permute-done.3.refs_3_ = bf16[2,256,256]{2,1,0:T(8,128)(2,1)S(1)} collective-permute-done((bf16[2,256,256]{2,1,0:T(8,128)(2,1)S(1)}, bf16[2,256,256]{2,1,0:T(8,128)(2,1)S(1)}, u32[]{:S(2)}, u32[]{:S(2)}) %collective-permute-start.3) | collective-permute-done | bytes 262176 | tf_op jit(solution)/shard_map/ppermute | solution.py:272
  129.6 2.0 assemble.2.query_ref
  131.6 15.8 %attention.1.near_ref = bf16[4,2,256,256]{3,2,1,0:T(8,128)(2,1)S(1)} custom-call(s32[2]{0:T(128)S(1)} %pad_add_fusion.here_ref, bf16[8,256,256]{2,1,0:T(8,128)(2,1)S(1)} %assemble.2.query_ref, bf16[3,528,256]{2,1,0:T(8,128)(2,1)} %collective-permute-done.8.left_ref, bf16[8,528,256]{2,1,0:T(8,128)(2,1)S(1)} %assemble.3.kv_ref, ...), custom_call_target="tpu_custom_call" | custom-call | flops 2400000000 | bytes 9437184 | tf_op jit(solution)/shard_map/attention/pallas_call | solution.py:189
  147.6 3.9 %collective-permute-start.11 = (bf16[2,256,256]{2,1,0:T(8,128)(2,1)S(1)}, bf16[2,256,256]{2,1,0:T(8,128)(2,1)S(1)}, u32[]{:S(2)}, u32[]{:S(2)}) collective-permute-start(bf16[2,256,256]{2,1,0:T(8,128)(2,1)S(1)} %get-tuple-element.60), channel_id=1, source_target_pairs={{0,4},{2,6},{4,0},{6,2},{1,5},{3,7},{5,1},{7,3},{8,12},{10,14},{12... | collective-permute-start | bytes 786440 | tf_op jit(solution)/shard_map/ppermute | solution.py:272
  151.6 5.3 %collective-permute-done.10.refs_0_ = bf16[2,256,256]{2,1,0:T(8,128)(2,1)S(1)} collective-permute-done((bf16[2,256,256]{2,1,0:T(8,128)(2,1)S(1)}, bf16[2,256,256]{2,1,0:T(8,128)(2,1)S(1)}, u32[]{:S(2)}, u32[]{:S(2)}) %collective-permute-start.10) | collective-permute-done | bytes 262176 | tf_op jit(solution)/shard_map/ppermute | solution.py:272
  156.9 11.8 %collective-permute-done.11.refs_1_ = bf16[2,256,256]{2,1,0:T(8,128)(2,1)S(1)} collective-permute-done((bf16[2,256,256]{2,1,0:T(8,128)(2,1)S(1)}, bf16[2,256,256]{2,1,0:T(8,128)(2,1)S(1)}, u32[]{:S(2)}, u32[]{:S(2)}) %collective-permute-start.11) | collective-permute-done | bytes 262176 | tf_op jit(solution)/shard_map/ppermute | solution.py:272
  168.6 3.8 %collective-permute-done.12.refs_2_ = bf16[2,256,256]{2,1,0:T(8,128)(2,1)S(1)} collective-permute-done((bf16[2,256,256]{2,1,0:T(8,128)(2,1)S(1)}, bf16[2,256,256]{2,1,0:T(8,128)(2,1)S(1)}, u32[]{:S(2)}, u32[]{:S(2)}) %collective-permute-start.12) | collective-permute-done | bytes 262176 | tf_op jit(solution)/shard_map/ppermute | solution.py:272
  172.4 2.0 divide.1
  174.4 0.8 copy-done
  175.2 1.9 collective-permute-done.13.got_ref
  177.3 0.6 add_add_fusion.place_ref
  177.9 4.8 %project.4 = bf16[256,1024]{1,0:T(8,128)(2,1)} custom-call(s32[9]{0:T(128)} %add_add_fusion.place_ref, bf16[4,256,256]{2,1,0:T(8,128)(2,1)} %copy-done, bf16[4,256,256]{2,1,0:T(8,128)(2,1)} %copy-done.5, bf16[256,4096]{1,0:T(8,128)(2,1)} %bitcast.32, bf16[2048,1024]{1,0:T(8,128)(2,1)} %all-gather.7.cloned.1.call-done.matrix_ref), custom_call_target="tpu_custom_call" | custom-call | flops 2 | bytes 2 | tf_op jit(solution)/shard_map/project/pallas_call | solution.py:242
  182.8 3.2 %collective-permute-start.15 = (bf16[256,1024]{1,0:T(8,128)(2,1)}, bf16[256,1024]{1,0:T(8,128)(2,1)S(1)}, u32[]{:S(2)}, u32[]{:S(2)}) collective-permute-start(bf16[256,1024]{1,0:T(8,128)(2,1)} %project.4), channel_id=1, source_target_pairs={{0,32},{32,64},{64,96},{96,128},{128,160},{160,192},{192,224},{224... | collective-permute-start | bytes 1572872 | tf_op jit(solution)/shard_map/ppermute | solution.py:264
  186.0 0.7 add_add_fusion.3
  186.6 4.9 %project.5 = bf16[256,1024]{1,0:T(8,128)(2,1)} custom-call(s32[9]{0:T(128)} %get-tuple-element.69.place_ref, bf16[4,256,256]{2,1,0:T(8,128)(2,1)} %copy-done, bf16[4,256,256]{2,1,0:T(8,128)(2,1)} %copy-done.5, bf16[256,4096]{1,0:T(8,128)(2,1)} %bitcast.33, bf16[2048,1024]{1,0:T(8,128)(2,1)} %collective-permute-done.16.matrix_ref), custom_call_target="tpu_custom_call" | custom-call | flops 2 | bytes 2 | tf_op jit(solution)/shard_map/project/pallas_call | solution.py:242
  191.5 22.1 %collective-permute-done.15 = bf16[256,1024]{1,0:T(8,128)(2,1)S(1)} collective-permute-done((bf16[256,1024]{1,0:T(8,128)(2,1)}, bf16[256,1024]{1,0:T(8,128)(2,1)S(1)}, u32[]{:S(2)}, u32[]{:S(2)}) %collective-permute-start.15) | collective-permute-done | bytes 524320 | tf_op jit(solution)/shard_map/ppermute | solution.py:264
  213.6 3.1 %collective-permute-start.17 = (bf16[256,1024]{1,0:T(8,128)(2,1)}, bf16[256,1024]{1,0:T(8,128)(2,1)S(1)}, u32[]{:S(2)}, u32[]{:S(2)}) collective-permute-start(bf16[256,1024]{1,0:T(8,128)(2,1)} %project.5), channel_id=1, source_target_pairs={{0,32},{32,64},{64,96},{96,128},{128,160},{160,192},{192,224},{224... | collective-permute-start | bytes 1572872 | tf_op jit(solution)/shard_map/ppermute | solution.py:264
  216.7 4.8 %project.6 = bf16[256,1024]{1,0:T(8,128)(2,1)} custom-call(s32[9]{0:T(128)} %get-tuple-element.70.place_ref, bf16[4,256,256]{2,1,0:T(8,128)(2,1)} %copy-done, bf16[4,256,256]{2,1,0:T(8,128)(2,1)} %copy-done.5, bf16[256,4096]{1,0:T(8,128)(2,1)} %bitcast.34, bf16[2048,1024]{1,0:T(8,128)(2,1)} %all-gather.11.cloned.1.call-done.matrix_ref), custom_call_target="tpu_custom_call" | custom-call | flops 2 | bytes 2 | tf_op jit(solution)/shard_map/project/pallas_call | solution.py:242
  221.6 2.1 collective-permute-start.18
  223.6 33.4 %collective-permute-done.17 = bf16[256,1024]{1,0:T(8,128)(2,1)S(1)} collective-permute-done((bf16[256,1024]{1,0:T(8,128)(2,1)}, bf16[256,1024]{1,0:T(8,128)(2,1)S(1)}, u32[]{:S(2)}, u32[]{:S(2)}) %collective-permute-start.17) | collective-permute-done | bytes 524320 | tf_op jit(solution)/shard_map/ppermute | solution.py:264
  257.0 4.8 %project.7 = bf16[256,1024]{1,0:T(8,128)(2,1)} custom-call(s32[9]{0:T(128)} %get-tuple-element.68.place_ref, bf16[4,256,256]{2,1,0:T(8,128)(2,1)} %copy-done, bf16[4,256,256]{2,1,0:T(8,128)(2,1)} %copy-done.5, bf16[256,4096]{1,0:T(8,128)(2,1)} %bitcast.35, bf16[2048,1024]{1,0:T(8,128)(2,1)} %collective-permute-done.19.matrix_ref), custom_call_target="tpu_custom_call" | custom-call | flops 2 | bytes 2 | tf_op jit(solution)/shard_map/project/pallas_call | solution.py:242
  262.0 0.2 broadcast_in_dim.24
  262.3 5.8 %collective-permute-done.18 = bf16[256,1024]{1,0:T(8,128)(2,1)S(1)} collective-permute-done((bf16[256,1024]{1,0:T(8,128)(2,1)}, bf16[256,1024]{1,0:T(8,128)(2,1)S(1)}, u32[]{:S(2)}, u32[]{:S(2)}) %collective-permute-start.18) | collective-permute-done | bytes 524320 | tf_op jit(solution)/shard_map/ppermute | solution.py:264
  268.2 23.4 %collective-permute-done.20 = bf16[256,1024]{1,0:T(8,128)(2,1)S(1)} collective-permute-done((bf16[256,1024]{1,0:T(8,128)(2,1)}, bf16[256,1024]{1,0:T(8,128)(2,1)S(1)}, u32[]{:S(2)}, u32[]{:S(2)}) %collective-permute-start.20) | collective-permute-done | bytes 524320 | tf_op jit(solution)/shard_map/ppermute | solution.py:264
  291.5 0.8 bitcast_dynamic-update-slice_fusion
  (48 shorter events, 1.5 us)
Async XLA Ops:
  6.5 4.7 %copy-start.1 = (bf16[1,256,2048]{2,1,0:T(8,128)(2,1)S(1)}, bf16[1,256,2048]{2,1,0:T(8,128)(2,1)}, u32[]{:S(2)}) copy-start(bf16[1,256,2048]{2,1,0:T(8,128)(2,1)} %param.8) | copy-start | bytes 3145732
  6.5 4.7 %copy-start.2 = (bf16[1,256,2048]{2,1,0:T(8,128)(2,1)S(1)}, bf16[1,256,2048]{2,1,0:T(8,128)(2,1)}, u32[]{:S(2)}) copy-start(bf16[1,256,2048]{2,1,0:T(8,128)(2,1)} %param.9) | copy-start | bytes 3145732
  6.5 4.7 %copy-start.4 = (s32[1,256]{1,0:T(1,128)S(1)}, s32[1,256]{1,0:T(1,128)}, u32[]{:S(2)}) copy-start(s32[1,256]{1,0:T(1,128)} %refs_2_.1) | copy-start | bytes 3076
  6.5 89.4 %all-gather.5.cloned.1.call-start = ((), (), s32[]{:S(2)}) async-start(), calls=%async_computation | async-start | bytes 1310720 | tf_op jit(solution)/shard_map/all_gather | solution.py:294
  7.7 1.6 collective-permute-start.14
  11.1 118.5 %all-gather.9.cloned.1.call-start = ((), (), s32[]{:S(2)}) async-start(), calls=%async_computation.2 | async-start | bytes 1310720 | tf_op jit(solution)/shard_map/all_gather | solution.py:294
  13.1 7.3 %copy-start.3 = (bf16[1,256,2048]{2,1,0:T(8,128)(2,1)S(1)}, bf16[1,256,2048]{2,1,0:T(8,128)(2,1)}, u32[]{:S(2)}) copy-start(bf16[1,256,2048]{2,1,0:T(8,128)(2,1)} %param.7) | copy-start | bytes 3145732
  13.1 2.9 collective-permute-start.4
  14.0 161.2 %all-gather.7.cloned.1.call-start = ((), (), s32[]{:S(2)}) async-start(), calls=%async_computation.1 | async-start | bytes 5242880 | tf_op jit(solution)/shard_map/all_gather | solution.py:294
  16.3 43.4 %collective-permute-start.6 = (bf16[2,528,256]{2,1,0:T(8,128)(2,1)S(1)}, bf16[2,528,256]{2,1,0:T(8,128)(2,1)S(1)}, u32[]{:S(2)}, u32[]{:S(2)}) collective-permute-start(bf16[2,528,256]{2,1,0:T(8,128)(2,1)S(1)} %get-tuple-element.41), channel_id=1, source_target_pairs={{0,4},{2,6},{4,0},{6,2},{1,5},{3,7},{5,1},{7,3},{8,12},{10,14},{12... | collective-permute-start | bytes 1622024 | tf_op jit(solution)/shard_map/ppermute | solution.py:272
  19.7 41.6 %collective-permute-start.5 = (bf16[2,528,256]{2,1,0:T(8,128)(2,1)S(1)}, bf16[2,528,256]{2,1,0:T(8,128)(2,1)S(1)}, u32[]{:S(2)}, u32[]{:S(2)}) collective-permute-start(bf16[2,528,256]{2,1,0:T(8,128)(2,1)S(1)} %get-tuple-element.40), channel_id=1, source_target_pairs={{0,2},{2,0},{4,6},{6,4},{1,3},{3,1},{5,7},{7,5},{8,10},{10,8},{12,... | collective-permute-start | bytes 1622024 | tf_op jit(solution)/shard_map/ppermute | solution.py:272
  19.8 75.3 %collective-permute-start.7 = (bf16[2,528,256]{2,1,0:T(8,128)(2,1)S(1)}, bf16[2,528,256]{2,1,0:T(8,128)(2,1)S(1)}, u32[]{:S(2)}, u32[]{:S(2)}) collective-permute-start(bf16[2,528,256]{2,1,0:T(8,128)(2,1)S(1)} %get-tuple-element.43), channel_id=1, source_target_pairs={{0,6},{2,4},{4,2},{6,0},{1,7},{3,5},{5,3},{7,1},{8,14},{10,12},{12... | collective-permute-start | bytes 1622024 | tf_op jit(solution)/shard_map/ppermute | solution.py:272
  21.1 2.0 collective-permute-start
  96.0 117.6 %all-gather.11.cloned.1.call-start = ((), (), s32[]{:S(2)}) async-start(), calls=%async_computation.3 | async-start | bytes 5242880 | tf_op jit(solution)/shard_map/all_gather | solution.py:294
  97.4 32.2 %collective-permute-start.8 = (bf16[3,528,256]{2,1,0:T(8,128)(2,1)}, bf16[3,528,256]{2,1,0:T(8,128)(2,1)}, u32[]{:S(2)}, u32[]{:S(2)}) collective-permute-start(bf16[3,528,256]{2,1,0:T(8,128)(2,1)} %get-tuple-element.58), channel_id=1, source_target_pairs={{0,8},{8,16},{16,24},{1,9},{9,17},{17,25},{2,10},{10,18},{18,26},{... | collective-permute-start | bytes 2433032 | tf_op jit(solution)/shard_map/ppermute | solution.py:302
  102.0 27.6 %collective-permute-start.9 = (bf16[3,528,256]{2,1,0:T(8,128)(2,1)}, bf16[3,528,256]{2,1,0:T(8,128)(2,1)}, u32[]{:S(2)}, u32[]{:S(2)}) collective-permute-start(bf16[3,528,256]{2,1,0:T(8,128)(2,1)} %get-tuple-element.57), channel_id=1, source_target_pairs={{8,0},{16,8},{24,16},{9,1},{17,9},{25,17},{10,2},{18,10},{26,18},{... | collective-permute-start | bytes 2433032 | tf_op jit(solution)/shard_map/ppermute | solution.py:303
  103.3 11.3 %collective-permute-start.1 = (bf16[2,256,256]{2,1,0:T(8,128)(2,1)}, bf16[2,256,256]{2,1,0:T(8,128)(2,1)S(1)}, u32[]{:S(2)}, u32[]{:S(2)}) collective-permute-start(bf16[2,256,256]{2,1,0:T(8,128)(2,1)} %get-tuple-element.34), channel_id=1, source_target_pairs={{0,2},{2,0},{4,6},{6,4},{1,3},{3,1},{5,7},{7,5},{8,10},{10,8},{12,... | collective-permute-start | bytes 786440 | tf_op jit(solution)/shard_map/ppermute | solution.py:272
  103.4 22.6 %collective-permute-start.2 = (bf16[2,256,256]{2,1,0:T(8,128)(2,1)}, bf16[2,256,256]{2,1,0:T(8,128)(2,1)S(1)}, u32[]{:S(2)}, u32[]{:S(2)}) collective-permute-start(bf16[2,256,256]{2,1,0:T(8,128)(2,1)} %get-tuple-element.35), channel_id=1, source_target_pairs={{0,4},{2,6},{4,0},{6,2},{1,5},{3,7},{5,1},{7,3},{8,12},{10,14},{12... | collective-permute-start | bytes 786440 | tf_op jit(solution)/shard_map/ppermute | solution.py:272
  107.7 21.9 %collective-permute-start.3 = (bf16[2,256,256]{2,1,0:T(8,128)(2,1)S(1)}, bf16[2,256,256]{2,1,0:T(8,128)(2,1)S(1)}, u32[]{:S(2)}, u32[]{:S(2)}) collective-permute-start(bf16[2,256,256]{2,1,0:T(8,128)(2,1)S(1)} %get-tuple-element.36), channel_id=1, source_target_pairs={{0,6},{2,4},{4,2},{6,0},{1,7},{3,5},{5,3},{7,1},{8,14},{10,12},{12... | collective-permute-start | bytes 786440 | tf_op jit(solution)/shard_map/ppermute | solution.py:272
  147.5 9.3 %collective-permute-start.10 = (bf16[2,256,256]{2,1,0:T(8,128)(2,1)S(1)}, bf16[2,256,256]{2,1,0:T(8,128)(2,1)S(1)}, u32[]{:S(2)}, u32[]{:S(2)}) collective-permute-start(bf16[2,256,256]{2,1,0:T(8,128)(2,1)S(1)} %get-tuple-element.61), channel_id=1, source_target_pairs={{0,2},{2,0},{4,6},{6,4},{1,3},{3,1},{5,7},{7,5},{8,10},{10,8},{12,... | collective-permute-start | bytes 786440 | tf_op jit(solution)/shard_map/ppermute | solution.py:272
  147.6 21.0 %collective-permute-start.11 = (bf16[2,256,256]{2,1,0:T(8,128)(2,1)S(1)}, bf16[2,256,256]{2,1,0:T(8,128)(2,1)S(1)}, u32[]{:S(2)}, u32[]{:S(2)}) collective-permute-start(bf16[2,256,256]{2,1,0:T(8,128)(2,1)S(1)} %get-tuple-element.60), channel_id=1, source_target_pairs={{0,4},{2,6},{4,0},{6,2},{1,5},{3,7},{5,1},{7,3},{8,12},{10,14},{12... | collective-permute-start | bytes 786440 | tf_op jit(solution)/shard_map/ppermute | solution.py:272
  151.6 20.8 %collective-permute-start.12 = (bf16[2,256,256]{2,1,0:T(8,128)(2,1)S(1)}, bf16[2,256,256]{2,1,0:T(8,128)(2,1)S(1)}, u32[]{:S(2)}, u32[]{:S(2)}) collective-permute-start(bf16[2,256,256]{2,1,0:T(8,128)(2,1)S(1)} %get-tuple-element.59), channel_id=1, source_target_pairs={{0,6},{2,4},{4,2},{6,0},{1,7},{3,5},{5,3},{7,1},{8,14},{10,12},{12... | collective-permute-start | bytes 786440 | tf_op jit(solution)/shard_map/ppermute | solution.py:272
  174.4 0.8 copy-start
  175.2 1.9 collective-permute-start.13
  177.1 0.8 copy-start.5
  177.1 9.5 %collective-permute-start.16 = (bf16[2048,1024]{1,0:T(8,128)(2,1)}, bf16[2048,1024]{1,0:T(8,128)(2,1)}, u32[]{:S(2)}, u32[]{:S(2)}) collective-permute-start(bf16[2048,1024]{1,0:T(8,128)(2,1)} %all-gather.7.cloned.1.call-done.matrix_ref), channel_id=1, source_target_pairs={{0,1},{1,0},{2,3},{3,2},{4,5},{5,4},{6,7},{7,6},{8,9},{9,8},{10,11... | collective-permute-start | bytes 12582920 | tf_op jit(solution)/shard_map/ppermute | solution.py:268
  182.8 30.8 %collective-permute-start.15 = (bf16[256,1024]{1,0:T(8,128)(2,1)}, bf16[256,1024]{1,0:T(8,128)(2,1)S(1)}, u32[]{:S(2)}, u32[]{:S(2)}) collective-permute-start(bf16[256,1024]{1,0:T(8,128)(2,1)} %project.4), channel_id=1, source_target_pairs={{0,32},{32,64},{64,96},{96,128},{128,160},{160,192},{192,224},{224... | collective-permute-start | bytes 1572872 | tf_op jit(solution)/shard_map/ppermute | solution.py:264
  213.6 43.5 %collective-permute-start.19 = (bf16[2048,1024]{1,0:T(8,128)(2,1)}, bf16[2048,1024]{1,0:T(8,128)(2,1)}, u32[]{:S(2)}, u32[]{:S(2)}) collective-permute-start(bf16[2048,1024]{1,0:T(8,128)(2,1)} %all-gather.11.cloned.1.call-done.matrix_ref), channel_id=1, source_target_pairs={{0,1},{1,0},{2,3},{3,2},{4,5},{5,4},{6,7},{7,6},{8,9},{9,8},{10,11... | collective-permute-start | bytes 12582920 | tf_op jit(solution)/shard_map/ppermute | solution.py:268
  213.6 43.4 %collective-permute-start.17 = (bf16[256,1024]{1,0:T(8,128)(2,1)}, bf16[256,1024]{1,0:T(8,128)(2,1)S(1)}, u32[]{:S(2)}, u32[]{:S(2)}) collective-permute-start(bf16[256,1024]{1,0:T(8,128)(2,1)} %project.5), channel_id=1, source_target_pairs={{0,32},{32,64},{64,96},{96,128},{128,160},{160,192},{192,224},{224... | collective-permute-start | bytes 1572872 | tf_op jit(solution)/shard_map/ppermute | solution.py:264
  221.6 46.5 %collective-permute-start.18 = (bf16[256,1024]{1,0:T(8,128)(2,1)}, bf16[256,1024]{1,0:T(8,128)(2,1)S(1)}, u32[]{:S(2)}, u32[]{:S(2)}) collective-permute-start(bf16[256,1024]{1,0:T(8,128)(2,1)} %project.6), channel_id=1, source_target_pairs={{0,32},{32,64},{64,96},{96,128},{128,160},{160,192},{192,224},{224... | collective-permute-start | bytes 1572872 | tf_op jit(solution)/shard_map/ppermute | solution.py:264
  261.9 29.6 %collective-permute-start.20 = (bf16[256,1024]{1,0:T(8,128)(2,1)}, bf16[256,1024]{1,0:T(8,128)(2,1)S(1)}, u32[]{:S(2)}, u32[]{:S(2)}) collective-permute-start(bf16[256,1024]{1,0:T(8,128)(2,1)} %project.7), channel_id=1, source_target_pairs={{0,32},{32,64},{64,96},{96,128},{128,160},{160,192},{192,224},{224... | collective-permute-start | bytes 1572872 | tf_op jit(solution)/shard_map/ppermute | solution.py:264
  268.1 23.4 %copy-start.6 = (bf16[1,256,4096]{2,1,0:T(8,128)(2,1)}, bf16[1,256,4096]{2,1,0:T(8,128)(2,1)S(1)}, u32[]{:S(2)}) copy-start(bf16[1,256,4096]{2,1,0:T(8,128)(2,1)S(1)} %bitcast_dynamic-update-slice_fusion.1) | copy-start | bytes 6291460
Sparse Core Ops, SparseCore 0:
  11.2 49.3 all-gather.4
  62.4 39.0 all-gather.8
  103.3 54.4 all-gather.6
  159.4 52.3 all-gather.10

commit v4 on v3

--- a/solution.py
+++ b/solution.py
@@ -19,6 +19,7 @@
 WINDOWS = (2, 3, 4, 5, 7)
 PARTS = 2
 CHIPS = LINE // 2
+MASKS = (0, 3, 2, 1)
 MIB = 1024 * 1024
 
 
@@ -44,10 +45,10 @@
             for index, ref in enumerate(arrays):
                 if ref.shape[0] == BLK:
                     piece = ref[:, j * PAIR : (j + 1) * PAIR]
-                    out_ref[(j // 2) ^ chip, index * BLK : (index + 1) * BLK] = piece
+                    out_ref[(CHIPS - ((j // 2) ^ chip)) % CHIPS, index * BLK : (index + 1) * BLK] = piece
                 else:
                     labels = (ref[...] + 1).astype(jnp.float32)
-                    out_ref[(j // 2) ^ chip, index * BLK :] = jnp.broadcast_to(labels, (MARK, BLK)).astype(jnp.bfloat16)
+                    out_ref[(CHIPS - ((j // 2) ^ chip)) % CHIPS, index * BLK :] = jnp.broadcast_to(labels, (MARK, BLK)).astype(jnp.bfloat16)
 
         pl.when(core == j % 2)(functools.partial(store, mine_ref))
         pl.when(core != j % 2)(functools.partial(store, other_ref))
@@ -91,7 +92,7 @@
     chip, core = here_ref[0], here_ref[1]
     pairs = []
     for k, ref in enumerate(far):
-        place = 2 * (chip ^ k)
+        place = 2 * (chip ^ MASKS[k])
         pairs += [(ref.at[0], out_ref.at[place + core]), (ref.at[1], out_ref.at[place + 1 - core])]
     run_copies(pairs, sems)
 
@@ -192,7 +193,7 @@
             num_scalar_prefetch=1,
             grid=(LINE,),
             in_specs=[pl.BlockSpec((1, BLK, PAIR), lambda i, here: (i, 0, 0))] + [ANY] * 3,
-            out_specs=pl.BlockSpec((1, 1, BLK, PAIR), lambda i, here: ((i // 2) ^ here[0], i % 2, 0, 0)),
+            out_specs=pl.BlockSpec((1, 1, BLK, PAIR), lambda i, here: ((CHIPS - ((i // 2) ^ here[0])) % CHIPS, i % 2, 0, 0)),
             scratch_shapes=[
                 pltpu.VMEM((BLOCKS, BLK, PAIR), jnp.bfloat16),
                 pltpu.VMEM((BLOCKS, BLK, PAIR), jnp.bfloat16),
@@ -269,7 +270,7 @@
 
 
 def across(pieces):
-    far = [lax.ppermute(piece, "zl", [(z, z ^ k) for z in range(CHIPS)]) for k, piece in enumerate(pieces) if k]
+    far = [lax.ppermute(piece, "zl", [(z, z ^ MASKS[k]) for z in range(CHIPS)]) for k, piece in enumerate(pieces) if k]
     return [pieces[0], *far]
 
 
@@ -311,7 +312,7 @@
     attended = [own, to_other_core(send)]
 
     out = jnp.zeros(hidden.shape, hidden.dtype)
-    chips = chip ^ jnp.arange(CHIPS, dtype=jnp.int32)
+    chips = chip ^ jnp.array(MASKS, jnp.int32)
     order = jnp.concatenate([2 * chips + core, 2 * chips + 1 - core])
     made, arrived = [], []
     for p, matrix in enumerate((first, second)):

time: 300 us -> 312 us (1.040)
  waiting for transfers between devices: 206 us -> 215 us
  starting transfers between devices: 27.4 us -> 33.2 us
    all_gather x4, waiting for transfers between devices: 0.03 us -> 23.5 us  [gather(): return lax.all_gather(piece, axis, axis=0, tiled=True)]
    ppermute x9, waiting for transfers between devices: 114 us -> 106 us  [across(): lax.ppermute(piece, 'zl', [(z, z ^ MASKS[k]) for z in range(CHIPS)])]
    ppermute x4, waiting for transfers between devices: 84.6 us -> 79.4 us  [to_next_section(): lax.ppermute(value, ('x', 'zh'), [(s, (s + 1) % 8) for s in range(8)])]
    ppermute x4, starting transfers between devices: 8.42 us -> 13 us  [to_next_section(): lax.ppermute(value, ('x', 'zh'), [(s, (s + 1) % 8) for s in range(8)])]
  transfers between devices with their start and end apart: 25 -> 25, of which waited for: 17 -> 15; matrix products, arithmetic and copies ran while one was open for 1% -> 1% of each run, Pallas kernels for 15% -> 14%
where the time goes in v4:
time: 312 us
  waiting for transfers between devices  215 us (69%)
  Pallas kernels  42.2 us (14%)
  starting transfers between devices  33.2 us (11%)
  between operations  13.4 us (4%)
  local copies, waits for them, and re-layouts  4.61 us (1%)
  other arithmetic  3.9 us (1%)
    ppermute x9, waiting for transfers between devices, across(): lax.ppermute(piece, 'zl', [(z, z ^ MASKS[k]) for z in range(CHIPS)])  106 us
    ppermute x4, waiting for transfers between devices, to_next_section(): lax.ppermute(value, ('x', 'zh'), [(s, (s + 1) % 8) for s in range(8)])  79.4 us
    all_gather x4, waiting for transfers between devices, gather(): return lax.all_gather(piece, axis, axis=0, tiled=True)  23.5 us
    pallas_call x4, Pallas kernels, project(): pl.pallas_call(project_body, in_specs=[SCALARS, WHOLE, WHOLE, ANY, ANY],...  19.8 us
    ppermute x9, starting transfers between devices, across(): lax.ppermute(piece, 'zl', [(z, z ^ MASKS[k]) for z in range(CHIPS)])  15 us
    pallas_call x1, Pallas kernels, attention(): pl.pallas_call(attention_body, grid_spec=pltpu.PrefetchScalarGridSpec(num...  13.6 us
    ppermute x4, starting transfers between devices, to_next_section(): lax.ppermute(value, ('x', 'zh'), [(s, (s + 1) % 8) for s in range(8)])  13 us
  transfers between devices with their start and end apart: 25, of which 15 were waited for; matrix products, arithmetic and copies ran while one was open for 1% of the time, Pallas kernels for 14%

profile of v4, /device:TPU:32, one launch (start us, length us, event | category | flops | bytes accessed | tf_op | source)
XLA Modules:
  0.0 312.0 jit_solution(7268323331167564696)
XLA Ops:
  6.5 1.1 dynamic-slice_bitcast_fusion
  7.8 1.5 collective-permute-done.14
  9.3 1.0 bitcast_select_fusion.1
  10.4 0.7 pad_maximum_fusion
  11.3 1.8 pack.3
  13.2 0.7 pad_maximum_fusion.1
  14.0 2.0 collective-permute-done.4.got_ref
  16.0 0.3 combine.3
  16.3 3.4 %collective-permute-start.6 = (bf16[2,528,256]{2,1,0:T(8,128)(2,1)S(1)}, bf16[2,528,256]{2,1,0:T(8,128)(2,1)S(1)}, u32[]{:S(2)}, u32[]{:S(2)}) collective-permute-start(bf16[2,528,256]{2,1,0:T(8,128)(2,1)S(1)} %get-tuple-element.41), channel_id=1, source_target_pairs={{0,4},{2,6},{4,0},{6,2},{1,5},{3,7},{5,1},{7,3},{8,12},{10,14},{12... | collective-permute-start | bytes 1622024 | tf_op jit(solution)/shard_map/ppermute | solution.py:273
  19.7 1.5 collective-permute-start.7
  21.3 0.7 pack.2
  22.1 1.9 collective-permute-done.got_ref
  24.0 1.2 combine.2
  25.2 46.0 %collective-permute-done.6.refs_2_ = bf16[2,528,256]{2,1,0:T(8,128)(2,1)S(1)} collective-permute-done((bf16[2,528,256]{2,1,0:T(8,128)(2,1)S(1)}, bf16[2,528,256]{2,1,0:T(8,128)(2,1)S(1)}, u32[]{:S(2)}, u32[]{:S(2)}) %collective-permute-start.6) | collective-permute-done | bytes 540704 | tf_op jit(solution)/shard_map/ppermute | solution.py:273
  71.2 12.5 %collective-permute-done.5.refs_1_ = bf16[2,528,256]{2,1,0:T(8,128)(2,1)S(1)} collective-permute-done((bf16[2,528,256]{2,1,0:T(8,128)(2,1)S(1)}, bf16[2,528,256]{2,1,0:T(8,128)(2,1)S(1)}, u32[]{:S(2)}, u32[]{:S(2)}) %collective-permute-start.5) | collective-permute-done | bytes 540704 | tf_op jit(solution)/shard_map/ppermute | solution.py:273
  83.6 0.9 assemble.3.kv_ref
  84.6 1.3 fusion.1
  85.9 3.5 %collective-permute-start.8 = (bf16[3,528,256]{2,1,0:T(8,128)(2,1)}, bf16[3,528,256]{2,1,0:T(8,128)(2,1)}, u32[]{:S(2)}, u32[]{:S(2)}) collective-permute-start(bf16[3,528,256]{2,1,0:T(8,128)(2,1)} %get-tuple-element.58), channel_id=1, source_target_pairs={{0,8},{8,16},{16,24},{1,9},{9,17},{17,25},{2,10},{10,18},{18,26},{... | collective-permute-start | bytes 2433032 | tf_op jit(solution)/shard_map/ppermute | solution.py:303
  89.4 1.3 collective-permute-start.9
  90.7 2.6 collective-permute-start.1
  93.2 1.6 collective-permute-start.3
  94.8 23.2 %collective-permute-done.1.refs_1_ = bf16[2,256,256]{2,1,0:T(8,128)(2,1)S(1)} collective-permute-done((bf16[2,256,256]{2,1,0:T(8,128)(2,1)}, bf16[2,256,256]{2,1,0:T(8,128)(2,1)S(1)}, u32[]{:S(2)}, u32[]{:S(2)}) %collective-permute-start.1) | collective-permute-done | bytes 262176 | tf_op jit(solution)/shard_map/ppermute | solution.py:273
  118.0 6.4 %collective-permute-done.2.refs_2_ = bf16[2,256,256]{2,1,0:T(8,128)(2,1)S(1)} collective-permute-done((bf16[2,256,256]{2,1,0:T(8,128)(2,1)}, bf16[2,256,256]{2,1,0:T(8,128)(2,1)S(1)}, u32[]{:S(2)}, u32[]{:S(2)}) %collective-permute-start.2) | collective-permute-done | bytes 262176 | tf_op jit(solution)/shard_map/ppermute | solution.py:273
  124.5 2.0 assemble.2.query_ref
  126.5 13.6 %attention.1.near_ref = bf16[4,2,256,256]{3,2,1,0:T(8,128)(2,1)S(1)} custom-call(s32[2]{0:T(128)S(1)} %pad_add_fusion.here_ref, bf16[8,256,256]{2,1,0:T(8,128)(2,1)S(1)} %assemble.2.query_ref, bf16[3,528,256]{2,1,0:T(8,128)(2,1)} %collective-permute-done.8.left_ref, bf16[8,528,256]{2,1,0:T(8,128)(2,1)S(1)} %assemble.3.kv_ref, ...), custom_call_target="tpu_custom_call" | custom-call | flops 2400000000 | bytes 9437184 | tf_op jit(solution)/shard_map/attention/pallas_call | solution.py:190
  140.1 1.8 collective-permute-start.10
  141.9 4.2 %collective-permute-start.11 = (bf16[2,256,256]{2,1,0:T(8,128)(2,1)S(1)}, bf16[2,256,256]{2,1,0:T(8,128)(2,1)S(1)}, u32[]{:S(2)}, u32[]{:S(2)}) collective-permute-start(bf16[2,256,256]{2,1,0:T(8,128)(2,1)S(1)} %get-tuple-element.60), channel_id=1, source_target_pairs={{0,4},{2,6},{4,0},{6,2},{1,5},{3,7},{5,1},{7,3},{8,12},{10,14},{12... | collective-permute-start | bytes 786440 | tf_op jit(solution)/shard_map/ppermute | solution.py:273
  146.1 14.5 %collective-permute-done.10.refs_0_ = bf16[2,256,256]{2,1,0:T(8,128)(2,1)S(1)} collective-permute-done((bf16[2,256,256]{2,1,0:T(8,128)(2,1)S(1)}, bf16[2,256,256]{2,1,0:T(8,128)(2,1)S(1)}, u32[]{:S(2)}, u32[]{:S(2)}) %collective-permute-start.10) | collective-permute-done | bytes 262176 | tf_op jit(solution)/shard_map/ppermute | solution.py:273
  160.6 3.7 %collective-permute-done.11.refs_1_ = bf16[2,256,256]{2,1,0:T(8,128)(2,1)S(1)} collective-permute-done((bf16[2,256,256]{2,1,0:T(8,128)(2,1)S(1)}, bf16[2,256,256]{2,1,0:T(8,128)(2,1)S(1)}, u32[]{:S(2)}, u32[]{:S(2)}) %collective-permute-start.11) | collective-permute-done | bytes 262176 | tf_op jit(solution)/shard_map/ppermute | solution.py:273
  164.4 2.0 divide.1
  166.4 0.8 copy-done
  167.2 7.9 %all-gather.7.cloned.1.call-done.matrix_ref = bf16[2048,1024]{1,0:T(8,128)(2,1)} async-done(((bf16[512,1024]{1,0:T(8,128)(2,1)}), bf16[2048,1024]{1,0:T(8,128)(2,1)}) %all-gather.7.cloned.1.call-update) | async-done | bytes 4194320 | tf_op jit(solution)/shard_map/all_gather | solution.py:295
  175.1 0.7 add_add_fusion.place_ref
  175.9 4.8 %project.4 = bf16[256,1024]{1,0:T(8,128)(2,1)} custom-call(s32[9]{0:T(128)} %add_add_fusion.place_ref, bf16[4,256,256]{2,1,0:T(8,128)(2,1)} %copy-done, bf16[4,256,256]{2,1,0:T(8,128)(2,1)} %copy-done.5, bf16[256,4096]{1,0:T(8,128)(2,1)} %bitcast.32, bf16[2048,1024]{1,0:T(8,128)(2,1)} %all-gather.7.cloned.1.call-done.matrix_ref), custom_call_target="tpu_custom_call" | custom-call | flops 2 | bytes 2 | tf_op jit(solution)/shard_map/project/pallas_call | solution.py:243
  180.7 4.9 %collective-permute-start.15 = (bf16[256,1024]{1,0:T(8,128)(2,1)}, bf16[256,1024]{1,0:T(8,128)(2,1)S(1)}, u32[]{:S(2)}, u32[]{:S(2)}) collective-permute-start(bf16[256,1024]{1,0:T(8,128)(2,1)} %project.4), channel_id=1, source_target_pairs={{0,32},{32,64},{64,96},{96,128},{128,160},{160,192},{192,224},{224... | collective-permute-start | bytes 1572872 | tf_op jit(solution)/shard_map/ppermute | solution.py:265
  185.6 0.7 add_add_fusion.3
  186.3 5.3 %project.5 = bf16[256,1024]{1,0:T(8,128)(2,1)} custom-call(s32[9]{0:T(128)} %get-tuple-element.69.place_ref, bf16[4,256,256]{2,1,0:T(8,128)(2,1)} %copy-done, bf16[4,256,256]{2,1,0:T(8,128)(2,1)} %copy-done.5, bf16[256,4096]{1,0:T(8,128)(2,1)} %bitcast.33, bf16[2048,1024]{1,0:T(8,128)(2,1)} %collective-permute-done.16.matrix_ref), custom_call_target="tpu_custom_call" | custom-call | flops 2 | bytes 2 | tf_op jit(solution)/shard_map/project/pallas_call | solution.py:243
  191.6 20.8 %collective-permute-done.15 = bf16[256,1024]{1,0:T(8,128)(2,1)S(1)} collective-permute-done((bf16[256,1024]{1,0:T(8,128)(2,1)}, bf16[256,1024]{1,0:T(8,128)(2,1)S(1)}, u32[]{:S(2)}, u32[]{:S(2)}) %collective-permute-start.15) | collective-permute-done | bytes 524320 | tf_op jit(solution)/shard_map/ppermute | solution.py:265
  212.4 15.5 %all-gather.11.cloned.1.call-done.matrix_ref = bf16[2048,1024]{1,0:T(8,128)(2,1)} async-done(((bf16[512,1024]{1,0:T(8,128)(2,1)}), bf16[2048,1024]{1,0:T(8,128)(2,1)}) %all-gather.11.cloned.1.call-update) | async-done | bytes 4194320 | tf_op jit(solution)/shard_map/all_gather | solution.py:295
  227.9 4.8 %collective-permute-start.17 = (bf16[256,1024]{1,0:T(8,128)(2,1)}, bf16[256,1024]{1,0:T(8,128)(2,1)S(1)}, u32[]{:S(2)}, u32[]{:S(2)}) collective-permute-start(bf16[256,1024]{1,0:T(8,128)(2,1)} %project.5), channel_id=1, source_target_pairs={{0,32},{32,64},{64,96},{96,128},{128,160},{160,192},{192,224},{224... | collective-permute-start | bytes 1572872 | tf_op jit(solution)/shard_map/ppermute | solution.py:265
  232.8 4.8 %project.6 = bf16[256,1024]{1,0:T(8,128)(2,1)} custom-call(s32[9]{0:T(128)} %get-tuple-element.70.place_ref, bf16[4,256,256]{2,1,0:T(8,128)(2,1)} %copy-done, bf16[4,256,256]{2,1,0:T(8,128)(2,1)} %copy-done.5, bf16[256,4096]{1,0:T(8,128)(2,1)} %bitcast.34, bf16[2048,1024]{1,0:T(8,128)(2,1)} %all-gather.11.cloned.1.call-done.matrix_ref), custom_call_target="tpu_custom_call" | custom-call | flops 2 | bytes 2 | tf_op jit(solution)/shard_map/project/pallas_call | solution.py:243
  237.6 2.1 collective-permute-start.18
  239.7 22.6 %collective-permute-done.17 = bf16[256,1024]{1,0:T(8,128)(2,1)S(1)} collective-permute-done((bf16[256,1024]{1,0:T(8,128)(2,1)}, bf16[256,1024]{1,0:T(8,128)(2,1)S(1)}, u32[]{:S(2)}, u32[]{:S(2)}) %collective-permute-start.17) | collective-permute-done | bytes 524320 | tf_op jit(solution)/shard_map/ppermute | solution.py:265
  262.3 4.8 %project.7 = bf16[256,1024]{1,0:T(8,128)(2,1)} custom-call(s32[9]{0:T(128)} %get-tuple-element.68.place_ref, bf16[4,256,256]{2,1,0:T(8,128)(2,1)} %copy-done, bf16[4,256,256]{2,1,0:T(8,128)(2,1)} %copy-done.5, bf16[256,4096]{1,0:T(8,128)(2,1)} %bitcast.35, bf16[2048,1024]{1,0:T(8,128)(2,1)} %collective-permute-done.19.matrix_ref), custom_call_target="tpu_custom_call" | custom-call | flops 2 | bytes 2 | tf_op jit(solution)/shard_map/project/pallas_call | solution.py:243
  267.1 1.2 collective-permute-start.20
  268.6 18.1 %collective-permute-done.18 = bf16[256,1024]{1,0:T(8,128)(2,1)S(1)} collective-permute-done((bf16[256,1024]{1,0:T(8,128)(2,1)}, bf16[256,1024]{1,0:T(8,128)(2,1)S(1)}, u32[]{:S(2)}, u32[]{:S(2)}) %collective-permute-start.18) | collective-permute-done | bytes 524320 | tf_op jit(solution)/shard_map/ppermute | solution.py:265
  286.8 17.9 %collective-permute-done.20 = bf16[256,1024]{1,0:T(8,128)(2,1)S(1)} collective-permute-done((bf16[256,1024]{1,0:T(8,128)(2,1)}, bf16[256,1024]{1,0:T(8,128)(2,1)S(1)}, u32[]{:S(2)}, u32[]{:S(2)}) %collective-permute-start.20) | collective-permute-done | bytes 524320 | tf_op jit(solution)/shard_map/ppermute | solution.py:265
  304.7 0.8 bitcast_dynamic-update-slice_fusion
  (50 shorter events, 1.3 us)
Async XLA Ops:
  6.5 4.7 %copy-start.1 = (bf16[1,256,2048]{2,1,0:T(8,128)(2,1)S(1)}, bf16[1,256,2048]{2,1,0:T(8,128)(2,1)}, u32[]{:S(2)}) copy-start(bf16[1,256,2048]{2,1,0:T(8,128)(2,1)} %param.9) | copy-start | bytes 3145732
  6.5 4.7 %copy-start.2 = (bf16[1,256,2048]{2,1,0:T(8,128)(2,1)S(1)}, bf16[1,256,2048]{2,1,0:T(8,128)(2,1)}, u32[]{:S(2)}) copy-start(bf16[1,256,2048]{2,1,0:T(8,128)(2,1)} %param.10) | copy-start | bytes 3145732
  6.5 4.7 %copy-start.4 = (s32[1,256]{1,0:T(1,128)S(1)}, s32[1,256]{1,0:T(1,128)}, u32[]{:S(2)}) copy-start(s32[1,256]{1,0:T(1,128)} %refs_2_.1) | copy-start | bytes 3076
  6.5 78.0 %all-gather.5.cloned.1.call-start = ((), (), s32[]{:S(2)}) async-start(), calls=%async_computation | async-start | bytes 1310720 | tf_op jit(solution)/shard_map/all_gather | solution.py:295
  7.7 1.6 collective-permute-start.14
  11.1 113.3 %all-gather.9.cloned.1.call-start = ((), (), s32[]{:S(2)}) async-start(), calls=%async_computation.2 | async-start | bytes 1310720 | tf_op jit(solution)/shard_map/all_gather | solution.py:295
  13.1 8.2 %copy-start.3 = (bf16[1,256,2048]{2,1,0:T(8,128)(2,1)S(1)}, bf16[1,256,2048]{2,1,0:T(8,128)(2,1)}, u32[]{:S(2)}) copy-start(bf16[1,256,2048]{2,1,0:T(8,128)(2,1)} %param.8) | copy-start | bytes 3145732
  13.1 2.9 collective-permute-start.4
  14.0 161.1 %all-gather.7.cloned.1.call-start = ((), (), s32[]{:S(2)}) async-start(), calls=%async_computation.1 | async-start | bytes 5242880 | tf_op jit(solution)/shard_map/all_gather | solution.py:295
  16.3 54.8 %collective-permute-start.6 = (bf16[2,528,256]{2,1,0:T(8,128)(2,1)S(1)}, bf16[2,528,256]{2,1,0:T(8,128)(2,1)S(1)}, u32[]{:S(2)}, u32[]{:S(2)}) collective-permute-start(bf16[2,528,256]{2,1,0:T(8,128)(2,1)S(1)} %get-tuple-element.41), channel_id=1, source_target_pairs={{0,4},{2,6},{4,0},{6,2},{1,5},{3,7},{5,1},{7,3},{8,12},{10,14},{12... | collective-permute-start | bytes 1622024 | tf_op jit(solution)/shard_map/ppermute | solution.py:273
  19.7 63.9 %collective-permute-start.5 = (bf16[2,528,256]{2,1,0:T(8,128)(2,1)S(1)}, bf16[2,528,256]{2,1,0:T(8,128)(2,1)S(1)}, u32[]{:S(2)}, u32[]{:S(2)}) collective-permute-start(bf16[2,528,256]{2,1,0:T(8,128)(2,1)S(1)} %get-tuple-element.40), channel_id=1, source_target_pairs={{0,6},{2,4},{4,2},{6,0},{1,7},{3,5},{5,3},{7,1},{8,14},{10,12},{12... | collective-permute-start | bytes 1622024 | tf_op jit(solution)/shard_map/ppermute | solution.py:273
  19.7 63.9 %collective-permute-start.7 = (bf16[2,528,256]{2,1,0:T(8,128)(2,1)S(1)}, bf16[2,528,256]{2,1,0:T(8,128)(2,1)S(1)}, u32[]{:S(2)}, u32[]{:S(2)}) collective-permute-start(bf16[2,528,256]{2,1,0:T(8,128)(2,1)S(1)} %get-tuple-element.43), channel_id=1, source_target_pairs={{0,2},{2,0},{4,6},{6,4},{1,3},{3,1},{5,7},{7,5},{8,10},{10,8},{12,... | collective-permute-start | bytes 1622024 | tf_op jit(solution)/shard_map/ppermute | solution.py:273
  22.0 2.0 collective-permute-start
  84.6 143.4 %all-gather.11.cloned.1.call-start = ((), (), s32[]{:S(2)}) async-start(), calls=%async_computation.3 | async-start | bytes 5242880 | tf_op jit(solution)/shard_map/all_gather | solution.py:295
  85.9 38.5 %collective-permute-start.8 = (bf16[3,528,256]{2,1,0:T(8,128)(2,1)}, bf16[3,528,256]{2,1,0:T(8,128)(2,1)}, u32[]{:S(2)}, u32[]{:S(2)}) collective-permute-start(bf16[3,528,256]{2,1,0:T(8,128)(2,1)} %get-tuple-element.58), channel_id=1, source_target_pairs={{0,8},{8,16},{16,24},{1,9},{9,17},{17,25},{2,10},{10,18},{18,26},{... | collective-permute-start | bytes 2433032 | tf_op jit(solution)/shard_map/ppermute | solution.py:303
  89.4 35.1 %collective-permute-start.9 = (bf16[3,528,256]{2,1,0:T(8,128)(2,1)}, bf16[3,528,256]{2,1,0:T(8,128)(2,1)}, u32[]{:S(2)}, u32[]{:S(2)}) collective-permute-start(bf16[3,528,256]{2,1,0:T(8,128)(2,1)} %get-tuple-element.57), channel_id=1, source_target_pairs={{8,0},{16,8},{24,16},{9,1},{17,9},{25,17},{10,2},{18,10},{26,18},{... | collective-permute-start | bytes 2433032 | tf_op jit(solution)/shard_map/ppermute | solution.py:304
  90.7 27.4 %collective-permute-start.1 = (bf16[2,256,256]{2,1,0:T(8,128)(2,1)}, bf16[2,256,256]{2,1,0:T(8,128)(2,1)S(1)}, u32[]{:S(2)}, u32[]{:S(2)}) collective-permute-start(bf16[2,256,256]{2,1,0:T(8,128)(2,1)} %get-tuple-element.34), channel_id=1, source_target_pairs={{0,6},{2,4},{4,2},{6,0},{1,7},{3,5},{5,3},{7,1},{8,14},{10,12},{12... | collective-permute-start | bytes 786440 | tf_op jit(solution)/shard_map/ppermute | solution.py:273
  93.2 31.2 %collective-permute-start.2 = (bf16[2,256,256]{2,1,0:T(8,128)(2,1)}, bf16[2,256,256]{2,1,0:T(8,128)(2,1)S(1)}, u32[]{:S(2)}, u32[]{:S(2)}) collective-permute-start(bf16[2,256,256]{2,1,0:T(8,128)(2,1)} %get-tuple-element.35), channel_id=1, source_target_pairs={{0,4},{2,6},{4,0},{6,2},{1,5},{3,7},{5,1},{7,3},{8,12},{10,14},{12... | collective-permute-start | bytes 786440 | tf_op jit(solution)/shard_map/ppermute | solution.py:273
  93.2 31.2 %collective-permute-start.3 = (bf16[2,256,256]{2,1,0:T(8,128)(2,1)S(1)}, bf16[2,256,256]{2,1,0:T(8,128)(2,1)S(1)}, u32[]{:S(2)}, u32[]{:S(2)}) collective-permute-start(bf16[2,256,256]{2,1,0:T(8,128)(2,1)S(1)} %get-tuple-element.36), channel_id=1, source_target_pairs={{0,2},{2,0},{4,6},{6,4},{1,3},{3,1},{5,7},{7,5},{8,10},{10,8},{12,... | collective-permute-start | bytes 786440 | tf_op jit(solution)/shard_map/ppermute | solution.py:273
  140.0 35.1 %copy-start.7 = (s32[4]{0:T(128)S(1)}, s32[4]{0:T(128)}, u32[]{:S(2)}) copy-start(s32[4]{0:T(128)} %constant.35.clone) | copy-start | bytes 52
  140.1 20.5 %collective-permute-start.10 = (bf16[2,256,256]{2,1,0:T(8,128)(2,1)S(1)}, bf16[2,256,256]{2,1,0:T(8,128)(2,1)S(1)}, u32[]{:S(2)}, u32[]{:S(2)}) collective-permute-start(bf16[2,256,256]{2,1,0:T(8,128)(2,1)S(1)} %get-tuple-element.61), channel_id=1, source_target_pairs={{0,6},{2,4},{4,2},{6,0},{1,7},{3,5},{5,3},{7,1},{8,14},{10,12},{12... | collective-permute-start | bytes 786440 | tf_op jit(solution)/shard_map/ppermute | solution.py:273
  141.9 22.5 %collective-permute-start.11 = (bf16[2,256,256]{2,1,0:T(8,128)(2,1)S(1)}, bf16[2,256,256]{2,1,0:T(8,128)(2,1)S(1)}, u32[]{:S(2)}, u32[]{:S(2)}) collective-permute-start(bf16[2,256,256]{2,1,0:T(8,128)(2,1)S(1)} %get-tuple-element.60), channel_id=1, source_target_pairs={{0,4},{2,6},{4,0},{6,2},{1,5},{3,7},{5,1},{7,3},{8,12},{10,14},{12... | collective-permute-start | bytes 786440 | tf_op jit(solution)/shard_map/ppermute | solution.py:273
  146.1 18.3 %collective-permute-start.12 = (bf16[2,256,256]{2,1,0:T(8,128)(2,1)S(1)}, bf16[2,256,256]{2,1,0:T(8,128)(2,1)S(1)}, u32[]{:S(2)}, u32[]{:S(2)}) collective-permute-start(bf16[2,256,256]{2,1,0:T(8,128)(2,1)S(1)} %get-tuple-element.59), channel_id=1, source_target_pairs={{0,2},{2,0},{4,6},{6,4},{1,3},{3,1},{5,7},{7,5},{8,10},{10,8},{12,... | collective-permute-start | bytes 786440 | tf_op jit(solution)/shard_map/ppermute | solution.py:273
  166.4 0.8 copy-start
  167.2 7.9 %collective-permute-start.13 = (bf16[4,256,256]{2,1,0:T(8,128)(2,1)S(1)}, bf16[4,256,256]{2,1,0:T(8,128)(2,1)S(1)}, u32[]{:S(2)}, u32[]{:S(2)}) collective-permute-start(bf16[4,256,256]{2,1,0:T(8,128)(2,1)S(1)} %get-tuple-element.45), channel_id=1, source_target_pairs={{0,1},{1,0},{2,3},{3,2},{4,5},{5,4},{6,7},{7,6},{8,9},{9,8},{10,11... | collective-permute-start | bytes 1572872 | tf_op jit(solution)/shard_map/ppermute | solution.py:269
  175.1 0.8 copy-start.5
  175.1 11.2 %collective-permute-start.16 = (bf16[2048,1024]{1,0:T(8,128)(2,1)}, bf16[2048,1024]{1,0:T(8,128)(2,1)}, u32[]{:S(2)}, u32[]{:S(2)}) collective-permute-start(bf16[2048,1024]{1,0:T(8,128)(2,1)} %all-gather.7.cloned.1.call-done.matrix_ref), channel_id=1, source_target_pairs={{0,1},{1,0},{2,3},{3,2},{4,5},{5,4},{6,7},{7,6},{8,9},{9,8},{10,11... | collective-permute-start | bytes 12582920 | tf_op jit(solution)/shard_map/ppermute | solution.py:269
  180.7 31.7 %collective-permute-start.15 = (bf16[256,1024]{1,0:T(8,128)(2,1)}, bf16[256,1024]{1,0:T(8,128)(2,1)S(1)}, u32[]{:S(2)}, u32[]{:S(2)}) collective-permute-start(bf16[256,1024]{1,0:T(8,128)(2,1)} %project.4), channel_id=1, source_target_pairs={{0,32},{32,64},{64,96},{96,128},{128,160},{160,192},{192,224},{224... | collective-permute-start | bytes 1572872 | tf_op jit(solution)/shard_map/ppermute | solution.py:265
  227.9 34.4 %collective-permute-start.19 = (bf16[2048,1024]{1,0:T(8,128)(2,1)}, bf16[2048,1024]{1,0:T(8,128)(2,1)}, u32[]{:S(2)}, u32[]{:S(2)}) collective-permute-start(bf16[2048,1024]{1,0:T(8,128)(2,1)} %all-gather.11.cloned.1.call-done.matrix_ref), channel_id=1, source_target_pairs={{0,1},{1,0},{2,3},{3,2},{4,5},{5,4},{6,7},{7,6},{8,9},{9,8},{10,11... | collective-permute-start | bytes 12582920 | tf_op jit(solution)/shard_map/ppermute | solution.py:269
  227.9 34.3 %collective-permute-start.17 = (bf16[256,1024]{1,0:T(8,128)(2,1)}, bf16[256,1024]{1,0:T(8,128)(2,1)S(1)}, u32[]{:S(2)}, u32[]{:S(2)}) collective-permute-start(bf16[256,1024]{1,0:T(8,128)(2,1)} %project.5), channel_id=1, source_target_pairs={{0,32},{32,64},{64,96},{96,128},{128,160},{160,192},{192,224},{224... | collective-permute-start | bytes 1572872 | tf_op jit(solution)/shard_map/ppermute | solution.py:265
  237.6 49.2 %collective-permute-start.18 = (bf16[256,1024]{1,0:T(8,128)(2,1)}, bf16[256,1024]{1,0:T(8,128)(2,1)S(1)}, u32[]{:S(2)}, u32[]{:S(2)}) collective-permute-start(bf16[256,1024]{1,0:T(8,128)(2,1)} %project.6), channel_id=1, source_target_pairs={{0,32},{32,64},{64,96},{96,128},{128,160},{160,192},{192,224},{224... | collective-permute-start | bytes 1572872 | tf_op jit(solution)/shard_map/ppermute | solution.py:265
  267.1 37.5 %collective-permute-start.20 = (bf16[256,1024]{1,0:T(8,128)(2,1)}, bf16[256,1024]{1,0:T(8,128)(2,1)S(1)}, u32[]{:S(2)}, u32[]{:S(2)}) collective-permute-start(bf16[256,1024]{1,0:T(8,128)(2,1)} %project.7), channel_id=1, source_target_pairs={{0,32},{32,64},{64,96},{96,128},{128,160},{160,192},{192,224},{224... | collective-permute-start | bytes 1572872 | tf_op jit(solution)/shard_map/ppermute | solution.py:265
  286.8 17.9 %copy-start.6 = (bf16[1,256,4096]{2,1,0:T(8,128)(2,1)}, bf16[1,256,4096]{2,1,0:T(8,128)(2,1)S(1)}, u32[]{:S(2)}) copy-start(bf16[1,256,4096]{2,1,0:T(8,128)(2,1)S(1)} %bitcast_dynamic-update-slice_fusion.1) | copy-start | bytes 6291460
Sparse Core Ops, SparseCore 0:
  11.2 61.3 all-gather.4
  74.4 48.8 all-gather.8
  125.2 49.8 all-gather.6
  176.7 51.1 all-gather.10

commit v5 on v3

--- a/solution.py
+++ b/solution.py
@@ -17,7 +17,8 @@
 MARK = 16
 LOG2E = 1.4426950408889634
 WINDOWS = (2, 3, 4, 5, 7)
-PARTS = 2
+PARTS = (1280, 768)
+LANE = 128
 CHIPS = LINE // 2
 MIB = 1024 * 1024
 
@@ -214,7 +215,7 @@
     for n in range(LINE):
         first = pl.multiple_of(place_ref[1 + n] * PAIR, PAIR)
         copies.append(pltpu.make_async_copy(matrix_ref.at[pl.ds(first, PAIR)], rows_ref.at[n], sems.at[n]))
-    first = pl.multiple_of(place_ref[0] * columns, columns)
+    first = pl.multiple_of(place_ref[0] * LANE, LANE)
     rest = pltpu.make_async_copy(hidden_ref.at[:, pl.ds(first, columns)], rest_ref, sems.at[LINE])
     for copy in (*copies, rest):
         copy.start()
@@ -278,7 +279,7 @@
     here = jnp.stack([chip, core]).astype(jnp.int32)
     hidden, weight = hidden[0], out_weight[0]
     half = hidden.shape[1] // 2
-    part = half // PARTS
+    begins = (0, PARTS[0])
 
     kv, kv_other = pack(here, keyv[0], value[0], segments)
     kv_out = combine(kv, to_other_core(kv_other))
@@ -288,7 +289,7 @@
     rows = [lax.dynamic_slice_in_dim(weight, which * half, half, 1) for which in (core, 1 - core)]
     rows[1] = to_other_core(rows[1])
     rows = [jnp.where(core == place, *rows) for place in (0, 1)]
-    rows = [jnp.concatenate([row[:, p * part : (p + 1) * part] for row in rows], axis=0) for p in range(PARTS)]
+    rows = [jnp.concatenate([row[:, at : at + part] for row in rows], axis=0) for at, part in zip(begins, PARTS)]
 
     def gather(piece, axis):
         return lax.all_gather(piece, axis, axis=0, tiled=True)
@@ -314,14 +315,14 @@
     chips = chip ^ jnp.arange(CHIPS, dtype=jnp.int32)
     order = jnp.concatenate([2 * chips + core, 2 * chips + 1 - core])
     made, arrived = [], []
-    for p, matrix in enumerate((first, second)):
+    for begin, matrix in zip(begins, (first, second)):
         matrix = after(matrix, *attended, *made[-1:], *arrived[-2:-1])
         for which, matrix in ((core, matrix), (1 - core, to_other_core(matrix))):
-            place = jnp.concatenate([(which * PARTS + p)[None], order]).astype(jnp.int32)
+            place = jnp.concatenate([((which * half + begin) // LANE)[None], order]).astype(jnp.int32)
             ready = [after(rows, *made[-1:], *arrived[-2:-1]) for rows in attended]
             made.append(project(place, ready, hidden, matrix))
             arrived.append(to_next_section(made[-1]))
-            out = lax.dynamic_update_slice(out, arrived[-1], (0, which * half + p * part))
+            out = lax.dynamic_update_slice(out, arrived[-1], (0, which * half + begin))
     return out[None]
 
 

time: 300 us -> 309 us (1.030)
  waiting for transfers between devices: 206 us -> 188 us
  blocking collectives: 0 us -> 17.6 us
  local copies, waits for them, and re-layouts: 4.55 us -> 11.8 us
  starting transfers between devices: 27.4 us -> 30.9 us
    ppermute x4, waiting for transfers between devices: 84.6 us -> 44 us  [to_next_section(): lax.ppermute(value, ('x', 'zh'), [(s, (s + 1) % 8) for s in range(8)])]
    all_gather x4 -> x3, waiting for transfers between devices: 0.03 us -> 29.8 us  [gather(): return lax.all_gather(piece, axis, axis=0, tiled=True)]
    all_gather x0 -> x1, blocking collectives: none -> 17.6 us  [gather(): return lax.all_gather(piece, axis, axis=0, tiled=True)]
    ppermute x9, waiting for transfers between devices: 114 us -> 106 us  [across(): lax.ppermute(piece, 'zl', [(z, z ^ k) for z in range(CHIPS)])]
    ppermute x4, starting transfers between devices: 8.42 us -> 13.8 us  [to_next_section(): lax.ppermute(value, ('x', 'zh'), [(s, (s + 1) % 8) for s in range(8)])]
    dynamic_update_slice x4, local copies, waits for them, and re-layouts: 0.96 us -> 5.47 us  [on_device(): out = lax.dynamic_update_slice(out, arrived[-1], (0, which * half + begin))]
  transfers between devices with their start and end apart: 25 -> 24, of which waited for: 17 -> 16; matrix products, arithmetic and copies ran while one was open for 1% -> 3% of each run, Pallas kernels for 15% -> 14%
where the time goes in v5:
time: 309 us; the launch traced here: 307 us
  waiting for transfers between devices  188 us (61%)
  Pallas kernels  42.4 us (14%)
  starting transfers between devices  30.9 us (10%)
  blocking collectives  17.6 us (6%)
  between operations  13.4 us (4%)
  local copies, waits for them, and re-layouts  11.8 us (4%)
  other arithmetic  3.21 us (1%)
    ppermute x9, waiting for transfers between devices, across(): lax.ppermute(piece, 'zl', [(z, z ^ k) for z in range(CHIPS)])  106 us
    ppermute x4, waiting for transfers between devices, to_next_section(): lax.ppermute(value, ('x', 'zh'), [(s, (s + 1) % 8) for s in range(8)])  44 us
    all_gather x3, waiting for transfers between devices, gather(): return lax.all_gather(piece, axis, axis=0, tiled=True)  29.8 us
    pallas_call x4, Pallas kernels, project(): pl.pallas_call(project_body, in_specs=[SCALARS, WHOLE, WHOLE, ANY, ANY],...  20.5 us
    all_gather x1, blocking collectives, gather(): return lax.all_gather(piece, axis, axis=0, tiled=True)  17.6 us
    ppermute x4, starting transfers between devices, to_next_section(): lax.ppermute(value, ('x', 'zh'), [(s, (s + 1) % 8) for s in range(8)])  13.8 us
    pallas_call x1, Pallas kernels, attention(): pl.pallas_call(attention_body, grid_spec=pltpu.PrefetchScalarGridSpec(num...  13.7 us
    ppermute x9, starting transfers between devices, across(): lax.ppermute(piece, 'zl', [(z, z ^ k) for z in range(CHIPS)])  12.6 us
  transfers between devices with their start and end apart: 24, of which 16 were waited for; matrix products, arithmetic and copies ran while one was open for 3% of the time, Pallas kernels for 14%

profile of v5, /device:TPU:32, one launch (start us, length us, event | category | flops | bytes accessed | tf_op | source)
XLA Modules:
  0.0 307.1 jit_solution(12547155284796547421)
XLA Ops:
  6.5 1.1 dynamic-slice_bitcast_fusion
  7.8 1.5 collective-permute-done.14
  9.3 1.0 bitcast_select_fusion.1
  10.4 0.8 pad_maximum_fusion
  11.3 0.9 pack.3
  12.4 2.6 collective-permute-done.4.got_ref
  15.3 3.4 %collective-permute-start.6 = (bf16[2,528,256]{2,1,0:T(8,128)(2,1)S(1)}, bf16[2,528,256]{2,1,0:T(8,128)(2,1)S(1)}, u32[]{:S(2)}, u32[]{:S(2)}) collective-permute-start(bf16[2,528,256]{2,1,0:T(8,128)(2,1)S(1)} %get-tuple-element.41), channel_id=1, source_target_pairs={{0,4},{2,6},{4,0},{6,2},{1,5},{3,7},{5,1},{7,3},{8,12},{10,14},{12... | collective-permute-start | bytes 1622024 | tf_op jit(solution)/shard_map/ppermute | solution.py:273
  19.3 0.7 pack.2
  20.1 1.9 collective-permute-done.got_ref
  22.0 1.4 combine.2
  23.5 43.4 %collective-permute-done.6.refs_2_ = bf16[2,528,256]{2,1,0:T(8,128)(2,1)S(1)} collective-permute-done((bf16[2,528,256]{2,1,0:T(8,128)(2,1)S(1)}, bf16[2,528,256]{2,1,0:T(8,128)(2,1)S(1)}, u32[]{:S(2)}, u32[]{:S(2)}) %collective-permute-start.6) | collective-permute-done | bytes 540704 | tf_op jit(solution)/shard_map/ppermute | solution.py:273
  66.8 20.0 %collective-permute-done.7.refs_3_ = bf16[2,528,256]{2,1,0:T(8,128)(2,1)S(1)} collective-permute-done((bf16[2,528,256]{2,1,0:T(8,128)(2,1)S(1)}, bf16[2,528,256]{2,1,0:T(8,128)(2,1)S(1)}, u32[]{:S(2)}, u32[]{:S(2)}) %collective-permute-start.7) | collective-permute-done | bytes 540704 | tf_op jit(solution)/shard_map/ppermute | solution.py:273
  86.8 0.9 assemble.3.kv_ref
  87.9 2.6 collective-permute-start.8
  90.5 1.3 collective-permute-start.9
  91.9 3.9 %collective-permute-start.2 = (bf16[2,256,256]{2,1,0:T(8,128)(2,1)S(1)}, bf16[2,256,256]{2,1,0:T(8,128)(2,1)S(1)}, u32[]{:S(2)}, u32[]{:S(2)}) collective-permute-start(bf16[2,256,256]{2,1,0:T(8,128)(2,1)S(1)} %get-tuple-element.35), channel_id=1, source_target_pairs={{0,4},{2,6},{4,0},{6,2},{1,5},{3,7},{5,1},{7,3},{8,12},{10,14},{12... | collective-permute-start | bytes 786440 | tf_op jit(solution)/shard_map/ppermute | solution.py:273
  95.8 7.1 %collective-permute-done.1.refs_1_ = bf16[2,256,256]{2,1,0:T(8,128)(2,1)S(1)} collective-permute-done((bf16[2,256,256]{2,1,0:T(8,128)(2,1)S(1)}, bf16[2,256,256]{2,1,0:T(8,128)(2,1)S(1)}, u32[]{:S(2)}, u32[]{:S(2)}) %collective-permute-start.1) | collective-permute-done | bytes 262176 | tf_op jit(solution)/shard_map/ppermute | solution.py:273
  102.9 10.9 %collective-permute-done.2.refs_2_ = bf16[2,256,256]{2,1,0:T(8,128)(2,1)S(1)} collective-permute-done((bf16[2,256,256]{2,1,0:T(8,128)(2,1)S(1)}, bf16[2,256,256]{2,1,0:T(8,128)(2,1)S(1)}, u32[]{:S(2)}, u32[]{:S(2)}) %collective-permute-start.2) | collective-permute-done | bytes 262176 | tf_op jit(solution)/shard_map/ppermute | solution.py:273
  113.8 4.1 %collective-permute-done.3.refs_3_ = bf16[2,256,256]{2,1,0:T(8,128)(2,1)S(1)} collective-permute-done((bf16[2,256,256]{2,1,0:T(8,128)(2,1)S(1)}, bf16[2,256,256]{2,1,0:T(8,128)(2,1)S(1)}, u32[]{:S(2)}, u32[]{:S(2)}) %collective-permute-start.3) | collective-permute-done | bytes 262176 | tf_op jit(solution)/shard_map/ppermute | solution.py:273
  117.9 2.0 assemble.2.query_ref
  119.9 13.7 %attention.1.near_ref = bf16[4,2,256,256]{3,2,1,0:T(8,128)(2,1)S(1)} custom-call(s32[2]{0:T(128)S(1)} %pad_add_fusion.here_ref, bf16[8,256,256]{2,1,0:T(8,128)(2,1)S(1)} %assemble.2.query_ref, bf16[3,528,256]{2,1,0:T(8,128)(2,1)S(1)} %collective-permute-done.8.left_ref, bf16[8,528,256]{2,1,0:T(8,128)(2,1)S(1)} %assemble.3.kv_ref, ...), custom_call_target="tpu_custom_call" | custom-call | flops 2400000000 | bytes 9437184 | tf_op jit(solution)/shard_map/attention/pallas_call | solution.py:190
  133.9 4.5 %collective-permute-start.11 = (bf16[2,256,256]{2,1,0:T(8,128)(2,1)S(1)}, bf16[2,256,256]{2,1,0:T(8,128)(2,1)S(1)}, u32[]{:S(2)}, u32[]{:S(2)}) collective-permute-start(bf16[2,256,256]{2,1,0:T(8,128)(2,1)S(1)} %get-tuple-element.60), channel_id=1, source_target_pairs={{0,4},{2,6},{4,0},{6,2},{1,5},{3,7},{5,1},{7,3},{8,12},{10,14},{12... | collective-permute-start | bytes 786440 | tf_op jit(solution)/shard_map/ppermute | solution.py:273
  138.3 4.7 %collective-permute-done.10.refs_0_ = bf16[2,256,256]{2,1,0:T(8,128)(2,1)S(1)} collective-permute-done((bf16[2,256,256]{2,1,0:T(8,128)(2,1)S(1)}, bf16[2,256,256]{2,1,0:T(8,128)(2,1)S(1)}, u32[]{:S(2)}, u32[]{:S(2)}) %collective-permute-start.10) | collective-permute-done | bytes 262176 | tf_op jit(solution)/shard_map/ppermute | solution.py:273
  143.1 12.2 %collective-permute-done.11.refs_1_ = bf16[2,256,256]{2,1,0:T(8,128)(2,1)S(1)} collective-permute-done((bf16[2,256,256]{2,1,0:T(8,128)(2,1)S(1)}, bf16[2,256,256]{2,1,0:T(8,128)(2,1)S(1)}, u32[]{:S(2)}, u32[]{:S(2)}) %collective-permute-start.11) | collective-permute-done | bytes 262176 | tf_op jit(solution)/shard_map/ppermute | solution.py:273
  155.3 3.5 %collective-permute-done.12.refs_2_ = bf16[2,256,256]{2,1,0:T(8,128)(2,1)S(1)} collective-permute-done((bf16[2,256,256]{2,1,0:T(8,128)(2,1)S(1)}, bf16[2,256,256]{2,1,0:T(8,128)(2,1)S(1)}, u32[]{:S(2)}, u32[]{:S(2)}) %collective-permute-start.12) | collective-permute-done | bytes 262176 | tf_op jit(solution)/shard_map/ppermute | solution.py:273
  158.8 2.0 divide.1
  160.8 0.8 copy-done
  161.6 1.9 collective-permute-done.13.got_ref
  163.7 1.0 slice.44
  164.7 17.6 %all_gather.14 = bf16[512,768]{1,0:T(8,128)(2,1)} all-gather(bf16[128,768]{1,0:T(8,128)(2,1)S(1)} %pad_maximum_fusion.1), channel_id=1, replica_groups=mesh['x'=4,'zh'=2,'y'=4,'zl'=4,'c'=2] {'zl'}, dimensions={0}, use_global_device_ids=true | all-gather | bytes 983040 | tf_op jit(solution)/shard_map/all_gather | solution.py:295
  183.0 5.5 %project.4 = bf16[256,1280]{1,0:T(8,128)(2,1)} custom-call(s32[9]{0:T(128)} %add_add_fusion.place_ref, bf16[4,256,256]{2,1,0:T(8,128)(2,1)} %copy-done, bf16[4,256,256]{2,1,0:T(8,128)(2,1)} %copy-done.5, bf16[256,4096]{1,0:T(8,128)(2,1)} %bitcast.32, bf16[2048,1280]{1,0:T(8,128)(2,1)} %all-gather.6.cloned.1.call-done.matrix_ref), custom_call_target="tpu_custom_call" | custom-call | flops 2 | bytes 2 | tf_op jit(solution)/shard_map/project/pallas_call | solution.py:243
  188.5 4.2 %collective-permute-start.15 = (bf16[256,1280]{1,0:T(8,128)(2,1)}, bf16[256,1280]{1,0:T(8,128)(2,1)}, u32[]{:S(2)}, u32[]{:S(2)}) collective-permute-start(bf16[256,1280]{1,0:T(8,128)(2,1)} %project.4), channel_id=1, source_target_pairs={{0,32},{32,64},{64,96},{96,128},{128,160},{160,192},{192,224},{224... | collective-permute-start | bytes 1966088 | tf_op jit(solution)/shard_map/ppermute | solution.py:265
  193.3 5.5 %project.5 = bf16[256,1280]{1,0:T(8,128)(2,1)} custom-call(s32[9]{0:T(128)} %get-tuple-element.65.place_ref, bf16[4,256,256]{2,1,0:T(8,128)(2,1)} %copy-done, bf16[4,256,256]{2,1,0:T(8,128)(2,1)} %copy-done.5, bf16[256,4096]{1,0:T(8,128)(2,1)} %bitcast.33, bf16[2048,1280]{1,0:T(8,128)(2,1)} %collective-permute-done.16.matrix_ref), custom_call_target="tpu_custom_call" | custom-call | flops 2 | bytes 2 | tf_op jit(solution)/shard_map/project/pallas_call | solution.py:243
  198.8 29.8 %all-gather.8.cloned.1.call-done.matrix_ref = bf16[2048,768]{1,0:T(8,128)(2,1)} async-done(((bf16[512,768]{1,0:T(8,128)(2,1)}), bf16[2048,768]{1,0:T(8,128)(2,1)}) %all-gather.8.cloned.1.call-update) | async-done | bytes 3145744 | tf_op jit(solution)/shard_map/all_gather | solution.py:295
  228.6 4.8 %collective-permute-start.17 = (bf16[256,1280]{1,0:T(8,128)(2,1)}, bf16[256,1280]{1,0:T(8,128)(2,1)}, u32[]{:S(2)}, u32[]{:S(2)}) collective-permute-start(bf16[256,1280]{1,0:T(8,128)(2,1)} %project.5), channel_id=1, source_target_pairs={{0,32},{32,64},{64,96},{96,128},{128,160},{160,192},{192,224},{224... | collective-permute-start | bytes 1966088 | tf_op jit(solution)/shard_map/ppermute | solution.py:265
  233.5 1.6 broadcast_in_dim.24
  235.0 2.0 bitcast_dynamic-update-slice_fusion.1
  237.0 4.8 %project.6 = bf16[256,768]{1,0:T(8,128)(2,1)} custom-call(s32[9]{0:T(128)} %get-tuple-element.66.place_ref, bf16[4,256,256]{2,1,0:T(8,128)(2,1)} %copy-done, bf16[4,256,256]{2,1,0:T(8,128)(2,1)} %copy-done.5, bf16[256,4096]{1,0:T(8,128)(2,1)} %bitcast.34, bf16[2048,768]{1,0:T(8,128)(2,1)} %all-gather.8.cloned.1.call-done.matrix_ref), custom_call_target="tpu_custom_call" | custom-call | flops 2 | bytes 2 | tf_op jit(solution)/shard_map/project/pallas_call | solution.py:243
  241.8 2.1 collective-permute-start.18
  243.9 24.7 %collective-permute-done.17 = bf16[256,1280]{1,0:T(8,128)(2,1)} collective-permute-done((bf16[256,1280]{1,0:T(8,128)(2,1)}, bf16[256,1280]{1,0:T(8,128)(2,1)}, u32[]{:S(2)}, u32[]{:S(2)}) %collective-permute-start.17) | collective-permute-done | bytes 655392 | tf_op jit(solution)/shard_map/ppermute | solution.py:265
  268.5 1.6 copy-done.6
  270.2 4.8 %project.7 = bf16[256,768]{1,0:T(8,128)(2,1)} custom-call(s32[9]{0:T(128)} %get-tuple-element.64.place_ref, bf16[4,256,256]{2,1,0:T(8,128)(2,1)} %copy-done, bf16[4,256,256]{2,1,0:T(8,128)(2,1)} %copy-done.5, bf16[256,4096]{1,0:T(8,128)(2,1)} %bitcast.35, bf16[2048,768]{1,0:T(8,128)(2,1)} %copy-done.6), custom_call_target="tpu_custom_call" | custom-call | flops 2 | bytes 2 | tf_op jit(solution)/shard_map/project/pallas_call | solution.py:243
  275.0 2.7 collective-permute-start.20
  277.7 2.0 bitcast_dynamic-update-slice_fusion
  279.6 7.8 %collective-permute-done.18 = bf16[256,768]{1,0:T(8,128)(2,1)S(1)} collective-permute-done((bf16[256,768]{1,0:T(8,128)(2,1)}, bf16[256,768]{1,0:T(8,128)(2,1)S(1)}, u32[]{:S(2)}, u32[]{:S(2)}) %collective-permute-start.18) | collective-permute-done | bytes 393248 | tf_op jit(solution)/shard_map/ppermute | solution.py:265
  287.5 0.8 bitcast_dynamic-update-slice_fusion.3
  288.2 11.5 %collective-permute-done.20 = bf16[256,768]{1,0:T(8,128)(2,1)S(1)} collective-permute-done((bf16[256,768]{1,0:T(8,128)(2,1)}, bf16[256,768]{1,0:T(8,128)(2,1)S(1)}, u32[]{:S(2)}, u32[]{:S(2)}) %collective-permute-start.20) | collective-permute-done | bytes 393248 | tf_op jit(solution)/shard_map/ppermute | solution.py:265
  299.8 0.8 bitcast_dynamic-update-slice_fusion.2
  (51 shorter events, 3.5 us)
Async XLA Ops:
  6.5 4.8 %copy-start.1 = (bf16[1,256,2048]{2,1,0:T(8,128)(2,1)S(1)}, bf16[1,256,2048]{2,1,0:T(8,128)(2,1)}, u32[]{:S(2)}) copy-start(bf16[1,256,2048]{2,1,0:T(8,128)(2,1)} %param.8) | copy-start | bytes 3145732
  6.5 4.8 %copy-start.2 = (bf16[1,256,2048]{2,1,0:T(8,128)(2,1)S(1)}, bf16[1,256,2048]{2,1,0:T(8,128)(2,1)}, u32[]{:S(2)}) copy-start(bf16[1,256,2048]{2,1,0:T(8,128)(2,1)} %param.9) | copy-start | bytes 3145732
  6.5 4.8 %copy-start.4 = (s32[1,256]{1,0:T(1,128)S(1)}, s32[1,256]{1,0:T(1,128)}, u32[]{:S(2)}) copy-start(s32[1,256]{1,0:T(1,128)} %refs_2_.1) | copy-start | bytes 3076
  6.5 81.2 %all-gather.4.cloned.1.call-start = ((), (), s32[]{:S(2)}) async-start(), calls=%async_computation | async-start | bytes 1638400 | tf_op jit(solution)/shard_map/all_gather | solution.py:295
  7.7 1.6 collective-permute-start.14
  10.3 5.0 %copy-start.7 = (bf16[64,2048]{1,0:T(8,128)(2,1)}, bf16[64,2048]{1,0:T(8,128)(2,1)S(1)}, u32[]{:S(2)}) copy-start(bf16[64,2048]{1,0:T(8,128)(2,1)S(1)} %get-tuple-element.62) | copy-start | bytes 786436
  11.2 150.5 %all-gather.6.cloned.1.call-start = ((), (), s32[]{:S(2)}) async-start(), calls=%async_computation.1 | async-start | bytes 6553600 | tf_op jit(solution)/shard_map/all_gather | solution.py:295
  11.3 8.0 %copy-start.3 = (bf16[1,256,2048]{2,1,0:T(8,128)(2,1)S(1)}, bf16[1,256,2048]{2,1,0:T(8,128)(2,1)}, u32[]{:S(2)}) copy-start(bf16[1,256,2048]{2,1,0:T(8,128)(2,1)} %param.7) | copy-start | bytes 3145732
  12.2 2.8 collective-permute-start.4
  15.3 51.5 %collective-permute-start.6 = (bf16[2,528,256]{2,1,0:T(8,128)(2,1)S(1)}, bf16[2,528,256]{2,1,0:T(8,128)(2,1)S(1)}, u32[]{:S(2)}, u32[]{:S(2)}) collective-permute-start(bf16[2,528,256]{2,1,0:T(8,128)(2,1)S(1)} %get-tuple-element.41), channel_id=1, source_target_pairs={{0,4},{2,6},{4,0},{6,2},{1,5},{3,7},{5,1},{7,3},{8,12},{10,14},{12... | collective-permute-start | bytes 1622024 | tf_op jit(solution)/shard_map/ppermute | solution.py:273
  18.7 48.2 %collective-permute-start.5 = (bf16[2,528,256]{2,1,0:T(8,128)(2,1)S(1)}, bf16[2,528,256]{2,1,0:T(8,128)(2,1)S(1)}, u32[]{:S(2)}, u32[]{:S(2)}) collective-permute-start(bf16[2,528,256]{2,1,0:T(8,128)(2,1)S(1)} %get-tuple-element.40), channel_id=1, source_target_pairs={{0,2},{2,0},{4,6},{6,4},{1,3},{3,1},{5,7},{7,5},{8,10},{10,8},{12,... | collective-permute-start | bytes 1622024 | tf_op jit(solution)/shard_map/ppermute | solution.py:273
  18.8 68.0 %collective-permute-start.7 = (bf16[2,528,256]{2,1,0:T(8,128)(2,1)S(1)}, bf16[2,528,256]{2,1,0:T(8,128)(2,1)S(1)}, u32[]{:S(2)}, u32[]{:S(2)}) collective-permute-start(bf16[2,528,256]{2,1,0:T(8,128)(2,1)S(1)} %get-tuple-element.43), channel_id=1, source_target_pairs={{0,6},{2,4},{4,2},{6,0},{1,7},{3,5},{5,3},{7,1},{8,14},{10,12},{12... | collective-permute-start | bytes 1622024 | tf_op jit(solution)/shard_map/ppermute | solution.py:273
  20.0 2.0 collective-permute-start
  87.7 140.9 %all-gather.8.cloned.1.call-start = ((), (), s32[]{:S(2)}) async-start(), calls=%async_computation.2 | async-start | bytes 3932160 | tf_op jit(solution)/shard_map/all_gather | solution.py:295
  87.9 32.0 %collective-permute-start.8 = (bf16[3,528,256]{2,1,0:T(8,128)(2,1)S(1)}, bf16[3,528,256]{2,1,0:T(8,128)(2,1)S(1)}, u32[]{:S(2)}, u32[]{:S(2)}) collective-permute-start(bf16[3,528,256]{2,1,0:T(8,128)(2,1)S(1)} %get-tuple-element.58), channel_id=1, source_target_pairs={{0,8},{8,16},{16,24},{1,9},{9,17},{17,25},{2,10},{10,18},{18,26},{... | collective-permute-start | bytes 2433032 | tf_op jit(solution)/shard_map/ppermute | solution.py:303
  90.5 29.4 %collective-permute-start.9 = (bf16[3,528,256]{2,1,0:T(8,128)(2,1)S(1)}, bf16[3,528,256]{2,1,0:T(8,128)(2,1)S(1)}, u32[]{:S(2)}, u32[]{:S(2)}) collective-permute-start(bf16[3,528,256]{2,1,0:T(8,128)(2,1)S(1)} %get-tuple-element.57), channel_id=1, source_target_pairs={{8,0},{16,8},{24,16},{9,1},{17,9},{25,17},{10,2},{18,10},{26,18},{... | collective-permute-start | bytes 2433032 | tf_op jit(solution)/shard_map/ppermute | solution.py:304
  91.8 11.1 %collective-permute-start.1 = (bf16[2,256,256]{2,1,0:T(8,128)(2,1)S(1)}, bf16[2,256,256]{2,1,0:T(8,128)(2,1)S(1)}, u32[]{:S(2)}, u32[]{:S(2)}) collective-permute-start(bf16[2,256,256]{2,1,0:T(8,128)(2,1)S(1)} %get-tuple-element.34), channel_id=1, source_target_pairs={{0,2},{2,0},{4,6},{6,4},{1,3},{3,1},{5,7},{7,5},{8,10},{10,8},{12,... | collective-permute-start | bytes 786440 | tf_op jit(solution)/shard_map/ppermute | solution.py:273
  91.9 21.9 %collective-permute-start.2 = (bf16[2,256,256]{2,1,0:T(8,128)(2,1)S(1)}, bf16[2,256,256]{2,1,0:T(8,128)(2,1)S(1)}, u32[]{:S(2)}, u32[]{:S(2)}) collective-permute-start(bf16[2,256,256]{2,1,0:T(8,128)(2,1)S(1)} %get-tuple-element.35), channel_id=1, source_target_pairs={{0,4},{2,6},{4,0},{6,2},{1,5},{3,7},{5,1},{7,3},{8,12},{10,14},{12... | collective-permute-start | bytes 786440 | tf_op jit(solution)/shard_map/ppermute | solution.py:273
  95.8 22.1 %collective-permute-start.3 = (bf16[2,256,256]{2,1,0:T(8,128)(2,1)S(1)}, bf16[2,256,256]{2,1,0:T(8,128)(2,1)S(1)}, u32[]{:S(2)}, u32[]{:S(2)}) collective-permute-start(bf16[2,256,256]{2,1,0:T(8,128)(2,1)S(1)} %get-tuple-element.36), channel_id=1, source_target_pairs={{0,6},{2,4},{4,2},{6,0},{1,7},{3,5},{5,3},{7,1},{8,14},{10,12},{12... | collective-permute-start | bytes 786440 | tf_op jit(solution)/shard_map/ppermute | solution.py:273
  133.8 9.3 %collective-permute-start.10 = (bf16[2,256,256]{2,1,0:T(8,128)(2,1)S(1)}, bf16[2,256,256]{2,1,0:T(8,128)(2,1)S(1)}, u32[]{:S(2)}, u32[]{:S(2)}) collective-permute-start(bf16[2,256,256]{2,1,0:T(8,128)(2,1)S(1)} %get-tuple-element.61), channel_id=1, source_target_pairs={{0,2},{2,0},{4,6},{6,4},{1,3},{3,1},{5,7},{7,5},{8,10},{10,8},{12,... | collective-permute-start | bytes 786440 | tf_op jit(solution)/shard_map/ppermute | solution.py:273
  133.9 21.5 %collective-permute-start.11 = (bf16[2,256,256]{2,1,0:T(8,128)(2,1)S(1)}, bf16[2,256,256]{2,1,0:T(8,128)(2,1)S(1)}, u32[]{:S(2)}, u32[]{:S(2)}) collective-permute-start(bf16[2,256,256]{2,1,0:T(8,128)(2,1)S(1)} %get-tuple-element.60), channel_id=1, source_target_pairs={{0,4},{2,6},{4,0},{6,2},{1,5},{3,7},{5,1},{7,3},{8,12},{10,14},{12... | collective-permute-start | bytes 786440 | tf_op jit(solution)/shard_map/ppermute | solution.py:273
  138.3 20.5 %collective-permute-start.12 = (bf16[2,256,256]{2,1,0:T(8,128)(2,1)S(1)}, bf16[2,256,256]{2,1,0:T(8,128)(2,1)S(1)}, u32[]{:S(2)}, u32[]{:S(2)}) collective-permute-start(bf16[2,256,256]{2,1,0:T(8,128)(2,1)S(1)} %get-tuple-element.59), channel_id=1, source_target_pairs={{0,6},{2,4},{4,2},{6,0},{1,7},{3,5},{5,3},{7,1},{8,14},{10,12},{12... | collective-permute-start | bytes 786440 | tf_op jit(solution)/shard_map/ppermute | solution.py:273
  160.8 0.8 copy-start
  161.6 1.9 collective-permute-start.13
  163.5 19.5 %copy-start.5 = (bf16[4,256,256]{2,1,0:T(8,128)(2,1)}, bf16[4,256,256]{2,1,0:T(8,128)(2,1)S(1)}, u32[]{:S(2)}) copy-start(bf16[4,256,256]{2,1,0:T(8,128)(2,1)S(1)} %collective-permute-done.13.got_ref) | copy-start | bytes 1572868
  163.5 29.8 %collective-permute-start.16 = (bf16[2048,1280]{1,0:T(8,128)(2,1)}, bf16[2048,1280]{1,0:T(8,128)(2,1)}, u32[]{:S(2)}, u32[]{:S(2)}) collective-permute-start(bf16[2048,1280]{1,0:T(8,128)(2,1)} %all-gather.6.cloned.1.call-done.matrix_ref), channel_id=1, source_target_pairs={{0,1},{1,0},{2,3},{3,2},{4,5},{5,4},{6,7},{7,6},{8,9},{9,8},{10,11... | collective-permute-start | bytes 15728648 | tf_op jit(solution)/shard_map/ppermute | solution.py:269
  188.5 40.1 %collective-permute-start.15 = (bf16[256,1280]{1,0:T(8,128)(2,1)}, bf16[256,1280]{1,0:T(8,128)(2,1)}, u32[]{:S(2)}, u32[]{:S(2)}) collective-permute-start(bf16[256,1280]{1,0:T(8,128)(2,1)} %project.4), channel_id=1, source_target_pairs={{0,32},{32,64},{64,96},{96,128},{128,160},{160,192},{192,224},{224... | collective-permute-start | bytes 1966088 | tf_op jit(solution)/shard_map/ppermute | solution.py:265
  228.6 39.9 %collective-permute-start.19 = (bf16[2048,768]{1,0:T(8,128)(2,1)}, bf16[2048,768]{1,0:T(8,128)(2,1)S(1)}, u32[]{:S(2)}, u32[]{:S(2)}) collective-permute-start(bf16[2048,768]{1,0:T(8,128)(2,1)} %all-gather.8.cloned.1.call-done.matrix_ref), channel_id=1, source_target_pairs={{0,1},{1,0},{2,3},{3,2},{4,5},{5,4},{6,7},{7,6},{8,9},{9,8},{10,11... | collective-permute-start | bytes 9437192 | tf_op jit(solution)/shard_map/ppermute | solution.py:269
  228.6 39.9 %collective-permute-start.17 = (bf16[256,1280]{1,0:T(8,128)(2,1)}, bf16[256,1280]{1,0:T(8,128)(2,1)}, u32[]{:S(2)}, u32[]{:S(2)}) collective-permute-start(bf16[256,1280]{1,0:T(8,128)(2,1)} %project.5), channel_id=1, source_target_pairs={{0,32},{32,64},{64,96},{96,128},{128,160},{160,192},{192,224},{224... | collective-permute-start | bytes 1966088 | tf_op jit(solution)/shard_map/ppermute | solution.py:265
  241.8 45.7 %collective-permute-start.18 = (bf16[256,768]{1,0:T(8,128)(2,1)}, bf16[256,768]{1,0:T(8,128)(2,1)S(1)}, u32[]{:S(2)}, u32[]{:S(2)}) collective-permute-start(bf16[256,768]{1,0:T(8,128)(2,1)} %project.6), channel_id=1, source_target_pairs={{0,32},{32,64},{64,96},{96,128},{128,160},{160,192},{192,224},{224... | collective-permute-start | bytes 1179656 | tf_op jit(solution)/shard_map/ppermute | solution.py:265
  268.5 1.6 copy-start.6
  275.0 24.8 %collective-permute-start.20 = (bf16[256,768]{1,0:T(8,128)(2,1)}, bf16[256,768]{1,0:T(8,128)(2,1)S(1)}, u32[]{:S(2)}, u32[]{:S(2)}) collective-permute-start(bf16[256,768]{1,0:T(8,128)(2,1)} %project.7), channel_id=1, source_target_pairs={{0,32},{32,64},{64,96},{96,128},{128,160},{160,192},{192,224},{224... | collective-permute-start | bytes 1179656 | tf_op jit(solution)/shard_map/ppermute | solution.py:265
Sparse Core Ops, SparseCore 0:
  11.3 59.3 all-gather.3
  87.9 66.7 all-gather.5
  182.5 46.1 all-gather.7
